TPU v7x, 32 devices: a whole 2x2x4 slice. The times are simulated.
32 devices in a mesh: occ: 8 (over z, y), virt: 4 (over x, core).
Axes of the slice: x: 2, y: 2, z: 4, core: 2. Of those that a mesh axis runs over, the one named last changes fastest.
Arguments:
- integrals: bfloat16 [8, 1024, 1536], P('occ', 'virt'), may hold values from -2 to 2
- occupied_energy: float32 [8], replicated, may hold values from -2 to -0.2
- virtual_energy: float32 [1024], replicated, may hold values from 0.5 to 4
- partner_list: int32 [2, 8], replicated, may hold values from 0 to 7, each once within a row
- tile_lists: int32 [2, 8, 4, 56], P(None, 'occ', 'virt'), may hold values from -1 to 63, as said below
Outputs:
- gradient: float32 [8, 1024, 1536], P('occ', 'virt')
Inputs may be any that keep to these rules, and one draw needn't show every extreme that they name: Each row partner_list[k] holds every block number once. In each list tile_lists[k, d, s] the live entries stand first, are distinct, and number from 24 to 56; the rest are -1. For each k and d one slice s holds exactly 56 live entries.
All inputs are finite; a program needn't handle non-finite values.
Results may differ from a plain program's by a relative error of at most 0.0021.
Values may be sent and summed in bfloat16 or wider, within the bound.
No kernel may reach another device: no remote copies, remote signals or barrier semaphores. Data moves between devices by JAX's collectives and lax.ppermute only.
A program may use at most 64 MiB of HBM per device.

v0:
```python
import math

import jax
import jax.numpy as jnp
from jax import lax
from jax.sharding import PartitionSpec as P

TILE = 64


def to_tiles(source, tile_width):
    orbitals, row_count, aux_width = source.shape
    tile_count = row_count // tile_width
    shaped = source.reshape(orbitals, tile_count, tile_width, aux_width)
    return shaped.transpose(1, 0, 2, 3).reshape(tile_count, orbitals * tile_width, aux_width)


def split_pieces(source, piece_count):
    orbitals, row_count, aux_width = source.shape
    return source.reshape(orbitals, piece_count, row_count // piece_count, aux_width)


def join_pieces(pieces):
    orbitals, piece_count, row_count, aux_width = pieces.shape
    return pieces.reshape(orbitals, piece_count * row_count, aux_width)


def one_hot(indices, width, dtype):
    return (indices[:, None] == jnp.arange(width, dtype=jnp.int32)[None, :]).astype(dtype)


def body(integrals, occupied_energy, virtual_energy, partner_list, tile_lists):
    orbitals, slice_rows, aux_width = integrals.shape
    tile_width = TILE
    occ_count = lax.axis_size("occ")
    myself = lax.axis_index("occ")
    slice_id = lax.axis_index("virt")
    full_rows = virtual_energy.shape[0]
    a_count = slice_rows // tile_width
    b_count = full_rows // tile_width
    spread = lax.all_to_all(
        split_pieces(integrals, occ_count), "occ", split_axis=1, concat_axis=1, tiled=True
    )
    outgoing = (
        jnp.take(spread, partner_list[0], axis=1),
        jnp.take(spread, partner_list[1], axis=1),
    )
    partner_one, partner_two = (
        lax.all_to_all(outgoing[0], "occ", split_axis=1, concat_axis=1, tiled=True),
        lax.all_to_all(outgoing[1], "occ", split_axis=1, concat_axis=1, tiled=True),
    )
    partners = (
        lax.all_gather(join_pieces(partner_one), "virt", axis=1, tiled=True),
        lax.all_gather(join_pieces(partner_two), "virt", axis=1, tiled=True),
    )
    own_tiles = to_tiles(integrals, tile_width)
    own_energy = lax.dynamic_slice_in_dim(occupied_energy, myself * orbitals, orbitals, 0)
    energy_left = lax.dynamic_slice_in_dim(
        virtual_energy, slice_id * slice_rows, slice_rows, 0
    ).reshape(a_count, tile_width)
    energy_right = virtual_energy.reshape(b_count, tile_width)
    slot_count = tile_lists.shape[-1]
    group_size = math.gcd(slot_count, 16)
    highest = lax.Precision.HIGHEST
    totals = jnp.zeros((a_count, orbitals * tile_width, aux_width), jnp.float32)
    for pairing in range(2):
        partner_tiles = to_tiles(partners[pairing], tile_width)
        partner_energy = lax.dynamic_slice_in_dim(
            occupied_energy, partner_list[pairing, myself] * orbitals, orbitals, 0
        )
        listed = tile_lists[pairing, 0, 0]

        def group_step(
            number,
            running,
            listed=listed,
            partner_tiles=partner_tiles,
            partner_energy=partner_energy,
        ):
            entries = lax.dynamic_slice_in_dim(listed, number * group_size, group_size, 0)
            in_use = entries >= 0
            clamped = jnp.maximum(entries, 0)
            a_tile = clamped // b_count
            c_tile = clamped % b_count
            a_pick = one_hot(a_tile, a_count, jnp.bfloat16)
            c_pick = one_hot(c_tile, b_count, jnp.bfloat16)
            a_float = one_hot(a_tile, a_count, jnp.float32)
            c_float = one_hot(c_tile, b_count, jnp.float32)
            own_rows = jnp.einsum(
                "ga,axp->gxp", a_pick, own_tiles, preferred_element_type=jnp.float32
            ).astype(jnp.bfloat16)
            partner_rows = jnp.einsum(
                "gc,cyp->gyp", c_pick, partner_tiles, preferred_element_type=jnp.float32
            ).astype(jnp.bfloat16)
            scores = jnp.einsum(
                "gxp,gyp->gxy", own_rows, partner_rows, preferred_element_type=jnp.float32
            )
            left_rows = jnp.dot(a_float, energy_left, precision=highest)
            right_rows = jnp.dot(c_float, energy_right, precision=highest)
            gap_left = (left_rows[:, None, :] - own_energy[None, :, None]).reshape(
                group_size, orbitals * tile_width
            )
            gap_right = (right_rows[:, None, :] - partner_energy[None, :, None]).reshape(
                group_size, orbitals * tile_width
            )
            ratio = scores / (gap_left[:, :, None] + gap_right[:, None, :])
            amplitude = jnp.where(in_use[:, None, None], ratio, jnp.zeros_like(ratio)).astype(
                jnp.bfloat16
            )
            contrib = jnp.einsum(
                "gxy,gyp->gxp", amplitude, partner_rows, preferred_element_type=jnp.float32
            )
            return running + jnp.einsum("ga,gxp->axp", a_float, contrib, precision=highest)

        group_count = slot_count // group_size
        totals = lax.fori_loop(0, group_count, group_step, totals)
    shaped = totals.reshape(a_count, orbitals, tile_width, aux_width).transpose(1, 0, 2, 3)
    return shaped.reshape(orbitals, slice_rows, aux_width)


def solution(mesh):
    return jax.shard_map(
        body,
        mesh=mesh,
        in_specs=(P("occ", "virt", None), P(), P(), P(), P(None, "occ", "virt", None)),
        out_specs=P("occ", "virt", None),
        check_vma=False,
    )
```

profile of v0, /device:TPU:0, one launch (start us, length us, event | category | flops | bytes accessed | tf_op | source)
XLA Modules:
  0.0 356.6 jit_solution(3856549787706133059)
XLA Ops:
  6.5 7.4 %all-to-all-start = ((bf16[1,8,32,1536]{3,2,0,1:T(8,128)(2,1)}), bf16[1,8,32,1536]{3,2,0,1:T(8,128)(2,1)S(1)}, u32[]{:S(2)}, u32[]{:S(2)}) async-start(bf16[1,8,32,1536]{3,2,0,1:T(8,128)(2,1)} %bitcast.99), calls=%async_computation | async-start | bytes 1572864 | tf_op jit(solution)/shard_map/all_to_all | solution.py:41
  14.0 20.1 %all-to-all-done = bf16[1,8,32,1536]{3,2,0,1:T(8,128)(2,1)S(1)} async-done(((bf16[1,8,32,1536]{3,2,0,1:T(8,128)(2,1)}), bf16[1,8,32,1536]{3,2,0,1:T(8,128)(2,1)S(1)}, u32[]{:S(2)}, u32[]{:S(2)}) %all-to-all-start) | async-done | bytes 786464 | tf_op jit(solution)/shard_map/all_to_all | solution.py:41
  34.9 23.7 %all_to_all.15 = bf16[1,8,32,1536]{3,2,0,1:T(8,128)(2,1)} all-to-all(bf16[1,8,32,1536]{3,2,0,1:T(8,128)(2,1)S(1)} %fusion.91), channel_id=1, replica_groups=mesh['occ'=8,'virt'=4] {'occ'}, dimensions={1} | all-to-all | bytes 1572864 | tf_op jit(solution)/shard_map/all_to_all | solution.py:49
  60.3 4.3 %all-to-all-start.2 = ((bf16[1,8,32,1536]{3,2,0,1:T(8,128)(2,1)}), bf16[1,8,32,1536]{3,2,0,1:T(8,128)(2,1)}, u32[]{:S(2)}, u32[]{:S(2)}) async-start(bf16[1,8,32,1536]{3,2,0,1:T(8,128)(2,1)} %fusion.90), calls=%async_computation.2 | async-start | bytes 1572864 | tf_op jit(solution)/shard_map/all_to_all | solution.py:50
  70.6 13.5 %all-to-all-done.2 = bf16[1,8,32,1536]{3,2,0,1:T(8,128)(2,1)} async-done(((bf16[1,8,32,1536]{3,2,0,1:T(8,128)(2,1)}), bf16[1,8,32,1536]{3,2,0,1:T(8,128)(2,1)}, u32[]{:S(2)}, u32[]{:S(2)}) %all-to-all-start.2) | async-done | bytes 786464 | tf_op jit(solution)/shard_map/all_to_all | solution.py:50
  86.4 5.3 %copy.33 = bf16[16,64,1536]{2,0,1:T(8,128)(2,1)} copy(bf16[16,64,1536]{2,1,0:T(8,128)(2,1)} %bitcast.97) | data formatting | bytes 6291456
  91.7 124.9 %while.32 = (s32[]{:T(128)}, f32[4,64,1536]{2,0,1:T(4,128)S(1)}, s32[56]{0:T(128)S(1)}, bf16[4,64,1536]{2,0,1:T(4,128)(2,1)S(1)}, bf16[16,64,1536]{2,0,1:T(8,128...) while((s32[]{:T(128)}, f32[4,64,1536]{2,0,1:T(4,128)S(1)}, ...), condition=%wide.region_1.3_spmd.clone, body=%wide.region_0.0_spmd.clone.sunk | while | flops 273147328 | bytes 25966124 | solution.py:116
  95.2 3.0 convolution_convert_fusion.10
  98.4 5.2 %fusion.151 = f32[8,64,1536]{2,1,0:T(8,128)} fusion(bf16[8,64,1536]{2,0,1:T(8,128)(2,1)S(1)} %convolution_convert_fusion.10, bf16[8,64,1536]{2,0,1:T(8,128)(2,1)} %convolution_convert_fusion.11, f32[8,64]{1,0:T(8,128)S(1)} %convolution_subtract_fusion.10, f32[8,64]{1,0:T(8,128)S(1)} %convolution_subtract_fusion.11, ...), kind=kOutput, calls=%fused_computation.42.clone.1 | convolution fusion | flops 201457664 | bytes 6295560 | tf_op jit(solution)/shard_map/while/body/eval_jaxpr/gxy,gyp->gxp/dot_general | solution.py:110
  103.6 6.4 %fusion.152 = f32[4,64,1536]{2,0,1:T(4,128)S(1)} fusion(f32[8,64,1536]{2,1,0:T(8,128)} %fusion.151, f32[4,64,1536]{2,0,1:T(4,128)S(1)} %get-tuple-element.723, pred[]{:T(512)S(6)} %compare.9, s32[8]{0:T(128)S(1)} %get-tuple-element.708), kind=kOutput, calls=%fused_computation.39.clone.1 | convolution fusion | flops 38535200 | bytes 6291489 | tf_op jit(solution)/shard_map/while/body/eval_jaxpr/ga,gxp->axp/dot_general | solution.py:113
  113.5 2.5 convolution_convert_fusion.10
  116.1 5.2 %fusion.151 = f32[8,64,1536]{2,1,0:T(8,128)} fusion(bf16[8,64,1536]{2,0,1:T(8,128)(2,1)S(1)} %convolution_convert_fusion.10, bf16[8,64,1536]{2,0,1:T(8,128)(2,1)} %convolution_convert_fusion.11, f32[8,64]{1,0:T(8,128)S(1)} %convolution_subtract_fusion.10, f32[8,64]{1,0:T(8,128)S(1)} %convolution_subtract_fusion.11, ...), kind=kOutput, calls=%fused_computation.42.clone.1 | convolution fusion | flops 201457664 | bytes 6295560 | tf_op jit(solution)/shard_map/while/body/eval_jaxpr/gxy,gyp->gxp/dot_general | solution.py:110
  121.4 6.4 %fusion.152 = f32[4,64,1536]{2,0,1:T(4,128)S(1)} fusion(f32[8,64,1536]{2,1,0:T(8,128)} %fusion.151, f32[4,64,1536]{2,0,1:T(4,128)S(1)} %get-tuple-element.723, pred[]{:T(512)S(6)} %compare.9, s32[8]{0:T(128)S(1)} %get-tuple-element.708), kind=kOutput, calls=%fused_computation.39.clone.1 | convolution fusion | flops 38535200 | bytes 6291489 | tf_op jit(solution)/shard_map/while/body/eval_jaxpr/ga,gxp->axp/dot_general | solution.py:113
  131.3 2.5 convolution_convert_fusion.10
  133.9 5.2 %fusion.151 = f32[8,64,1536]{2,1,0:T(8,128)} fusion(bf16[8,64,1536]{2,0,1:T(8,128)(2,1)S(1)} %convolution_convert_fusion.10, bf16[8,64,1536]{2,0,1:T(8,128)(2,1)} %convolution_convert_fusion.11, f32[8,64]{1,0:T(8,128)S(1)} %convolution_subtract_fusion.10, f32[8,64]{1,0:T(8,128)S(1)} %convolution_subtract_fusion.11, ...), kind=kOutput, calls=%fused_computation.42.clone.1 | convolution fusion | flops 201457664 | bytes 6295560 | tf_op jit(solution)/shard_map/while/body/eval_jaxpr/gxy,gyp->gxp/dot_general | solution.py:110
  139.2 6.4 %fusion.152 = f32[4,64,1536]{2,0,1:T(4,128)S(1)} fusion(f32[8,64,1536]{2,1,0:T(8,128)} %fusion.151, f32[4,64,1536]{2,0,1:T(4,128)S(1)} %get-tuple-element.723, pred[]{:T(512)S(6)} %compare.9, s32[8]{0:T(128)S(1)} %get-tuple-element.708), kind=kOutput, calls=%fused_computation.39.clone.1 | convolution fusion | flops 38535200 | bytes 6291489 | tf_op jit(solution)/shard_map/while/body/eval_jaxpr/ga,gxp->axp/dot_general | solution.py:113
  149.1 2.5 convolution_convert_fusion.10
  151.7 5.2 %fusion.151 = f32[8,64,1536]{2,1,0:T(8,128)} fusion(bf16[8,64,1536]{2,0,1:T(8,128)(2,1)S(1)} %convolution_convert_fusion.10, bf16[8,64,1536]{2,0,1:T(8,128)(2,1)} %convolution_convert_fusion.11, f32[8,64]{1,0:T(8,128)S(1)} %convolution_subtract_fusion.10, f32[8,64]{1,0:T(8,128)S(1)} %convolution_subtract_fusion.11, ...), kind=kOutput, calls=%fused_computation.42.clone.1 | convolution fusion | flops 201457664 | bytes 6295560 | tf_op jit(solution)/shard_map/while/body/eval_jaxpr/gxy,gyp->gxp/dot_general | solution.py:110
  156.9 6.4 %fusion.152 = f32[4,64,1536]{2,0,1:T(4,128)S(1)} fusion(f32[8,64,1536]{2,1,0:T(8,128)} %fusion.151, f32[4,64,1536]{2,0,1:T(4,128)S(1)} %get-tuple-element.723, pred[]{:T(512)S(6)} %compare.9, s32[8]{0:T(128)S(1)} %get-tuple-element.708), kind=kOutput, calls=%fused_computation.39.clone.1 | convolution fusion | flops 38535200 | bytes 6291489 | tf_op jit(solution)/shard_map/while/body/eval_jaxpr/ga,gxp->axp/dot_general | solution.py:113
  166.9 2.5 convolution_convert_fusion.10
  169.5 5.2 %fusion.151 = f32[8,64,1536]{2,1,0:T(8,128)} fusion(bf16[8,64,1536]{2,0,1:T(8,128)(2,1)S(1)} %convolution_convert_fusion.10, bf16[8,64,1536]{2,0,1:T(8,128)(2,1)} %convolution_convert_fusion.11, f32[8,64]{1,0:T(8,128)S(1)} %convolution_subtract_fusion.10, f32[8,64]{1,0:T(8,128)S(1)} %convolution_subtract_fusion.11, ...), kind=kOutput, calls=%fused_computation.42.clone.1 | convolution fusion | flops 201457664 | bytes 6295560 | tf_op jit(solution)/shard_map/while/body/eval_jaxpr/gxy,gyp->gxp/dot_general | solution.py:110
  174.7 6.4 %fusion.152 = f32[4,64,1536]{2,0,1:T(4,128)S(1)} fusion(f32[8,64,1536]{2,1,0:T(8,128)} %fusion.151, f32[4,64,1536]{2,0,1:T(4,128)S(1)} %get-tuple-element.723, pred[]{:T(512)S(6)} %compare.9, s32[8]{0:T(128)S(1)} %get-tuple-element.708), kind=kOutput, calls=%fused_computation.39.clone.1 | convolution fusion | flops 38535200 | bytes 6291489 | tf_op jit(solution)/shard_map/while/body/eval_jaxpr/ga,gxp->axp/dot_general | solution.py:113
  184.6 2.5 convolution_convert_fusion.10
  187.2 5.2 %fusion.151 = f32[8,64,1536]{2,1,0:T(8,128)} fusion(bf16[8,64,1536]{2,0,1:T(8,128)(2,1)S(1)} %convolution_convert_fusion.10, bf16[8,64,1536]{2,0,1:T(8,128)(2,1)} %convolution_convert_fusion.11, f32[8,64]{1,0:T(8,128)S(1)} %convolution_subtract_fusion.10, f32[8,64]{1,0:T(8,128)S(1)} %convolution_subtract_fusion.11, ...), kind=kOutput, calls=%fused_computation.42.clone.1 | convolution fusion | flops 201457664 | bytes 6295560 | tf_op jit(solution)/shard_map/while/body/eval_jaxpr/gxy,gyp->gxp/dot_general | solution.py:110
  192.5 6.4 %fusion.152 = f32[4,64,1536]{2,0,1:T(4,128)S(1)} fusion(f32[8,64,1536]{2,1,0:T(8,128)} %fusion.151, f32[4,64,1536]{2,0,1:T(4,128)S(1)} %get-tuple-element.723, pred[]{:T(512)S(6)} %compare.9, s32[8]{0:T(128)S(1)} %get-tuple-element.708), kind=kOutput, calls=%fused_computation.39.clone.1 | convolution fusion | flops 38535200 | bytes 6291489 | tf_op jit(solution)/shard_map/while/body/eval_jaxpr/ga,gxp->axp/dot_general | solution.py:113
  202.4 2.5 convolution_convert_fusion.10
  205.0 5.2 %fusion.151 = f32[8,64,1536]{2,1,0:T(8,128)} fusion(bf16[8,64,1536]{2,0,1:T(8,128)(2,1)S(1)} %convolution_convert_fusion.10, bf16[8,64,1536]{2,0,1:T(8,128)(2,1)} %convolution_convert_fusion.11, f32[8,64]{1,0:T(8,128)S(1)} %convolution_subtract_fusion.10, f32[8,64]{1,0:T(8,128)S(1)} %convolution_subtract_fusion.11, ...), kind=kOutput, calls=%fused_computation.42.clone.1 | convolution fusion | flops 201457664 | bytes 6295560 | tf_op jit(solution)/shard_map/while/body/eval_jaxpr/gxy,gyp->gxp/dot_general | solution.py:110
  210.3 6.4 %fusion.152 = f32[4,64,1536]{2,0,1:T(4,128)S(1)} fusion(f32[8,64,1536]{2,1,0:T(8,128)} %fusion.151, f32[4,64,1536]{2,0,1:T(4,128)S(1)} %get-tuple-element.723, pred[]{:T(512)S(6)} %compare.9, s32[8]{0:T(128)S(1)} %get-tuple-element.708), kind=kOutput, calls=%fused_computation.39.clone.1 | convolution fusion | flops 38535200 | bytes 6291489 | tf_op jit(solution)/shard_map/while/body/eval_jaxpr/ga,gxp->axp/dot_general | solution.py:113
  216.7 5.3 %copy.36 = bf16[16,64,1536]{2,0,1:T(8,128)(2,1)} copy(bf16[16,64,1536]{2,1,0:T(8,128)(2,1)} %bitcast.98) | data formatting | bytes 6291456 | tf_op jit(solution)/shard_map/while | solution.py:116
  222.0 126.1 %while.31 = (s32[]{:T(128)}, f32[4,64,1536]{2,0,1:T(4,128)S(1)}, s32[56]{0:T(128)S(1)}, bf16[4,64,1536]{2,0,1:T(4,128)(2,1)S(1)}, bf16[16,64,1536]{2,0,1:T(8,128...) while((s32[]{:T(128)}, f32[4,64,1536]{2,0,1:T(4,128)S(1)}, ...), condition=%wide.region_3.5_spmd, body=%wide.region_2.4_spmd.sunk | while | flops 272754112 | bytes 25966116 | solution.py:116
  225.5 2.5 convolution_convert_fusion.8
  228.1 5.2 %fusion.138 = f32[8,64,1536]{2,1,0:T(8,128)} fusion(bf16[8,64,1536]{2,0,1:T(8,128)(2,1)S(1)} %convolution_convert_fusion.8, bf16[8,64,1536]{2,0,1:T(8,128)(2,1)} %convolution_convert_fusion.9, f32[8,64]{1,0:T(8,128)S(1)} %convolution_subtract_fusion.8, f32[8,64]{1,0:T(8,128)S(1)} %convolution_subtract_fusion.9, ...), kind=kOutput, calls=%fused_computation.9.clone.1 | convolution fusion | flops 201457664 | bytes 6295560 | tf_op jit(solution)/shard_map/while/body/eval_jaxpr/gxy,gyp->gxp/dot_general | solution.py:110
  233.3 6.7 %fusion.139 = f32[4,64,1536]{2,0,1:T(4,128)S(1)} fusion(f32[4,64,1536]{2,0,1:T(4,128)S(1)} %get-tuple-element.762, f32[8,64,1536]{2,1,0:T(8,128)} %fusion.138, s32[8]{0:T(128)S(1)} %get-tuple-element.697), kind=kOutput, calls=%fused_computation.6.clone.1 | convolution fusion | flops 38141984 | bytes 6291488 | tf_op jit(solution)/shard_map/while/body/eval_jaxpr/ga,gxp->axp/dot_general | solution.py:113
  246.1 5.2 %fusion.138 = f32[8,64,1536]{2,1,0:T(8,128)} fusion(bf16[8,64,1536]{2,0,1:T(8,128)(2,1)S(1)} %convolution_convert_fusion.8, bf16[8,64,1536]{2,0,1:T(8,128)(2,1)} %convolution_convert_fusion.9, f32[8,64]{1,0:T(8,128)S(1)} %convolution_subtract_fusion.8, f32[8,64]{1,0:T(8,128)S(1)} %convolution_subtract_fusion.9, ...), kind=kOutput, calls=%fused_computation.9.clone.1 | convolution fusion | flops 201457664 | bytes 6295560 | tf_op jit(solution)/shard_map/while/body/eval_jaxpr/gxy,gyp->gxp/dot_general | solution.py:110
  251.3 6.7 %fusion.139 = f32[4,64,1536]{2,0,1:T(4,128)S(1)} fusion(f32[4,64,1536]{2,0,1:T(4,128)S(1)} %get-tuple-element.762, f32[8,64,1536]{2,1,0:T(8,128)} %fusion.138, s32[8]{0:T(128)S(1)} %get-tuple-element.697), kind=kOutput, calls=%fused_computation.6.clone.1 | convolution fusion | flops 38141984 | bytes 6291488 | tf_op jit(solution)/shard_map/while/body/eval_jaxpr/ga,gxp->axp/dot_general | solution.py:113
  261.5 2.5 convolution_convert_fusion.8
  264.1 5.2 %fusion.138 = f32[8,64,1536]{2,1,0:T(8,128)} fusion(bf16[8,64,1536]{2,0,1:T(8,128)(2,1)S(1)} %convolution_convert_fusion.8, bf16[8,64,1536]{2,0,1:T(8,128)(2,1)} %convolution_convert_fusion.9, f32[8,64]{1,0:T(8,128)S(1)} %convolution_subtract_fusion.8, f32[8,64]{1,0:T(8,128)S(1)} %convolution_subtract_fusion.9, ...), kind=kOutput, calls=%fused_computation.9.clone.1 | convolution fusion | flops 201457664 | bytes 6295560 | tf_op jit(solution)/shard_map/while/body/eval_jaxpr/gxy,gyp->gxp/dot_general | solution.py:110
  269.3 6.7 %fusion.139 = f32[4,64,1536]{2,0,1:T(4,128)S(1)} fusion(f32[4,64,1536]{2,0,1:T(4,128)S(1)} %get-tuple-element.762, f32[8,64,1536]{2,1,0:T(8,128)} %fusion.138, s32[8]{0:T(128)S(1)} %get-tuple-element.697), kind=kOutput, calls=%fused_computation.6.clone.1 | convolution fusion | flops 38141984 | bytes 6291488 | tf_op jit(solution)/shard_map/while/body/eval_jaxpr/ga,gxp->axp/dot_general | solution.py:113
  279.5 2.5 convolution_convert_fusion.8
  282.2 5.2 %fusion.138 = f32[8,64,1536]{2,1,0:T(8,128)} fusion(bf16[8,64,1536]{2,0,1:T(8,128)(2,1)S(1)} %convolution_convert_fusion.8, bf16[8,64,1536]{2,0,1:T(8,128)(2,1)} %convolution_convert_fusion.9, f32[8,64]{1,0:T(8,128)S(1)} %convolution_subtract_fusion.8, f32[8,64]{1,0:T(8,128)S(1)} %convolution_subtract_fusion.9, ...), kind=kOutput, calls=%fused_computation.9.clone.1 | convolution fusion | flops 201457664 | bytes 6295560 | tf_op jit(solution)/shard_map/while/body/eval_jaxpr/gxy,gyp->gxp/dot_general | solution.py:110
  287.3 6.7 %fusion.139 = f32[4,64,1536]{2,0,1:T(4,128)S(1)} fusion(f32[4,64,1536]{2,0,1:T(4,128)S(1)} %get-tuple-element.762, f32[8,64,1536]{2,1,0:T(8,128)} %fusion.138, s32[8]{0:T(128)S(1)} %get-tuple-element.697), kind=kOutput, calls=%fused_computation.6.clone.1 | convolution fusion | flops 38141984 | bytes 6291488 | tf_op jit(solution)/shard_map/while/body/eval_jaxpr/ga,gxp->axp/dot_general | solution.py:113
  297.6 2.5 convolution_convert_fusion.8
  300.2 5.2 %fusion.138 = f32[8,64,1536]{2,1,0:T(8,128)} fusion(bf16[8,64,1536]{2,0,1:T(8,128)(2,1)S(1)} %convolution_convert_fusion.8, bf16[8,64,1536]{2,0,1:T(8,128)(2,1)} %convolution_convert_fusion.9, f32[8,64]{1,0:T(8,128)S(1)} %convolution_subtract_fusion.8, f32[8,64]{1,0:T(8,128)S(1)} %convolution_subtract_fusion.9, ...), kind=kOutput, calls=%fused_computation.9.clone.1 | convolution fusion | flops 201457664 | bytes 6295560 | tf_op jit(solution)/shard_map/while/body/eval_jaxpr/gxy,gyp->gxp/dot_general | solution.py:110
  305.4 6.7 %fusion.139 = f32[4,64,1536]{2,0,1:T(4,128)S(1)} fusion(f32[4,64,1536]{2,0,1:T(4,128)S(1)} %get-tuple-element.762, f32[8,64,1536]{2,1,0:T(8,128)} %fusion.138, s32[8]{0:T(128)S(1)} %get-tuple-element.697), kind=kOutput, calls=%fused_computation.6.clone.1 | convolution fusion | flops 38141984 | bytes 6291488 | tf_op jit(solution)/shard_map/while/body/eval_jaxpr/ga,gxp->axp/dot_general | solution.py:113
  318.2 5.2 %fusion.138 = f32[8,64,1536]{2,1,0:T(8,128)} fusion(bf16[8,64,1536]{2,0,1:T(8,128)(2,1)S(1)} %convolution_convert_fusion.8, bf16[8,64,1536]{2,0,1:T(8,128)(2,1)} %convolution_convert_fusion.9, f32[8,64]{1,0:T(8,128)S(1)} %convolution_subtract_fusion.8, f32[8,64]{1,0:T(8,128)S(1)} %convolution_subtract_fusion.9, ...), kind=kOutput, calls=%fused_computation.9.clone.1 | convolution fusion | flops 201457664 | bytes 6295560 | tf_op jit(solution)/shard_map/while/body/eval_jaxpr/gxy,gyp->gxp/dot_general | solution.py:110
  323.4 6.7 %fusion.139 = f32[4,64,1536]{2,0,1:T(4,128)S(1)} fusion(f32[4,64,1536]{2,0,1:T(4,128)S(1)} %get-tuple-element.762, f32[8,64,1536]{2,1,0:T(8,128)} %fusion.138, s32[8]{0:T(128)S(1)} %get-tuple-element.697), kind=kOutput, calls=%fused_computation.6.clone.1 | convolution fusion | flops 38141984 | bytes 6291488 | tf_op jit(solution)/shard_map/while/body/eval_jaxpr/ga,gxp->axp/dot_general | solution.py:113
  336.2 5.2 %fusion.138 = f32[8,64,1536]{2,1,0:T(8,128)} fusion(bf16[8,64,1536]{2,0,1:T(8,128)(2,1)S(1)} %convolution_convert_fusion.8, bf16[8,64,1536]{2,0,1:T(8,128)(2,1)} %convolution_convert_fusion.9, f32[8,64]{1,0:T(8,128)S(1)} %convolution_subtract_fusion.8, f32[8,64]{1,0:T(8,128)S(1)} %convolution_subtract_fusion.9, ...), kind=kOutput, calls=%fused_computation.9.clone.1 | convolution fusion | flops 201457664 | bytes 6295560 | tf_op jit(solution)/shard_map/while/body/eval_jaxpr/gxy,gyp->gxp/dot_general | solution.py:110
  341.4 6.7 %fusion.139 = f32[4,64,1536]{2,0,1:T(4,128)S(1)} fusion(f32[4,64,1536]{2,0,1:T(4,128)S(1)} %get-tuple-element.762, f32[8,64,1536]{2,1,0:T(8,128)} %fusion.138, s32[8]{0:T(128)S(1)} %get-tuple-element.697), kind=kOutput, calls=%fused_computation.6.clone.1 | convolution fusion | flops 38141984 | bytes 6291488 | tf_op jit(solution)/shard_map/while/body/eval_jaxpr/ga,gxp->axp/dot_general | solution.py:113
  (161 shorter events, 66.1 us)
Async XLA Ops:
  6.5 7.5 %copy-start.7 = (s32[2,8]{1,0:T(2,128)S(1)}, s32[2,8]{1,0:T(2,128)}, u32[]{:S(2)}) copy-start(s32[2,8]{1,0:T(2,128)} %param.14) | copy-start | bytes 196
  6.5 27.6 %all-to-all-start = ((bf16[1,8,32,1536]{3,2,0,1:T(8,128)(2,1)}), bf16[1,8,32,1536]{3,2,0,1:T(8,128)(2,1)S(1)}, u32[]{:S(2)}, u32[]{:S(2)}) async-start(bf16[1,8,32,1536]{3,2,0,1:T(8,128)(2,1)} %bitcast.99), calls=%async_computation | async-start | bytes 1572864 | tf_op jit(solution)/shard_map/all_to_all | solution.py:41
  13.9 72.4 %all-gather.3.cloned.1.call-start = ((), (), s32[]{:S(2)}) async-start(), calls=%async_computation.3 | async-start | bytes 3932160 | tf_op jit(solution)/shard_map/all_gather | solution.py:53
  59.3 8.6 %copy-start.5 = (f32[1024]{0:T(1024)S(1)}, f32[1024]{0:T(1024)}, u32[]{:S(2)}) copy-start(f32[1024]{0:T(1024)} %param.13) | copy-start | bytes 12292
  59.3 8.8 %copy-start.4 = (bf16[1,256,1536]{2,1,0:T(8,128)(2,1)S(1)}, bf16[1,256,1536]{2,1,0:T(8,128)(2,1)}, u32[]{:S(2)}) copy-start(bf16[1,256,1536]{2,1,0:T(8,128)(2,1)} %param.11) | copy-start | bytes 2359300
  60.3 9.6 %copy-start.6 = (f32[8]{0:T(128)S(1)}, f32[8]{0:T(128)}, u32[]{:S(2)}) copy-start(f32[8]{0:T(128)} %param.12) | copy-start | bytes 100
  60.3 10.3 %copy-start.8 = (s32[2,1,1,56]{3,2,1,0:T(1,128)S(1)}, s32[2,1,1,56]{3,2,1,0:T(1,128)}, u32[]{:S(2)}) copy-start(s32[2,1,1,56]{3,2,1,0:T(1,128)} %param.15) | copy-start | bytes 1348
  60.3 23.8 %all-to-all-start.2 = ((bf16[1,8,32,1536]{3,2,0,1:T(8,128)(2,1)}), bf16[1,8,32,1536]{3,2,0,1:T(8,128)(2,1)}, u32[]{:S(2)}, u32[]{:S(2)}) async-start(bf16[1,8,32,1536]{3,2,0,1:T(8,128)(2,1)} %fusion.90), calls=%async_computation.2 | async-start | bytes 1572864 | tf_op jit(solution)/shard_map/all_to_all | solution.py:50
  64.7 152.0 %all-gather.5.cloned.1.call-start = ((), (), s32[]{:S(2)}) async-start(), calls=%async_computation.4 | async-start | bytes 3932160 | tf_op jit(solution)/shard_map/all_gather | solution.py:54
  91.7 3.5 copy-start
  103.6 6.4 %copy-start.1 = (bf16[4,64,1536]{2,0,1:T(4,128)(2,1)S(1)}, bf16[4,64,1536]{2,0,1:T(4,128)(2,1)}, u32[]{:S(2)}) copy-start(bf16[4,64,1536]{2,0,1:T(4,128)(2,1)} %copy-done) | copy-start | bytes 2359300 | tf_op jit(solution)/shard_map/while
  110.0 3.5 copy-start
  121.4 6.4 %copy-start.1 = (bf16[4,64,1536]{2,0,1:T(4,128)(2,1)S(1)}, bf16[4,64,1536]{2,0,1:T(4,128)(2,1)}, u32[]{:S(2)}) copy-start(bf16[4,64,1536]{2,0,1:T(4,128)(2,1)} %copy-done) | copy-start | bytes 2359300 | tf_op jit(solution)/shard_map/while
  127.8 3.5 copy-start
  139.2 6.4 %copy-start.1 = (bf16[4,64,1536]{2,0,1:T(4,128)(2,1)S(1)}, bf16[4,64,1536]{2,0,1:T(4,128)(2,1)}, u32[]{:S(2)}) copy-start(bf16[4,64,1536]{2,0,1:T(4,128)(2,1)} %copy-done) | copy-start | bytes 2359300 | tf_op jit(solution)/shard_map/while
  145.6 3.5 copy-start
  156.9 6.4 %copy-start.1 = (bf16[4,64,1536]{2,0,1:T(4,128)(2,1)S(1)}, bf16[4,64,1536]{2,0,1:T(4,128)(2,1)}, u32[]{:S(2)}) copy-start(bf16[4,64,1536]{2,0,1:T(4,128)(2,1)} %copy-done) | copy-start | bytes 2359300 | tf_op jit(solution)/shard_map/while
  163.4 3.5 copy-start
  174.7 6.4 %copy-start.1 = (bf16[4,64,1536]{2,0,1:T(4,128)(2,1)S(1)}, bf16[4,64,1536]{2,0,1:T(4,128)(2,1)}, u32[]{:S(2)}) copy-start(bf16[4,64,1536]{2,0,1:T(4,128)(2,1)} %copy-done) | copy-start | bytes 2359300 | tf_op jit(solution)/shard_map/while
  181.1 3.5 copy-start
  192.5 6.4 %copy-start.1 = (bf16[4,64,1536]{2,0,1:T(4,128)(2,1)S(1)}, bf16[4,64,1536]{2,0,1:T(4,128)(2,1)}, u32[]{:S(2)}) copy-start(bf16[4,64,1536]{2,0,1:T(4,128)(2,1)} %copy-done) | copy-start | bytes 2359300 | tf_op jit(solution)/shard_map/while
  198.9 3.5 copy-start
  210.3 6.4 %copy-start.1 = (bf16[4,64,1536]{2,0,1:T(4,128)(2,1)S(1)}, bf16[4,64,1536]{2,0,1:T(4,128)(2,1)}, u32[]{:S(2)}) copy-start(bf16[4,64,1536]{2,0,1:T(4,128)(2,1)} %copy-done) | copy-start | bytes 2359300 | tf_op jit(solution)/shard_map/while
  222.0 3.5 copy-start.2
  233.3 6.7 %copy-start.3 = (bf16[4,64,1536]{2,0,1:T(4,128)(2,1)S(1)}, bf16[4,64,1536]{2,0,1:T(4,128)(2,1)}, u32[]{:S(2)}) copy-start(bf16[4,64,1536]{2,0,1:T(4,128)(2,1)} %copy-done.2) | copy-start | bytes 2359300 | tf_op jit(solution)/shard_map/while
  240.0 3.5 copy-start.2
  251.3 6.7 %copy-start.3 = (bf16[4,64,1536]{2,0,1:T(4,128)(2,1)S(1)}, bf16[4,64,1536]{2,0,1:T(4,128)(2,1)}, u32[]{:S(2)}) copy-start(bf16[4,64,1536]{2,0,1:T(4,128)(2,1)} %copy-done.2) | copy-start | bytes 2359300 | tf_op jit(solution)/shard_map/while
  258.0 3.5 copy-start.2
  269.3 6.7 %copy-start.3 = (bf16[4,64,1536]{2,0,1:T(4,128)(2,1)S(1)}, bf16[4,64,1536]{2,0,1:T(4,128)(2,1)}, u32[]{:S(2)}) copy-start(bf16[4,64,1536]{2,0,1:T(4,128)(2,1)} %copy-done.2) | copy-start | bytes 2359300 | tf_op jit(solution)/shard_map/while
  276.0 3.5 copy-start.2
  287.3 6.7 %copy-start.3 = (bf16[4,64,1536]{2,0,1:T(4,128)(2,1)S(1)}, bf16[4,64,1536]{2,0,1:T(4,128)(2,1)}, u32[]{:S(2)}) copy-start(bf16[4,64,1536]{2,0,1:T(4,128)(2,1)} %copy-done.2) | copy-start | bytes 2359300 | tf_op jit(solution)/shard_map/while
  294.1 3.5 copy-start.2
  305.4 6.7 %copy-start.3 = (bf16[4,64,1536]{2,0,1:T(4,128)(2,1)S(1)}, bf16[4,64,1536]{2,0,1:T(4,128)(2,1)}, u32[]{:S(2)}) copy-start(bf16[4,64,1536]{2,0,1:T(4,128)(2,1)} %copy-done.2) | copy-start | bytes 2359300 | tf_op jit(solution)/shard_map/while
  312.1 3.5 copy-start.2
  323.4 6.7 %copy-start.3 = (bf16[4,64,1536]{2,0,1:T(4,128)(2,1)S(1)}, bf16[4,64,1536]{2,0,1:T(4,128)(2,1)}, u32[]{:S(2)}) copy-start(bf16[4,64,1536]{2,0,1:T(4,128)(2,1)} %copy-done.2) | copy-start | bytes 2359300 | tf_op jit(solution)/shard_map/while
  330.1 3.5 copy-start.2
  341.4 6.7 %copy-start.3 = (bf16[4,64,1536]{2,0,1:T(4,128)(2,1)S(1)}, bf16[4,64,1536]{2,0,1:T(4,128)(2,1)}, u32[]{:S(2)}) copy-start(bf16[4,64,1536]{2,0,1:T(4,128)(2,1)} %copy-done.2) | copy-start | bytes 2359300 | tf_op jit(solution)/shard_map/while
Sparse Core Ops, SparseCore 0:
  58.8 27.5 all-gather.2
  87.9 28.5 all-gather.4
where the time goes:
time: 358 us; the launch traced here: 357 us
  matrix products  248 us (69%)
  waiting for transfers between devices  35.9 us (10%)
  blocking collectives  23.7 us (7%)
  between operations  17.3 us (5%)
  local copies, waits for them, and re-layouts  15.7 us (4%)
  starting transfers between devices  11.8 us (3%)
    dot_general x14, matrix products, group_step(): jnp.einsum('ga,gxp->axp', a_float, contrib, precision=highest)  91.7 us
    dot_general x14, matrix products, group_step(): jnp.einsum('gxy,gyp->gxp', amplitude, partner_rows, preferred_element_typ...  73 us
    dot_general x14, matrix products, group_step(): jnp.einsum('gc,cyp->gyp', c_pick, partner_tiles, preferred_element_type=j...  35.8 us
    dot_general x14, matrix products, group_step(): jnp.einsum('ga,axp->gxp', a_pick, own_tiles, preferred_element_type=jnp.f...  24.7 us
    all_to_all x1, blocking collectives, body(): lax.all_to_all(outgoing[0], 'occ', split_axis=1, concat_axis=1, tiled=True)  23.7 us
    all_to_all x1, waiting for transfers between devices, body(): lax.all_to_all(split_pieces(integrals, occ_count), 'occ', split_axis=1, c...  20.1 us
    all_to_all x1, waiting for transfers between devices, body(): lax.all_to_all(outgoing[1], 'occ', split_axis=1, concat_axis=1, tiled=True)  13.5 us
    dot_general x14, matrix products, group_step(): left_rows = jnp.dot(a_float, energy_left, precision=highest)  11.6 us
  transfers between devices with their start and end apart: 4, of which 3 were waited for; matrix products, arithmetic and copies ran while one was open for 37% of the time, Pallas kernels for 0%

commit v1 on v0

v1 whole, which is shorter than its diff:
```python
import jax
import jax.numpy as jnp
from jax import lax
from jax.experimental import pallas as pl
from jax.experimental.pallas import tpu as pltpu
from jax.sharding import PartitionSpec as P

TILE = 64
CHUNKS = 4


def xor_pairs(count, mask):
    return [(i, i ^ mask) for i in range(count)]


def listed_weights(entries, a_count, b_count, left_gap, right_gap, slice_order):
    pair_ids = jnp.arange(a_count * b_count, dtype=jnp.int32)
    listed = jnp.any(entries[:, :, None] == pair_ids[None, None, :], axis=1)
    pairings = entries.shape[0]
    slices = slice_order.shape[0]
    listed = listed.reshape(pairings, a_count, slices, b_count // slices)
    listed = jnp.take(listed, slice_order, axis=2)
    listed = jnp.repeat(jnp.repeat(listed, TILE, axis=1), TILE, axis=3)
    right = jnp.take(right_gap, slice_order, axis=1)
    gap = left_gap[None, :, None, None] + right[:, None, :, :]
    return jnp.where(listed, 1.0 / gap, 0.0)


def part_kernel(own_ref, weight_ref, *refs, first):
    if first:
        *row_refs, out_ref = refs
    else:
        *row_refs, total_ref, out_ref = refs
    own = own_ref[...]
    aux = own.shape[-1]
    rows = jnp.concatenate([r[...].reshape(-1, aux) for r in row_refs], axis=0)
    scores = lax.dot_general(own, rows, (((1,), (1,)), ((), ())), preferred_element_type=jnp.float32)
    amplitude = (scores * weight_ref[...]).astype(jnp.bfloat16)
    part = jnp.dot(amplitude, rows, preferred_element_type=jnp.float32)
    if first:
        out_ref[...] = part
    else:
        out_ref[...] = total_ref[...] + part


def add_part(own, weights, rows, total):
    slice_rows, aux = own.shape
    first = total is None
    args = [own, weights, *rows] + ([] if first else [total])
    width = weights.shape[-1]
    nbytes = 2 * (slice_rows + width) * aux + 4 * slice_rows * (width + 2 * aux)
    return pl.pallas_call(
        lambda *refs: part_kernel(*refs, first=first),
        out_shape=jax.ShapeDtypeStruct((slice_rows, aux), jnp.float32),
        in_specs=[pl.BlockSpec(memory_space=pltpu.VMEM)] * len(args),
        out_specs=pl.BlockSpec(memory_space=pltpu.VMEM),
        input_output_aliases={} if first else {len(args) - 1: 0},
        compiler_params=pltpu.CompilerParams(vmem_limit_bytes=48 * 1024 * 1024),
        cost_estimate=pl.CostEstimate(
            flops=4 * slice_rows * width * aux, bytes_accessed=nbytes, transcendentals=0
        ),
    )(*args)


def body(integrals, occupied_energy, virtual_energy, partner_list, tile_lists):
    orbitals, slice_rows, aux = integrals.shape
    occ_count = lax.axis_size("occ")
    virt_count = lax.axis_size("virt")
    myself = lax.axis_index("occ")
    slice_id = lax.axis_index("virt")
    a_count = slice_rows // TILE
    b_count = virtual_energy.shape[0] // TILE
    pairings = partner_list.shape[0]
    bits = occ_count.bit_length() - 1
    pick_bits = bits // 2
    spread_masks = [1 << (bits - 1)] + [1 << i for i in range(bits - pick_bits - 1)]
    pick_unit = 1 << (bits - pick_bits - 1)
    pick_masks = [pick_unit * i for i in range(1, 1 << pick_bits)]
    pick_all = pick_unit * ((1 << pick_bits) - 1)

    own = integrals.reshape(slice_rows, aux)
    partners = jnp.take(partner_list, myself, axis=1)
    slice_order = slice_id ^ jnp.arange(virt_count, dtype=jnp.int32)
    slice_order = jnp.stack([slice_id ^ m for m in range(virt_count)])
    own_energy = lax.dynamic_index_in_dim(occupied_energy, myself, 0, False)
    left_gap = lax.dynamic_slice_in_dim(virtual_energy, slice_id * slice_rows, slice_rows, 0) - own_energy
    right_gap = virtual_energy.reshape(1, virt_count, slice_rows) - occupied_energy[partners][:, None, None]
    weights = listed_weights(tile_lists[:, 0, 0], a_count, b_count, left_gap, right_gap, slice_order)

    rows = slice_rows // CHUNKS
    total = None
    early = []
    for mask in spread_masks[1:]:
        pass
    own_side = {0: own}
    for mask in spread_masks[1:]:
        for held in list(own_side):
            own_side[held ^ mask] = lax.ppermute(own_side[held], "occ", xor_pairs(occ_count, mask))
    for c in range(CHUNKS):
        lo = c * rows
        held = {m: v[lo : lo + rows] for m, v in own_side.items()}
        side = {spread_masks[0]: lax.ppermute(own[lo : lo + rows], "occ", xor_pairs(occ_count, spread_masks[0]))}
        for mask in spread_masks[1:]:
            for m in list(side):
                side[m ^ mask] = lax.ppermute(side[m], "occ", xor_pairs(occ_count, mask))
        held.update(side)

        def chosen(wanted, held=held):
            rel = (wanted ^ myself) & (occ_count - 1 - pick_all)
            result = held[0]
            for m, v in held.items():
                if m:
                    result = jnp.where(rel == m, v, result)
            return result

        picked = jnp.stack([chosen(partners[k]) for k in range(pairings)])
        for mask in pick_masks:
            there = jnp.take(partner_list, myself ^ mask, axis=1)
            outgoing = jnp.stack([chosen(there[k]) for k in range(pairings)])
            arrived = lax.ppermute(outgoing, "occ", xor_pairs(occ_count, mask))
            differs = ((partners ^ myself) & pick_all) == mask
            picked = jnp.where(differs[:, None, None], arrived, picked)
        slices = {0: picked}
        mask = virt_count // 2
        while mask:
            for m in list(slices):
                slices[m ^ mask] = lax.ppermute(slices[m], "virt", xor_pairs(virt_count, mask))
            mask //= 2
        order = list(range(virt_count))
        w = weights[:, :, :, lo : lo + rows].transpose(1, 2, 0, 3).reshape(slice_rows, -1)
        total = add_part(own, w, [slices[m] for m in order], total)
    return total[None]


def solution(mesh):
    return jax.shard_map(
        body,
        mesh=mesh,
        in_specs=(P("occ", "virt", None), P(), P(), P(), P(None, "occ", "virt", None)),
        out_specs=P("occ", "virt", None),
        check_vma=False,
    )
```

time: 358 us -> 149 us (0.42)
  matrix products: 248 us -> 0 us
  waiting for transfers between devices: 35.9 us -> 83.1 us
  blocking collectives: 23.7 us -> 0 us
  Pallas kernels: 0 us -> 15.4 us
  between operations: 17.3 us -> 2.73 us
  starting transfers between devices: 11.8 us -> 21.1 us
  other arithmetic: 3.48 us -> 9.25 us
    dot_general x84 -> x0, matrix products: 248 us -> none  [the longest x14 91.7 us: group_step(): jnp.einsum('ga,gxp->axp', a_float, contrib, precision=highest)]
    ppermute x0 -> x25, waiting for transfers between devices: none -> 83.1 us  [the longest x4 28.3 us: body(): arrived = lax.ppermute(outgoing, 'occ', xor_pairs(occ_count, mask))]
    all_to_all x2 -> x0, waiting for transfers between devices: 33.6 us -> none  [the longest x1 20.1 us: body(): lax.all_to_all(split_pieces(integrals, occ_count), 'occ', split_axis=1, c...]
    all_to_all x1 -> x0, blocking collectives: 23.7 us -> none  [body(): lax.all_to_all(outgoing[0], 'occ', split_axis=1, concat_axis=1, tiled=True)]
    ppermute x0 -> x25, starting transfers between devices: none -> 21.1 us  [the longest x12 6.33 us: body(): lax.ppermute(slices[m], 'virt', xor_pairs(virt_count, mask))]
    pallas_call x0 -> x4, Pallas kernels: none -> 15.4 us  [add_part(): pl.pallas_call(lambda *refs: part_kernel(*refs, first=first), out_shape=j...]
    all_to_all x2 -> x0, starting transfers between devices: 11.8 us -> none  [the longest x1 7.41 us: body(): lax.all_to_all(split_pieces(integrals, occ_count), 'occ', split_axis=1, c...]
    while x58 -> x0, local copies, waits for them, and re-layouts: 7.02 us -> none  [the longest x2 6.91 us: body(): totals = lax.fori_loop(0, group_count, group_step, totals)]
  transfers between devices with their start and end apart: 4 -> 25, of which waited for: 3 -> 14; matrix products, arithmetic and copies ran while one was open for 37% -> 13% of each run, Pallas kernels for 0% -> 8%
where the time goes in v1:
time: 149 us; the launch traced here: 148 us
  waiting for transfers between devices  83.1 us (56%)
  starting transfers between devices  21.1 us (14%)
  local copies, waits for them, and re-layouts  16.8 us (11%)
  Pallas kernels  15.4 us (10%)
  other arithmetic  9.25 us (6%)
  between operations  2.73 us (2%)
    ppermute x4, waiting for transfers between devices, body(): arrived = lax.ppermute(outgoing, 'occ', xor_pairs(occ_count, mask))  28.3 us
    ppermute x12, waiting for transfers between devices, body(): lax.ppermute(slices[m], 'virt', xor_pairs(virt_count, mask))  24.5 us
    ppermute x4, waiting for transfers between devices, body(): lax.ppermute(own[lo:lo + rows], 'occ', xor_pairs(occ_count, spread_masks[...  23.9 us
    pallas_call x4, Pallas kernels, add_part(): pl.pallas_call(lambda *refs: part_kernel(*refs, first=first), out_shape=j...  15.4 us
    ppermute x4, waiting for transfers between devices, body(): side[m ^ mask] = lax.ppermute(side[m], 'occ', xor_pairs(occ_count, mask))  6.34 us
    ppermute x12, starting transfers between devices, body(): lax.ppermute(slices[m], 'virt', xor_pairs(virt_count, mask))  6.33 us
    ppermute x4, starting transfers between devices, body(): lax.ppermute(own[lo:lo + rows], 'occ', xor_pairs(occ_count, spread_masks[...  5.91 us
    transpose x5, local copies, waits for them, and re-layouts, body(): weights[:, :, :, lo:lo + rows].transpose(1, 2, 0, 3).reshape(slice_rows, -1)  5.27 us
  transfers between devices with their start and end apart: 25, of which 14 were waited for; matrix products, arithmetic and copies ran while one was open for 13% of the time, Pallas kernels for 8%

profile of v1, /device:TPU:0, one launch (start us, length us, event | category | flops | bytes accessed | tf_op | source)
XLA Modules:
  0.0 148.3 jit_solution(9179229210617096209)
XLA Ops:
  0.0 3.0 %collective-permute-start.2 = (bf16[256,1536]{1,0:T(8,128)(2,1)}, bf16[256,1536]{1,0:T(8,128)(2,1)S(1)}, u32[]{:S(2)}, u32[]{:S(2)}) collective-permute-start(bf16[256,1536]{1,0:T(8,128)(2,1)} %bitcast.110), channel_id=1, source_target_pairs={{0,4},{4,0},{8,12},{12,8},{16,20},{20,16},{24,28},{28,24},{1,5},{5... | collective-permute-start | bytes 2359304 | tf_op jit(solution)/shard_map/ppermute | solution.py:98
  3.0 1.3 slice_bitcast_fusion.4
  4.2 2.7 %collective-permute-start = (bf16[64,1536]{1,0:T(8,128)(2,1)S(1)}, bf16[64,1536]{1,0:T(8,128)(2,1)S(1)}, u32[]{:S(2)}, u32[]{:S(2)}) collective-permute-start(bf16[64,1536]{1,0:T(8,128)(2,1)S(1)} %get-tuple-element.41), channel_id=1, source_target_pairs={{0,16},{4,20},{8,24},{12,28},{16,0},{20,4},{24,8},{28,12},{1,17},{... | collective-permute-start | bytes 589832 | tf_op jit(solution)/shard_map/ppermute | solution.py:102
  7.2 2.6 %collective-permute-start.19 = (bf16[64,1536]{1,0:T(8,128)(2,1)S(1)}, bf16[64,1536]{1,0:T(8,128)(2,1)S(1)}, u32[]{:S(2)}, u32[]{:S(2)}) collective-permute-start(bf16[64,1536]{1,0:T(8,128)(2,1)S(1)} %get-tuple-element.39), channel_id=1, source_target_pairs={{0,16},{4,20},{8,24},{12,28},{16,0},{20,4},{24,8},{28,12},{1,17},{... | collective-permute-start | bytes 589832 | tf_op jit(solution)/shard_map/ppermute | solution.py:102
  10.2 1.0 select_reduce_fusion
  11.1 0.7 fusion.2
  14.3 0.7 sub.23
  15.0 0.8 fusion
  15.9 13.7 %collective-permute-done = bf16[64,1536]{1,0:T(8,128)(2,1)S(1)} collective-permute-done((bf16[64,1536]{1,0:T(8,128)(2,1)S(1)}, bf16[64,1536]{1,0:T(8,128)(2,1)S(1)}, u32[]{:S(2)}, u32[]{:S(2)}) %collective-permute-start) | collective-permute-done | bytes 196640 | tf_op jit(solution)/shard_map/ppermute | solution.py:102
  30.0 3.8 %collective-permute-done.13 = bf16[64,1536]{1,0:T(8,128)(2,1)S(1)} collective-permute-done((bf16[64,1536]{1,0:T(8,128)(2,1)S(1)}, bf16[64,1536]{1,0:T(8,128)(2,1)S(1)}, u32[]{:S(2)}, u32[]{:S(2)}) %collective-permute-start.13) | collective-permute-done | bytes 196640 | tf_op jit(solution)/shard_map/ppermute | solution.py:102
  34.2 3.8 %collective-permute-done.19 = bf16[64,1536]{1,0:T(8,128)(2,1)S(1)} collective-permute-done((bf16[64,1536]{1,0:T(8,128)(2,1)S(1)}, bf16[64,1536]{1,0:T(8,128)(2,1)S(1)}, u32[]{:S(2)}, u32[]{:S(2)}) %collective-permute-start.19) | collective-permute-done | bytes 196640 | tf_op jit(solution)/shard_map/ppermute | solution.py:102
  38.4 2.6 %collective-permute-done.7 = bf16[64,1536]{1,0:T(8,128)(2,1)S(1)} collective-permute-done((bf16[64,1536]{1,0:T(8,128)(2,1)S(1)}, bf16[64,1536]{1,0:T(8,128)(2,1)S(1)}, u32[]{:S(2)}, u32[]{:S(2)}) %collective-permute-start.7) | collective-permute-done | bytes 196640 | tf_op jit(solution)/shard_map/ppermute | solution.py:102
  41.6 3.2 %collective-permute-done.20 = bf16[64,1536]{1,0:T(8,128)(2,1)S(1)} collective-permute-done((bf16[64,1536]{1,0:T(8,128)(2,1)S(1)}, bf16[64,1536]{1,0:T(8,128)(2,1)S(1)}, u32[]{:S(2)}, u32[]{:S(2)}) %collective-permute-start.20) | collective-permute-done | bytes 196640 | tf_op jit(solution)/shard_map/ppermute | solution.py:105
  44.7 3.1 %collective-permute-done.8 = bf16[64,1536]{1,0:T(8,128)(2,1)S(1)} collective-permute-done((bf16[64,1536]{1,0:T(8,128)(2,1)S(1)}, bf16[64,1536]{1,0:T(8,128)(2,1)S(1)}, u32[]{:S(2)}, u32[]{:S(2)}) %collective-permute-start.8) | collective-permute-done | bytes 196640 | tf_op jit(solution)/shard_map/ppermute | solution.py:105
  48.2 0.8 pad_maximum_fusion
  49.0 0.7 collective-permute-start.3
  49.8 0.8 pad_maximum_fusion.2
  50.6 1.4 collective-permute-start.15
  52.0 0.8 pad_maximum_fusion.1
  52.8 0.7 collective-permute-start.9
  53.6 1.4 collective-permute-start.21
  55.0 1.1 gather_fusion.1
  56.2 5.1 %collective-permute-done.3 = bf16[2,64,1536]{2,1,0:T(8,128)(2,1)} collective-permute-done((bf16[2,64,1536]{2,1,0:T(8,128)(2,1)}, bf16[2,64,1536]{2,1,0:T(8,128)(2,1)}, u32[]{:S(2)}, u32[]{:S(2)}) %collective-permute-start.3) | collective-permute-done | bytes 393248 | tf_op jit(solution)/shard_map/ppermute | solution.py:120
  61.4 8.4 %collective-permute-done.15 = bf16[2,64,1536]{2,1,0:T(8,128)(2,1)} collective-permute-done((bf16[2,64,1536]{2,1,0:T(8,128)(2,1)}, bf16[2,64,1536]{2,1,0:T(8,128)(2,1)}, u32[]{:S(2)}, u32[]{:S(2)}) %collective-permute-start.15) | collective-permute-done | bytes 393248 | tf_op jit(solution)/shard_map/ppermute | solution.py:120
  69.8 8.4 %collective-permute-done.9 = bf16[2,64,1536]{2,1,0:T(8,128)(2,1)} collective-permute-done((bf16[2,64,1536]{2,1,0:T(8,128)(2,1)}, bf16[2,64,1536]{2,1,0:T(8,128)(2,1)}, u32[]{:S(2)}, u32[]{:S(2)}) %collective-permute-start.9) | collective-permute-done | bytes 393248 | tf_op jit(solution)/shard_map/ppermute | solution.py:120
  78.2 6.3 %collective-permute-done.21 = bf16[2,64,1536]{2,1,0:T(8,128)(2,1)S(1)} collective-permute-done((bf16[2,64,1536]{2,1,0:T(8,128)(2,1)S(1)}, bf16[2,64,1536]{2,1,0:T(8,128)(2,1)S(1)}, u32[]{:S(2)}, u32[]{:S(2)}) %collective-permute-start.21) | collective-permute-done | bytes 393248 | tf_op jit(solution)/shard_map/ppermute | solution.py:120
  84.6 0.7 copy-done.12
  85.3 2.4 %maximum_select_fusion.3 = (bf16[2,64,1536]{2,1,0:T(8,128)(2,1)S(1)}, bf16[2,64,1536]{2,1,0:T(8,128)(2,1)}, bf16[2,64,1536]{2,1,0:T(8,128)(2,1)S(1)}, bf16[2,64,1536]{2,1,0:T(8,128)(2,1)S(1)}) fusion(bf16[2,64,1536]{2,1,0:T(8,128)(2,1)} %copy-done.12, bf16[1,64,1536]{2,1,0:T(8,128)(2,1)S(1)} %get-tuple-element.24, ...), kind=kLoop, calls=%fused_computation.15 | loop fusion | flops 1572864 | bytes 4718594 | tf_op jit(solution)/shard_map/jit(_where)/select_n | solution.py:122
  87.7 1.5 %collective-permute-start.23 = (bf16[2,64,1536]{2,1,0:T(8,128)(2,1)S(1)}, bf16[2,64,1536]{2,1,0:T(8,128)(2,1)S(1)}, u32[]{:S(2)}, u32[]{:S(2)}) collective-permute-start(bf16[2,64,1536]{2,1,0:T(8,128)(2,1)S(1)} %get-tuple-element.43.refs_2_), channel_id=1, source_target_pairs={{0,2},{1,3},{2,0},{3,1},{4,6},{5,7},{6,4},{7,5},{8,10},{9,11},{10,... | collective-permute-start | bytes 1179656 | tf_op jit(solution)/shard_map/ppermute | solution.py:127
  90.7 1.5 %collective-permute-start.11 = (bf16[2,64,1536]{2,1,0:T(8,128)(2,1)}, bf16[2,64,1536]{2,1,0:T(8,128)(2,1)}, u32[]{:S(2)}, u32[]{:S(2)}) collective-permute-start(bf16[2,64,1536]{2,1,0:T(8,128)(2,1)} %get-tuple-element.44.refs_2_), channel_id=1, source_target_pairs={{0,2},{1,3},{2,0},{3,1},{4,6},{5,7},{6,4},{7,5},{8,10},{9,11},{10,... | collective-permute-start | bytes 1179656 | tf_op jit(solution)/shard_map/ppermute | solution.py:127
  92.2 7.6 %collective-permute-done.23.refs_4_ = bf16[2,64,1536]{2,1,0:T(8,128)(2,1)S(1)} collective-permute-done((bf16[2,64,1536]{2,1,0:T(8,128)(2,1)S(1)}, bf16[2,64,1536]{2,1,0:T(8,128)(2,1)S(1)}, u32[]{:S(2)}, u32[]{:S(2)}) %collective-permute-start.23) | collective-permute-done | bytes 393248 | tf_op jit(solution)/shard_map/ppermute | solution.py:127
  99.7 1.5 %collective-permute-start.5 = (bf16[2,64,1536]{2,1,0:T(8,128)(2,1)S(1)}, bf16[2,64,1536]{2,1,0:T(8,128)(2,1)}, u32[]{:S(2)}, u32[]{:S(2)}) collective-permute-start(bf16[2,64,1536]{2,1,0:T(8,128)(2,1)S(1)} %get-tuple-element.46.refs_2_), channel_id=1, source_target_pairs={{0,2},{1,3},{2,0},{3,1},{4,6},{5,7},{6,4},{7,5},{8,10},{9,11},{10,... | collective-permute-start | bytes 1179656 | tf_op jit(solution)/shard_map/ppermute | solution.py:127
  102.6 5.7 %collective-permute-done.17.refs_4_ = bf16[2,64,1536]{2,1,0:T(8,128)(2,1)} collective-permute-done((bf16[2,64,1536]{2,1,0:T(8,128)(2,1)S(1)}, bf16[2,64,1536]{2,1,0:T(8,128)(2,1)}, u32[]{:S(2)}, u32[]{:S(2)}) %collective-permute-start.17) | collective-permute-done | bytes 393248 | tf_op jit(solution)/shard_map/ppermute | solution.py:127
  108.3 1.4 dynamic-slice_subtract_fusion
  111.0 5.7 %collective-permute-done.11.refs_4_ = bf16[2,64,1536]{2,1,0:T(8,128)(2,1)} collective-permute-done((bf16[2,64,1536]{2,1,0:T(8,128)(2,1)}, bf16[2,64,1536]{2,1,0:T(8,128)(2,1)}, u32[]{:S(2)}, u32[]{:S(2)}) %collective-permute-start.11) | collective-permute-done | bytes 393248 | tf_op jit(solution)/shard_map/ppermute | solution.py:127
  116.7 5.5 %collective-permute-done.5.refs_4_ = bf16[2,64,1536]{2,1,0:T(8,128)(2,1)} collective-permute-done((bf16[2,64,1536]{2,1,0:T(8,128)(2,1)S(1)}, bf16[2,64,1536]{2,1,0:T(8,128)(2,1)}, u32[]{:S(2)}, u32[]{:S(2)}) %collective-permute-start.5) | collective-permute-done | bytes 393248 | tf_op jit(solution)/shard_map/ppermute | solution.py:127
  122.7 1.2 slice_bitcast_fusion
  124.2 1.1 copy.26
  125.5 1.1 copy.25
  126.8 1.9 %copy.24 = f32[256,4,2,64]{0,3,2,1:T(8,128)} copy(f32[256,4,2,64]{0,3,1,2:T(8,128)} %get-tuple-element.22) | data formatting | bytes 1048576 | tf_op jit(solution)/shard_map/transpose | solution.py:130
  128.7 1.2 copy.31.refs_1_
  129.9 1.0 copy-done.4
  130.9 1.0 copy-done.6
  131.9 1.0 copy-done.8
  132.9 3.3 %shard_map.55.refs_6_ = f32[256,1536]{1,0:T(8,128)} custom-call(bf16[256,1536]{1,0:T(8,128)(2,1)S(1)} %bitcast.111, f32[256,512]{1,0:T(8,128)S(1)} %copy.28.refs_1_, bf16[2,64,1536]{2,1,0:T(8,128)(2,1)S(1)} %copy-done.4, bf16[2,64,1536]{2,1,0:T(8,128)(2,1)S(1)} %copy-done.8, bf16[2,64,1536]{2,1,0:T(8,128)(2,1)S(1)} %copy-done.6, ...), custom_call_target="tpu_custom_call" | custom-call | flops 805306368 | bytes 6029312 | tf_op jit(solution)/shard_map/pallas_call | solution.py:52
  136.2 3.9 %shard_map.56.refs_6_ = f32[256,1536]{1,0:T(8,128)} custom-call(bf16[256,1536]{1,0:T(8,128)(2,1)S(1)} %bitcast.112, f32[256,512]{1,0:T(8,128)S(1)} %copy.29.refs_1_, bf16[2,64,1536]{2,1,0:T(8,128)(2,1)S(1)} %copy-done.2, bf16[2,64,1536]{2,1,0:T(8,128)(2,1)S(1)} %copy-done.10, ...), custom_call_target="tpu_custom_call", output_to_operand_aliasing={{}: (6, {})} | custom-call | flops 805306368 | bytes 6029312 | tf_op jit(solution)/shard_map/pallas_call | solution.py:52
  140.1 4.1 %shard_map.57.refs_6_ = f32[256,1536]{1,0:T(8,128)} custom-call(bf16[256,1536]{1,0:T(8,128)(2,1)S(1)} %bitcast.113, f32[256,512]{1,0:T(8,128)S(1)} %copy.30.refs_1_, bf16[2,64,1536]{2,1,0:T(8,128)(2,1)} %get-tuple-element.44.refs_2_, bf16[2,64,1536]{2,1,0:T(8,128)(2,1)} %collective-permute-done.10.refs_3_, ...), custom_call_target="tpu_custom_call", output_to_operand_aliasing={{}: (6, {})} | custom-call | flops 805306368 | bytes 6029312 | tf_op jit(solution)/shard_map/pallas_call | solution.py:52
  144.3 4.0 %shard_map.58 = f32[256,1536]{1,0:T(8,128)} custom-call(bf16[256,1536]{1,0:T(8,128)(2,1)S(1)} %bitcast.114, f32[256,512]{1,0:T(8,128)S(1)} %copy.31.refs_1_, bf16[2,64,1536]{2,1,0:T(8,128)(2,1)S(1)} %get-tuple-element.46.refs_2_, bf16[2,64,1536]{2,1,0:T(8,128)(2,1)} %collective-permute-done.4.refs_3_, ...), custom_call_target="tpu_custom_call", output_to_operand_aliasing={{}: (6, {})} | custom-call | flops 805306368 | bytes 6029312 | tf_op jit(solution)/shard_map/pallas_call | solution.py:52
  (79 shorter events, 8.5 us)
Async XLA Ops:
  0.0 47.9 %copy-start = (bf16[1,256,1536]{2,1,0:T(8,128)(2,1)S(1)}, bf16[1,256,1536]{2,1,0:T(8,128)(2,1)}, u32[]{:S(2)}) copy-start(bf16[1,256,1536]{2,1,0:T(8,128)(2,1)} %param.7) | copy-start | bytes 2359300
  0.0 47.9 %collective-permute-start.2 = (bf16[256,1536]{1,0:T(8,128)(2,1)}, bf16[256,1536]{1,0:T(8,128)(2,1)S(1)}, u32[]{:S(2)}, u32[]{:S(2)}) collective-permute-start(bf16[256,1536]{1,0:T(8,128)(2,1)} %bitcast.110), channel_id=1, source_target_pairs={{0,4},{4,0},{8,12},{12,8},{16,20},{20,16},{24,28},{28,24},{1,5},{5... | collective-permute-start | bytes 2359304 | tf_op jit(solution)/shard_map/ppermute | solution.py:98
  4.2 25.3 %collective-permute-start = (bf16[64,1536]{1,0:T(8,128)(2,1)S(1)}, bf16[64,1536]{1,0:T(8,128)(2,1)S(1)}, u32[]{:S(2)}, u32[]{:S(2)}) collective-permute-start(bf16[64,1536]{1,0:T(8,128)(2,1)S(1)} %get-tuple-element.41), channel_id=1, source_target_pairs={{0,16},{4,20},{8,24},{12,28},{16,0},{20,4},{24,8},{28,12},{1,17},{... | collective-permute-start | bytes 589832 | tf_op jit(solution)/shard_map/ppermute | solution.py:102
  6.9 26.9 %collective-permute-start.13 = (bf16[64,1536]{1,0:T(8,128)(2,1)S(1)}, bf16[64,1536]{1,0:T(8,128)(2,1)S(1)}, u32[]{:S(2)}, u32[]{:S(2)}) collective-permute-start(bf16[64,1536]{1,0:T(8,128)(2,1)S(1)} %get-tuple-element.42), channel_id=1, source_target_pairs={{0,16},{4,20},{8,24},{12,28},{16,0},{20,4},{24,8},{28,12},{1,17},{... | collective-permute-start | bytes 589832 | tf_op jit(solution)/shard_map/ppermute | solution.py:102
  7.2 30.8 %collective-permute-start.19 = (bf16[64,1536]{1,0:T(8,128)(2,1)S(1)}, bf16[64,1536]{1,0:T(8,128)(2,1)S(1)}, u32[]{:S(2)}, u32[]{:S(2)}) collective-permute-start(bf16[64,1536]{1,0:T(8,128)(2,1)S(1)} %get-tuple-element.39), channel_id=1, source_target_pairs={{0,16},{4,20},{8,24},{12,28},{16,0},{20,4},{24,8},{28,12},{1,17},{... | collective-permute-start | bytes 589832 | tf_op jit(solution)/shard_map/ppermute | solution.py:102
  9.8 31.2 %collective-permute-start.7 = (bf16[64,1536]{1,0:T(8,128)(2,1)S(1)}, bf16[64,1536]{1,0:T(8,128)(2,1)S(1)}, u32[]{:S(2)}, u32[]{:S(2)}) collective-permute-start(bf16[64,1536]{1,0:T(8,128)(2,1)S(1)} %get-tuple-element.40), channel_id=1, source_target_pairs={{0,16},{4,20},{8,24},{12,28},{16,0},{20,4},{24,8},{28,12},{1,17},{... | collective-permute-start | bytes 589832 | tf_op jit(solution)/shard_map/ppermute | solution.py:102
  29.6 12.0 %collective-permute-start.1 = (bf16[64,1536]{1,0:T(8,128)(2,1)S(1)}, bf16[64,1536]{1,0:T(8,128)(2,1)S(1)}, u32[]{:S(2)}, u32[]{:S(2)}) collective-permute-start(bf16[64,1536]{1,0:T(8,128)(2,1)S(1)} %collective-permute-done), channel_id=1, source_target_pairs={{0,4},{4,0},{8,12},{12,8},{16,20},{20,16},{24,28},{28,24},{1,5},{5... | collective-permute-start | bytes 589832 | tf_op jit(solution)/shard_map/ppermute | solution.py:105
  33.8 7.8 %collective-permute-start.14 = (bf16[64,1536]{1,0:T(8,128)(2,1)S(1)}, bf16[64,1536]{1,0:T(8,128)(2,1)S(1)}, u32[]{:S(2)}, u32[]{:S(2)}) collective-permute-start(bf16[64,1536]{1,0:T(8,128)(2,1)S(1)} %collective-permute-done.13), channel_id=1, source_target_pairs={{0,4},{4,0},{8,12},{12,8},{16,20},{20,16},{24,28},{28,24},{1,5},{5... | collective-permute-start | bytes 589832 | tf_op jit(solution)/shard_map/ppermute | solution.py:105
  38.0 6.7 %collective-permute-start.20 = (bf16[64,1536]{1,0:T(8,128)(2,1)S(1)}, bf16[64,1536]{1,0:T(8,128)(2,1)S(1)}, u32[]{:S(2)}, u32[]{:S(2)}) collective-permute-start(bf16[64,1536]{1,0:T(8,128)(2,1)S(1)} %collective-permute-done.19), channel_id=1, source_target_pairs={{0,4},{4,0},{8,12},{12,8},{16,20},{20,16},{24,28},{28,24},{1,5},{5... | collective-permute-start | bytes 589832 | tf_op jit(solution)/shard_map/ppermute | solution.py:105
  41.1 6.8 %collective-permute-start.8 = (bf16[64,1536]{1,0:T(8,128)(2,1)S(1)}, bf16[64,1536]{1,0:T(8,128)(2,1)S(1)}, u32[]{:S(2)}, u32[]{:S(2)}) collective-permute-start(bf16[64,1536]{1,0:T(8,128)(2,1)S(1)} %collective-permute-done.7), channel_id=1, source_target_pairs={{0,4},{4,0},{8,12},{12,8},{16,20},{20,16},{24,28},{28,24},{1,5},{5... | collective-permute-start | bytes 589832 | tf_op jit(solution)/shard_map/ppermute | solution.py:105
  49.0 12.4 %collective-permute-start.3 = (bf16[2,64,1536]{2,1,0:T(8,128)(2,1)}, bf16[2,64,1536]{2,1,0:T(8,128)(2,1)}, u32[]{:S(2)}, u32[]{:S(2)}) collective-permute-start(bf16[2,64,1536]{2,1,0:T(8,128)(2,1)} %pad_maximum_fusion), channel_id=1, source_target_pairs={{0,8},{4,12},{8,0},{12,4},{16,24},{20,28},{24,16},{28,20},{1,9},{5... | collective-permute-start | bytes 1179656 | tf_op jit(solution)/shard_map/ppermute | solution.py:120
  50.6 4.5 %copy-start.11 = (f32[8]{0:T(128)S(1)}, f32[8]{0:T(128)}, u32[]{:S(2)}) copy-start(f32[8]{0:T(128)} %param.8) | copy-start | bytes 100
  50.6 19.3 %collective-permute-start.15 = (bf16[2,64,1536]{2,1,0:T(8,128)(2,1)}, bf16[2,64,1536]{2,1,0:T(8,128)(2,1)}, u32[]{:S(2)}, u32[]{:S(2)}) collective-permute-start(bf16[2,64,1536]{2,1,0:T(8,128)(2,1)} %pad_maximum_fusion.2), channel_id=1, source_target_pairs={{0,8},{4,12},{8,0},{12,4},{16,24},{20,28},{24,16},{28,20},{1,9},{5... | collective-permute-start | bytes 1179656 | tf_op jit(solution)/shard_map/ppermute | solution.py:120
  52.8 25.4 %collective-permute-start.9 = (bf16[2,64,1536]{2,1,0:T(8,128)(2,1)}, bf16[2,64,1536]{2,1,0:T(8,128)(2,1)}, u32[]{:S(2)}, u32[]{:S(2)}) collective-permute-start(bf16[2,64,1536]{2,1,0:T(8,128)(2,1)} %pad_maximum_fusion.1), channel_id=1, source_target_pairs={{0,8},{4,12},{8,0},{12,4},{16,24},{20,28},{24,16},{28,20},{1,9},{5... | collective-permute-start | bytes 1179656 | tf_op jit(solution)/shard_map/ppermute | solution.py:120
  53.6 31.0 %collective-permute-start.21 = (bf16[2,64,1536]{2,1,0:T(8,128)(2,1)S(1)}, bf16[2,64,1536]{2,1,0:T(8,128)(2,1)S(1)}, u32[]{:S(2)}, u32[]{:S(2)}) collective-permute-start(bf16[2,64,1536]{2,1,0:T(8,128)(2,1)S(1)} %pad_maximum_fusion.3), channel_id=1, source_target_pairs={{0,8},{4,12},{8,0},{12,4},{16,24},{20,28},{24,16},{28,20},{1,9},{5... | collective-permute-start | bytes 1179656 | tf_op jit(solution)/shard_map/ppermute | solution.py:120
  84.6 0.7 copy-start.12
  85.3 4.5 %copy-start.13 = (f32[2]{0:T(128)S(1)}, f32[2]{0:T(128)}, u32[]{:S(2)}) copy-start(f32[2]{0:T(128)} %gather_fusion.1) | copy-start | bytes 28
  87.7 36.2 %copy-start.1 = (bf16[2,64,1536]{2,1,0:T(8,128)(2,1)}, bf16[2,64,1536]{2,1,0:T(8,128)(2,1)S(1)}, u32[]{:S(2)}) copy-start(bf16[2,64,1536]{2,1,0:T(8,128)(2,1)S(1)} %get-tuple-element.45.refs_2_) | copy-start | bytes 1179652
  87.7 36.2 %copy-start.3 = (bf16[2,64,1536]{2,1,0:T(8,128)(2,1)}, bf16[2,64,1536]{2,1,0:T(8,128)(2,1)S(1)}, u32[]{:S(2)}) copy-start(bf16[2,64,1536]{2,1,0:T(8,128)(2,1)S(1)} %get-tuple-element.43.refs_2_) | copy-start | bytes 1179652
  87.7 12.1 %collective-permute-start.23 = (bf16[2,64,1536]{2,1,0:T(8,128)(2,1)S(1)}, bf16[2,64,1536]{2,1,0:T(8,128)(2,1)S(1)}, u32[]{:S(2)}, u32[]{:S(2)}) collective-permute-start(bf16[2,64,1536]{2,1,0:T(8,128)(2,1)S(1)} %get-tuple-element.43.refs_2_), channel_id=1, source_target_pairs={{0,2},{1,3},{2,0},{3,1},{4,6},{5,7},{6,4},{7,5},{8,10},{9,11},{10,... | collective-permute-start | bytes 1179656 | tf_op jit(solution)/shard_map/ppermute | solution.py:127
  89.2 12.1 %collective-permute-start.22 = (bf16[2,64,1536]{2,1,0:T(8,128)(2,1)S(1)}, bf16[2,64,1536]{2,1,0:T(8,128)(2,1)S(1)}, u32[]{:S(2)}, u32[]{:S(2)}) collective-permute-start(bf16[2,64,1536]{2,1,0:T(8,128)(2,1)S(1)} %get-tuple-element.43.refs_2_), channel_id=1, source_target_pairs={{0,1},{1,0},{2,3},{3,2},{4,5},{5,4},{6,7},{7,6},{8,9},{9,8},{10,11... | collective-permute-start | bytes 1179656 | tf_op jit(solution)/shard_map/ppermute | solution.py:127
  89.9 18.3 %collective-permute-start.17 = (bf16[2,64,1536]{2,1,0:T(8,128)(2,1)S(1)}, bf16[2,64,1536]{2,1,0:T(8,128)(2,1)}, u32[]{:S(2)}, u32[]{:S(2)}) collective-permute-start(bf16[2,64,1536]{2,1,0:T(8,128)(2,1)S(1)} %get-tuple-element.45.refs_2_), channel_id=1, source_target_pairs={{0,2},{1,3},{2,0},{3,1},{4,6},{5,7},{6,4},{7,5},{8,10},{9,11},{10,... | collective-permute-start | bytes 1179656 | tf_op jit(solution)/shard_map/ppermute | solution.py:127
  90.5 19.9 %collective-permute-start.16 = (bf16[2,64,1536]{2,1,0:T(8,128)(2,1)S(1)}, bf16[2,64,1536]{2,1,0:T(8,128)(2,1)S(1)}, u32[]{:S(2)}, u32[]{:S(2)}) collective-permute-start(bf16[2,64,1536]{2,1,0:T(8,128)(2,1)S(1)} %get-tuple-element.45.refs_2_), channel_id=1, source_target_pairs={{0,1},{1,0},{2,3},{3,2},{4,5},{5,4},{6,7},{7,6},{8,9},{9,8},{10,11... | collective-permute-start | bytes 1179656 | tf_op jit(solution)/shard_map/ppermute | solution.py:127
  90.7 26.0 %collective-permute-start.11 = (bf16[2,64,1536]{2,1,0:T(8,128)(2,1)}, bf16[2,64,1536]{2,1,0:T(8,128)(2,1)}, u32[]{:S(2)}, u32[]{:S(2)}) collective-permute-start(bf16[2,64,1536]{2,1,0:T(8,128)(2,1)} %get-tuple-element.44.refs_2_), channel_id=1, source_target_pairs={{0,2},{1,3},{2,0},{3,1},{4,6},{5,7},{6,4},{7,5},{8,10},{9,11},{10,... | collective-permute-start | bytes 1179656 | tf_op jit(solution)/shard_map/ppermute | solution.py:127
  99.7 24.2 %copy-start.5 = (bf16[2,64,1536]{2,1,0:T(8,128)(2,1)}, bf16[2,64,1536]{2,1,0:T(8,128)(2,1)S(1)}, u32[]{:S(2)}) copy-start(bf16[2,64,1536]{2,1,0:T(8,128)(2,1)S(1)} %collective-permute-done.23.refs_4_) | copy-start | bytes 1179652
  99.7 22.5 %collective-permute-start.5 = (bf16[2,64,1536]{2,1,0:T(8,128)(2,1)S(1)}, bf16[2,64,1536]{2,1,0:T(8,128)(2,1)}, u32[]{:S(2)}, u32[]{:S(2)}) collective-permute-start(bf16[2,64,1536]{2,1,0:T(8,128)(2,1)S(1)} %get-tuple-element.46.refs_2_), channel_id=1, source_target_pairs={{0,2},{1,3},{2,0},{3,1},{4,6},{5,7},{6,4},{7,5},{8,10},{9,11},{10,... | collective-permute-start | bytes 1179656 | tf_op jit(solution)/shard_map/ppermute | solution.py:127
  101.2 22.7 %copy-start.7 = (bf16[2,64,1536]{2,1,0:T(8,128)(2,1)}, bf16[2,64,1536]{2,1,0:T(8,128)(2,1)S(1)}, u32[]{:S(2)}) copy-start(bf16[2,64,1536]{2,1,0:T(8,128)(2,1)S(1)} %collective-permute-done.22.refs_3_) | copy-start | bytes 1179652
  101.2 21.0 %collective-permute-start.24 = (bf16[2,64,1536]{2,1,0:T(8,128)(2,1)S(1)}, bf16[2,64,1536]{2,1,0:T(8,128)(2,1)}, u32[]{:S(2)}, u32[]{:S(2)}) collective-permute-start(bf16[2,64,1536]{2,1,0:T(8,128)(2,1)S(1)} %collective-permute-done.23.refs_4_), channel_id=1, source_target_pairs={{0,1},{1,0},{2,3},{3,2},{4,5},{5,4},{6,7},{7,6},{8,9},{9,8},{10,11... | collective-permute-start | bytes 1179656 | tf_op jit(solution)/shard_map/ppermute | solution.py:127
  108.3 27.9 %collective-permute-start.18 = (bf16[2,64,1536]{2,1,0:T(8,128)(2,1)}, bf16[2,64,1536]{2,1,0:T(8,128)(2,1)}, u32[]{:S(2)}, u32[]{:S(2)}) collective-permute-start(bf16[2,64,1536]{2,1,0:T(8,128)(2,1)} %collective-permute-done.17.refs_4_), channel_id=1, source_target_pairs={{0,1},{1,0},{2,3},{3,2},{4,5},{5,4},{6,7},{7,6},{8,9},{9,8},{10,11... | collective-permute-start | bytes 1179656 | tf_op jit(solution)/shard_map/ppermute | solution.py:127
  110.4 13.5 %copy-start.9 = (bf16[2,64,1536]{2,1,0:T(8,128)(2,1)}, bf16[2,64,1536]{2,1,0:T(8,128)(2,1)S(1)}, u32[]{:S(2)}) copy-start(bf16[2,64,1536]{2,1,0:T(8,128)(2,1)S(1)} %collective-permute-done.16.refs_3_) | copy-start | bytes 1179652
  110.4 29.7 %collective-permute-start.10 = (bf16[2,64,1536]{2,1,0:T(8,128)(2,1)}, bf16[2,64,1536]{2,1,0:T(8,128)(2,1)}, u32[]{:S(2)}, u32[]{:S(2)}) collective-permute-start(bf16[2,64,1536]{2,1,0:T(8,128)(2,1)} %get-tuple-element.44.refs_2_), channel_id=1, source_target_pairs={{0,1},{1,0},{2,3},{3,2},{4,5},{5,4},{6,7},{7,6},{8,9},{9,8},{10,11... | collective-permute-start | bytes 1179656 | tf_op jit(solution)/shard_map/ppermute | solution.py:127
  116.7 27.6 %collective-permute-start.4 = (bf16[2,64,1536]{2,1,0:T(8,128)(2,1)S(1)}, bf16[2,64,1536]{2,1,0:T(8,128)(2,1)}, u32[]{:S(2)}, u32[]{:S(2)}) collective-permute-start(bf16[2,64,1536]{2,1,0:T(8,128)(2,1)S(1)} %get-tuple-element.46.refs_2_), channel_id=1, source_target_pairs={{0,1},{1,0},{2,3},{3,2},{4,5},{5,4},{6,7},{7,6},{8,9},{9,8},{10,11... | collective-permute-start | bytes 1179656 | tf_op jit(solution)/shard_map/ppermute | solution.py:127
  122.2 17.9 %collective-permute-start.12 = (bf16[2,64,1536]{2,1,0:T(8,128)(2,1)}, bf16[2,64,1536]{2,1,0:T(8,128)(2,1)}, u32[]{:S(2)}, u32[]{:S(2)}) collective-permute-start(bf16[2,64,1536]{2,1,0:T(8,128)(2,1)} %collective-permute-done.11.refs_4_), channel_id=1, source_target_pairs={{0,1},{1,0},{2,3},{3,2},{4,5},{5,4},{6,7},{7,6},{8,9},{9,8},{10,11... | collective-permute-start | bytes 1179656 | tf_op jit(solution)/shard_map/ppermute | solution.py:127
  122.2 22.1 %collective-permute-start.6 = (bf16[2,64,1536]{2,1,0:T(8,128)(2,1)}, bf16[2,64,1536]{2,1,0:T(8,128)(2,1)}, u32[]{:S(2)}, u32[]{:S(2)}) collective-permute-start(bf16[2,64,1536]{2,1,0:T(8,128)(2,1)} %collective-permute-done.5.refs_4_), channel_id=1, source_target_pairs={{0,1},{1,0},{2,3},{3,2},{4,5},{5,4},{6,7},{7,6},{8,9},{9,8},{10,11... | collective-permute-start | bytes 1179656 | tf_op jit(solution)/shard_map/ppermute | solution.py:127
  129.9 1.0 copy-start.4
  130.9 1.0 copy-start.6
  131.9 1.0 copy-start.8
  132.9 3.3 %copy-start.2 = (bf16[2,64,1536]{2,1,0:T(8,128)(2,1)S(1)}, bf16[2,64,1536]{2,1,0:T(8,128)(2,1)}, u32[]{:S(2)}) copy-start(bf16[2,64,1536]{2,1,0:T(8,128)(2,1)} %copy-done.1) | copy-start | bytes 1179652
  132.9 3.3 %copy-start.10 = (bf16[2,64,1536]{2,1,0:T(8,128)(2,1)S(1)}, bf16[2,64,1536]{2,1,0:T(8,128)(2,1)}, u32[]{:S(2)}) copy-start(bf16[2,64,1536]{2,1,0:T(8,128)(2,1)} %copy-done.9) | copy-start | bytes 1179652

commit v2 on v1

v2 whole, which is shorter than its diff:
```python
import jax
import jax.numpy as jnp
from jax import lax
from jax.experimental import pallas as pl
from jax.experimental.pallas import tpu as pltpu
from jax.sharding import PartitionSpec as P

TILE = 64
SHARES = (2, 2, 2, 2)
PACE = 2
FL, BY = 10**10, 1
NEAR_FIRST = 1
TAIL = 2
XWAIT = 2
GATE = 0
VMEM = pl.BlockSpec(memory_space=pltpu.VMEM)
SMEM = pl.BlockSpec(memory_space=pltpu.SMEM)
ANY = pl.BlockSpec(memory_space=pl.ANY)


def send(value, axis, mask):
    return lax.ppermute(value, axis, [(i, i ^ mask) for i in range(lax.axis_size(axis))])


def after(value, *earlier):
    return lax.optimization_barrier((value, *earlier))[0] if earlier else value


def turn(x, index, axis):
    size = x.shape[axis]
    step = 1
    while step < size:
        shape = x.shape[:axis] + (size // (2 * step), 2, step) + x.shape[axis + 1 :]
        flipped = jnp.flip(x.reshape(shape), axis + 1).reshape(x.shape)
        x = jnp.where((index & step) != 0, flipped, x)
        step *= 2
    return x


class Chain:
    def __init__(self):
        self.last = []

    def call(self, kernel, smem, arrays, outs, name, waits=()):
        waits = [*self.last, *waits]
        count = len(smem) + len(arrays)

        def run(*refs):
            kernel(*refs[:count], *refs[count + len(waits) :])

        result = pl.pallas_call(
            run,
            out_shape=tuple(outs),
            in_specs=[SMEM] * len(smem) + [VMEM] * len(arrays) + [ANY] * len(waits),
            out_specs=(VMEM,) * len(outs),
            compiler_params=pltpu.CompilerParams(vmem_limit_bytes=40 * 1024 * 1024),
            cost_estimate=pl.CostEstimate(flops=FL, bytes_accessed=BY, transcendentals=0),
            name=name,
        )(*smem, *arrays, *waits)
        self.last = [result[0]]
        return result


def part_kernel(*refs, row_count, added):
    left_ref, gap_ref, table_ref, right_ref, key_ref = refs[:5]
    row_refs = refs[5 : 5 + row_count]
    added_refs = refs[5 + row_count : 5 + row_count + added]
    out_refs = refs[5 + row_count + added :]
    rows = jnp.concatenate([r[...] for r in row_refs], axis=0)
    scores = lax.dot_general(
        left_ref[...], rows, (((1,), (1,)), ((), ())), preferred_element_type=jnp.float32
    )
    key = key_ref[...]
    ids = lax.broadcasted_iota(jnp.int32, (table_ref.shape[1], key.shape[1]), 0)
    one_hot = (ids == key).astype(jnp.float32).astype(jnp.bfloat16)
    listed = jnp.dot(table_ref[...], one_hot, preferred_element_type=jnp.float32)
    gap = gap_ref[...] + right_ref[...]
    amplitude = jnp.where(listed > 0.5, scores / gap, 0.0).astype(jnp.bfloat16)
    part = jnp.dot(amplitude, rows, preferred_element_type=jnp.float32)
    for ref in added_refs:
        part += ref[...]
    at = 0
    for ref in out_refs:
        ref[...] = part[at : at + ref.shape[0]]
        at += ref.shape[0]


def body(integrals, occupied_energy, virtual_energy, partner_list, tile_lists):
    orbitals, slice_rows, aux = integrals.shape
    occ_count = lax.axis_size("occ")
    virt_count = lax.axis_size("virt")
    myself = lax.axis_index("occ")
    slice_id = lax.axis_index("virt")
    a_count = slice_rows // TILE
    b_count = virtual_energy.shape[0] // TILE
    pairings = partner_list.shape[0]
    bits = occ_count.bit_length() - 1
    place_bits = bits // 2
    unit = 1 << (bits - place_bits - 1)
    places = 1 << place_bits
    half = occ_count // 2
    column_masks = [1 << i for i in range(bits - place_bits - 1)]
    place = (myself // unit) % places
    piece = slice_rows // places
    shares = SHARES if piece >= 16 * sum(SHARES) else (1,)
    count = len(shares)
    edges = [piece * sum(shares[:c]) // sum(shares) for c in range(count + 1)]
    spans = list(zip(edges[:-1], edges[1:]))
    x_order = [m for m in range(virt_count) if not m & 1]

    def block(n):
        return jax.ShapeDtypeStruct((n, aux), jnp.bfloat16)

    own = integrals.reshape(slice_rows, aux)
    ids = jnp.stack([myself, place]).astype(jnp.int32)
    chain = Chain()

    def cut(ids_ref, own_ref, *out_refs):
        for m in range(places):
            at = pl.multiple_of((ids_ref[1] ^ m) * piece, piece)
            data = own_ref[pl.ds(at, piece), :]
            out_refs[m][...] = data
            for c, (lo, hi) in enumerate(spans):
                out_refs[places + c * places + m][...] = data[lo:hi]

    cuts = chain.call(cut, [ids], [own], [block(piece)] * places + [block(hi - lo) for lo, hi in spans for _ in range(places)], "cut")
    turned = cuts[:places]

    def start_far(c, *deps):
        return [
            send(after(cuts[places + c * places + m], *deps), "occ", half ^ (m * unit)) for m in range(places)
        ]

    lists = tile_lists[:, 0, 0]
    lists_beside = send(lists, "virt", 1)
    beside = send(own, "virt", 1) if count > TAIL else None
    far = {0: start_far(0)}
    near = []
    for m in range(1, places):
        split = edges[NEAR_FIRST] if count > 1 else piece
        first = send(turned[m][:split], "occ", m * unit)
        near.append([(0, first)])
    own_side = {}
    for mask in column_masks:
        for m in [0, *own_side]:
            mine = own_side[m] if m else after(turned[0], *([lists_beside, beside] if count > TAIL else []))
            own_side[m ^ mask] = send(mine, "occ", mask)
    for c in range(1, min(PACE, count)):
        far[c] = start_far(c)

    partner_energy = jnp.take(occupied_energy, jnp.take(partner_list, myself, axis=1), axis=0)
    own_energy = lax.dynamic_index_in_dim(occupied_energy, myself, 0, False)

    def left_side(entries):
        pair_ids = jnp.arange(a_count * b_count, dtype=jnp.int32)
        listed = jnp.any(entries[:, :, None] == pair_ids[None, None, :], axis=1)
        table = listed.reshape(pairings, a_count, b_count).transpose(1, 0, 2)
        return jnp.repeat(table.reshape(a_count, pairings * b_count), TILE, axis=0).astype(jnp.bfloat16)

    energies = turn(turn(virtual_energy.reshape(virt_count, places, piece), slice_id, 0), place, 1)
    energy_mine = turn(virtual_energy.reshape(virt_count, slice_rows), slice_id, 0)
    table = jnp.concatenate([left_side(lists), left_side(lists_beside)], axis=0)
    gap_left = energy_mine[:2].reshape(-1, 1) - own_energy
    right = energies[:, None] - partner_energy[None, :, None, None]
    virt_at = (slice_id ^ jnp.arange(virt_count, dtype=jnp.int32))[:, None, None]
    place_at = (place ^ jnp.arange(places, dtype=jnp.int32))[None, :, None]
    row = (virt_at * places + place_at) * piece + jnp.arange(piece, dtype=jnp.int32)
    key = jnp.arange(pairings, dtype=jnp.int32)[None, :, None, None] * b_count + row[:, None] // TILE

    def column(x, order, chunks):
        return jnp.concatenate([x[m, :, :, slice(*spans[c])].reshape(1, -1) for c in chunks for m in order], axis=1)

    early = list(range(count - TAIL))
    late = list(range(max(count - TAIL, 0), count))
    full_order = x_order + [m ^ 1 for m in x_order]
    set_last = (gap_left[:slice_rows], table[:slice_rows], column(right, full_order, late), column(key, full_order, late))
    set_early = (gap_left, table, column(right, x_order, early), column(key, x_order, early)) if early else ()

    def add_part(left, sides, row_refs, added, outs, name, waits=()):
        arrays = [left, *sides, *row_refs, *added]

        def kernel(*refs):
            part_kernel(*refs, row_count=len(row_refs), added=len(added))

        shapes = [jax.ShapeDtypeStruct((n, aux), jnp.float32) for n in outs]
        return chain.call(kernel, [], arrays, shapes, name, waits)

    far_masks = [half ^ (m * unit) for m in range(places)]
    near_masks = [m * unit for m in range(1, places)]
    group = near_masks + far_masks
    side, got, local, value, wide = {}, {}, {}, {}, {}

    def near_of(t, m):
        at, value = [(at, v) for at, v in near[m] if at <= spans[t][0]][-1]
        return value, spans[t][0] - at

    def stack_side(t):
        lo, hi = spans[t]
        rows = hi - lo
        nears = [near_of(t, m) for m in range(places - 1)]

        def kernel(*refs):
            *in_refs, out_ref = refs
            for i, ref in enumerate(in_refs):
                at = nears[i][1] if i < len(nears) else 0
                out_ref[i * rows : (i + 1) * rows, :] = ref[at : at + rows, :]

        waits = [*set_last, *set_early] if t == 0 else []
        arrays = [v for v, _ in nears] + far[t]
        out = chain.call(kernel, [], arrays, [block(len(group) * rows)], f"stack{t}", waits)[0]
        if t == 0 and count > 1:
            for m in range(1, places):
                split = edges[NEAR_FIRST]
                near[m - 1].append((split, send(after(turned[m][split:], out), "occ", m * unit)))
        stacked = {0: out}
        for mask in column_masks:
            for m in list(stacked):
                stacked[m ^ mask] = send(stacked[m], "occ", mask)
        side[t] = {col: v for col, v in stacked.items() if col}
        return out

    def choose(t):
        lo, hi = spans[t]
        rows = hi - lo
        sources = [(0, turned[0], lo)]
        sources += [(m, v, lo) for m, v in own_side.items()]
        sources += [(m, *near_of(t, i)) for i, m in enumerate(near_masks)]
        sources += [(m, v, 0) for m, v in zip(far_masks, far[t])]
        arrays = [v for _, v, _ in sources]
        for col, v in side[t].items():
            sources += [(m ^ col, len(arrays), i * rows) for i, m in enumerate(group)]
            arrays.append(v)

        def kernel(ids_ref, partner_ref, *refs):
            in_refs, out_refs = refs[: len(arrays)], refs[len(arrays) :]
            for m in range(places):
                for k in range(pairings):
                    here = partner_ref[k, ids_ref[0] ^ (m * unit)] ^ ids_ref[0]
                    for i, (mask, which, at) in enumerate(sources):
                        ref = in_refs[which] if isinstance(which, int) else in_refs[i]

                        @pl.when(here == mask)
                        def _(ref=ref, at=at, k=k, m=m):
                            out_refs[m][k * rows : (k + 1) * rows, :] = ref[at : at + rows, :]

        waits = wide[t - XWAIT] if t >= XWAIT else []
        outs = chain.call(kernel, [ids, partner_list], arrays, [block(pairings * rows)] * places, f"choose{t}", waits)
        local[t] = outs[0]
        got[t] = [send(outs[m], "occ", m * unit) for m in range(1, places)]
        return outs[0]

    def join(t, waits=()):
        rows = spans[t][1] - spans[t][0]

        def kernel(*refs):
            *in_refs, out_ref = refs
            for m, ref in enumerate(in_refs):
                for k in range(pairings):
                    at = (k * places + m) * rows
                    out_ref[at : at + rows, :] = ref[k * rows : (k + 1) * rows, :]

        value[t] = chain.call(
            kernel, [], [local[t], *got[t]], [block(pairings * places * rows)], f"join{t}", waits
        )[0]
        ready = {0: value[t]}
        mask = virt_count // 2
        while mask > 1:
            for m in list(ready):
                ready[m ^ mask] = send(ready[m], "virt", mask)
            mask //= 2
        wide[t] = [ready[m] for m in x_order]

    added = []
    for t in range(count):
        stack_side(t)
        if GATE == 0 and t + PACE < count:
            far[t + PACE] = start_far(t + PACE, *chain.last)
        if t:
            join(t - 1)
        if GATE == 1 and t + PACE < count:
            far[t + PACE] = start_far(t + PACE, *chain.last)
        choose(t)
        if GATE == 2 and t + PACE < count:
            far[t + PACE] = start_far(t + PACE, *chain.last)
    if early:
        lefts = jnp.concatenate([own, beside], axis=0)
        mine, other = add_part(
            lefts, set_early, [v for c in early for v in wide[c]], [], [slice_rows] * 2, "early"
        )
        added = [mine, send(other, "virt", 1)]
    join(count - 1)
    final = [v for c in late for v in wide[c] + [send(w, "virt", 1) for w in wide[c]]]
    return add_part(own, set_last, final, added, [slice_rows], "last")[0][None]


def solution(mesh):
    return jax.shard_map(
        body,
        mesh=mesh,
        in_specs=(P("occ", "virt", None), P(), P(), P(), P(None, "occ", "virt", None)),
        out_specs=P("occ", "virt", None),
        check_vma=False,
    )
```

time: 149 us -> 89.8 us (0.60)
  waiting for transfers between devices: 83.1 us -> 37.7 us
  starting transfers between devices: 21.1 us -> 35.3 us
  local copies, waits for them, and re-layouts: 16.8 us -> 5.59 us
  other arithmetic: 9.25 us -> 1.62 us
  Pallas kernels: 15.4 us -> 8.92 us
  between operations: 2.73 us -> 0.51 us
    ppermute x25 -> x30, waiting for transfers between devices: 83.1 us -> 37.7 us  [send(): lax.ppermute(value, axis, [(i, i ^ mask) for i in range(lax.axis_size(axi...]
    ppermute x25 -> x30, starting transfers between devices: 21.1 us -> 35.3 us  [send(): lax.ppermute(value, axis, [(i, i ^ mask) for i in range(lax.axis_size(axi...]
    pallas_call x4 -> x15, Pallas kernels: 15.4 us -> 8.92 us  [call(): pl.pallas_call(run, out_shape=tuple(outs), in_specs=[SMEM] * len(smem) +...]
    transpose x5 -> x0, local copies, waits for them, and re-layouts: 5.27 us -> none  [body(): weights[:, :, :, lo:lo + rows].transpose(1, 2, 0, 3).reshape(slice_rows, -1)]
    select_n x7, other arithmetic: 3.92 us -> 0.32 us  [the longest x1 0.19 us: body(): jnp.take(partner_list, myself, axis=1)]
    another operation x9 -> x1, other arithmetic: 2.98 us -> 0.07 us  [body(): ids = jnp.stack([myself, place]).astype(jnp.int32)]
    unnamed x28 -> x34, local copies, waits for them, and re-layouts: 3.76 us -> 1.46 us
    another operation x0 -> x26, local copies, waits for them, and re-layouts: none -> 2.02 us  [the longest x24 1.98 us: column(): x[m, :, :, slice(*spans[c])].reshape(1, -1)]
  transfers between devices with their start and end apart: 25 -> 30, of which waited for: 14 -> 12; matrix products, arithmetic and copies ran while one was open for 13% -> 7% of each run, Pallas kernels for 8% -> 6%
where the time goes in v2:
time: 89.8 us; the launch traced here: 89.7 us
  waiting for transfers between devices  37.7 us (42%)
  starting transfers between devices  35.3 us (39%)
  Pallas kernels  8.92 us (10%)
  local copies, waits for them, and re-layouts  5.59 us (6%)
  other arithmetic  1.62 us (2%)
    ppermute x30, waiting for transfers between devices, send(): lax.ppermute(value, axis, [(i, i ^ mask) for i in range(lax.axis_size(axi...  37.7 us
    ppermute x30, starting transfers between devices, send(): lax.ppermute(value, axis, [(i, i ^ mask) for i in range(lax.axis_size(axi...  35.3 us
    pallas_call x15, Pallas kernels, call(): pl.pallas_call(run, out_shape=tuple(outs), in_specs=[SMEM] * len(smem) +...  8.92 us
    another operation x24, local copies, waits for them, and re-layouts, column(): x[m, :, :, slice(*spans[c])].reshape(1, -1)  1.98 us
  transfers between devices with their start and end apart: 30, of which 12 were waited for; matrix products, arithmetic and copies ran while one was open for 7% of the time, Pallas kernels for 6%

profile of v2, /device:TPU:0, one launch (start us, length us, event | category | flops | bytes accessed | tf_op | source)
XLA Modules:
  0.0 89.7 jit_solution(9603569413543973611)
XLA Ops:
  0.0 0.5 collective-permute-start.1
  0.5 1.1 %copy-done = bf16[1,256,1536]{2,1,0:T(8,128)(2,1)S(1)} copy-done((bf16[1,256,1536]{2,1,0:T(8,128)(2,1)S(1)}, bf16[1,256,1536]{2,1,0:T(8,128)(2,1)}, u32[]{:S(2)}) %copy-start) | copy-done | bytes 786456
  1.7 0.7 cut.1
  2.3 2.6 %collective-permute-start.3 = (bf16[32,1536]{1,0:T(8,128)(2,1)S(1)}, bf16[32,1536]{1,0:T(8,128)(2,1)S(1)}, u32[]{:S(2)}, u32[]{:S(2)}) collective-permute-start(bf16[32,1536]{1,0:T(8,128)(2,1)S(1)} %slice.107), channel_id=1, source_target_pairs={{0,8},{4,12},{8,0},{12,4},{16,24},{20,28},{24,16},{28,20},{1,9},{5... | collective-permute-start | bytes 294920 | tf_op jit(solution)/shard_map/ppermute | solution.py:22
  5.0 2.6 %collective-permute-start.4 = (bf16[32,1536]{1,0:T(8,128)(2,1)S(1)}, bf16[32,1536]{1,0:T(8,128)(2,1)S(1)}, u32[]{:S(2)}, u32[]{:S(2)}) collective-permute-start(bf16[32,1536]{1,0:T(8,128)(2,1)S(1)} %get-tuple-element.34), channel_id=1, source_target_pairs={{0,16},{4,20},{8,24},{12,28},{16,0},{20,4},{24,8},{28,12},{1,17},{... | collective-permute-start | bytes 294920 | tf_op jit(solution)/shard_map/ppermute | solution.py:22
  7.9 0.2 fusion.5
  8.1 0.6 dynamic_slice.4
  8.7 0.6 gather_fusion
  12.2 0.7 fusion.3
  12.9 0.1 copy.31
  13.1 0.1 copy.29.refs_4_.refs_1_
  13.8 1.8 %collective-permute-start.2 = (bf16[128,1536]{1,0:T(8,128)(2,1)S(1)}, bf16[128,1536]{1,0:T(8,128)(2,1)S(1)}, u32[]{:S(2)}, u32[]{:S(2)}) collective-permute-start(bf16[128,1536]{1,0:T(8,128)(2,1)S(1)} %get-tuple-element.32.refs_3_.refs_2_), channel_id=1, source_target_pairs={{0,4},{4,0},{8,12},{12,8},{16,20},{20,16},{24,28},{28,24},{1,5},{5... | collective-permute-start | bytes 1179656 | tf_op jit(solution)/shard_map/ppermute | solution.py:22
  15.6 0.2 collective-permute-done.4.refs_1_.refs_5_
  15.8 1.6 %collective-permute-start.11 = (bf16[96,1536]{1,0:T(8,128)(2,1)S(1)}, bf16[96,1536]{1,0:T(8,128)(2,1)S(1)}, u32[]{:S(2)}, u32[]{:S(2)}) collective-permute-start(bf16[96,1536]{1,0:T(8,128)(2,1)S(1)} %stack0.1.refs_8_), channel_id=1, source_target_pairs={{0,4},{4,0},{8,12},{12,8},{16,20},{20,16},{24,28},{28,24},{1,5},{5... | collective-permute-start | bytes 884744 | tf_op jit(solution)/shard_map/ppermute | solution.py:22
  17.3 2.5 %collective-permute-start.10 = (bf16[32,1536]{1,0:T(8,128)(2,1)S(1)}, bf16[32,1536]{1,0:T(8,128)(2,1)S(1)}, u32[]{:S(2)}, u32[]{:S(2)}) collective-permute-start(bf16[32,1536]{1,0:T(8,128)(2,1)S(1)} %get-tuple-element.42), channel_id=1, source_target_pairs={{0,24},{4,28},{8,16},{12,20},{16,8},{20,12},{24,0},{28,4},{1,25},{... | collective-permute-start | bytes 294920 | tf_op jit(solution)/shard_map/ppermute | solution.py:22
  19.9 0.9 %collective-permute-start.9 = (bf16[32,1536]{1,0:T(8,128)(2,1)S(1)}, bf16[32,1536]{1,0:T(8,128)(2,1)S(1)}, u32[]{:S(2)}, u32[]{:S(2)}) collective-permute-start(bf16[32,1536]{1,0:T(8,128)(2,1)S(1)} %get-tuple-element.41), channel_id=1, source_target_pairs={{0,16},{4,20},{8,24},{12,28},{16,0},{20,4},{24,8},{28,12},{1,17},{... | collective-permute-start | bytes 294920 | tf_op jit(solution)/shard_map/ppermute | solution.py:22
  20.8 1.0 %collective-permute-start.6 = (bf16[96,1536]{1,0:T(8,128)(2,1)S(1)}, bf16[96,1536]{1,0:T(8,128)(2,1)S(1)}, u32[]{:S(2)}, u32[]{:S(2)}) collective-permute-start(bf16[96,1536]{1,0:T(8,128)(2,1)S(1)} %slice.106), channel_id=1, source_target_pairs={{0,8},{4,12},{8,0},{12,4},{16,24},{20,28},{24,16},{28,20},{1,9},{5... | collective-permute-start | bytes 884744 | tf_op jit(solution)/shard_map/ppermute | solution.py:22
  21.9 9.7 %collective-permute-done.11.refs_7_ = bf16[96,1536]{1,0:T(8,128)(2,1)S(1)} collective-permute-done((bf16[96,1536]{1,0:T(8,128)(2,1)S(1)}, bf16[96,1536]{1,0:T(8,128)(2,1)S(1)}, u32[]{:S(2)}, u32[]{:S(2)}) %collective-permute-start.11) | collective-permute-done | bytes 294944 | tf_op jit(solution)/shard_map/ppermute | solution.py:22
  31.7 3.8 %collective-permute-start.8 = (bf16[32,1536]{1,0:T(8,128)(2,1)S(1)}, bf16[32,1536]{1,0:T(8,128)(2,1)S(1)}, u32[]{:S(2)}, u32[]{:S(2)}) collective-permute-start(bf16[32,1536]{1,0:T(8,128)(2,1)S(1)} %get-tuple-element.40), channel_id=1, source_target_pairs={{0,24},{4,28},{8,16},{12,20},{16,8},{20,12},{24,0},{28,4},{1,25},{... | collective-permute-start | bytes 294920 | tf_op jit(solution)/shard_map/ppermute | solution.py:22
  35.5 0.7 choose0.1
  36.3 0.6 collective-permute-start.13
  36.9 1.8 %collective-permute-start.12 = (bf16[96,1536]{1,0:T(8,128)(2,1)S(1)}, bf16[96,1536]{1,0:T(8,128)(2,1)S(1)}, u32[]{:S(2)}, u32[]{:S(2)}) collective-permute-start(bf16[96,1536]{1,0:T(8,128)(2,1)S(1)} %stack1.1.refs_2_), channel_id=1, source_target_pairs={{0,4},{4,0},{8,12},{12,8},{16,20},{20,16},{24,28},{28,24},{1,5},{5... | collective-permute-start | bytes 884744 | tf_op jit(solution)/shard_map/ppermute | solution.py:22
  38.7 2.2 %collective-permute-start.18 = (bf16[32,1536]{1,0:T(8,128)(2,1)S(1)}, bf16[32,1536]{1,0:T(8,128)(2,1)S(1)}, u32[]{:S(2)}, u32[]{:S(2)}) collective-permute-start(bf16[32,1536]{1,0:T(8,128)(2,1)S(1)} %get-tuple-element.50), channel_id=1, source_target_pairs={{0,16},{4,20},{8,24},{12,28},{16,0},{20,4},{24,8},{28,12},{1,17},{... | collective-permute-start | bytes 294920 | tf_op jit(solution)/shard_map/ppermute | solution.py:22
  40.9 6.0 %collective-permute-done.13.refs_1_ = bf16[64,1536]{1,0:T(8,128)(2,1)S(1)} collective-permute-done((bf16[64,1536]{1,0:T(8,128)(2,1)S(1)}, bf16[64,1536]{1,0:T(8,128)(2,1)S(1)}, u32[]{:S(2)}, u32[]{:S(2)}) %collective-permute-start.13) | collective-permute-done | bytes 196640 | tf_op jit(solution)/shard_map/ppermute | solution.py:22
  46.9 2.8 %collective-permute-start.19 = (bf16[32,1536]{1,0:T(8,128)(2,1)S(1)}, bf16[32,1536]{1,0:T(8,128)(2,1)S(1)}, u32[]{:S(2)}, u32[]{:S(2)}) collective-permute-start(bf16[32,1536]{1,0:T(8,128)(2,1)S(1)} %get-tuple-element.52), channel_id=1, source_target_pairs={{0,24},{4,28},{8,16},{12,20},{16,8},{20,12},{24,0},{28,4},{1,25},{... | collective-permute-start | bytes 294920 | tf_op jit(solution)/shard_map/ppermute | solution.py:22
  49.7 1.6 %collective-permute-start.16 = (bf16[128,1536]{1,0:T(8,128)(2,1)S(1)}, bf16[128,1536]{1,0:T(8,128)(2,1)S(1)}, u32[]{:S(2)}, u32[]{:S(2)}) collective-permute-start(bf16[128,1536]{1,0:T(8,128)(2,1)S(1)} %join0.1.refs_8_.refs_9_.refs_5_), channel_id=1, source_target_pairs={{0,2},{1,3},{2,0},{3,1},{4,6},{5,7},{6,4},{7,5},{8,10},{9,11},{10,... | collective-permute-start | bytes 1179656 | tf_op jit(solution)/shard_map/ppermute | solution.py:22
  51.2 0.7 choose1.1
  52.1 1.6 %collective-permute-start.14 = (bf16[96,1536]{1,0:T(8,128)(2,1)S(1)}, bf16[96,1536]{1,0:T(8,128)(2,1)S(1)}, u32[]{:S(2)}, u32[]{:S(2)}) collective-permute-start(bf16[96,1536]{1,0:T(8,128)(2,1)S(1)} %stack2.1.refs_2_), channel_id=1, source_target_pairs={{0,4},{4,0},{8,12},{12,8},{16,20},{20,16},{24,28},{28,24},{1,5},{5... | collective-permute-start | bytes 884744 | tf_op jit(solution)/shard_map/ppermute | solution.py:22
  53.7 4.1 %collective-permute-done.15.refs_1_ = bf16[64,1536]{1,0:T(8,128)(2,1)S(1)} collective-permute-done((bf16[64,1536]{1,0:T(8,128)(2,1)S(1)}, bf16[64,1536]{1,0:T(8,128)(2,1)S(1)}, u32[]{:S(2)}, u32[]{:S(2)}) %collective-permute-start.15) | collective-permute-done | bytes 196640 | tf_op jit(solution)/shard_map/ppermute | solution.py:22
  57.8 1.2 %collective-permute-start.24 = (bf16[128,1536]{1,0:T(8,128)(2,1)S(1)}, bf16[128,1536]{1,0:T(8,128)(2,1)S(1)}, u32[]{:S(2)}, u32[]{:S(2)}) collective-permute-start(bf16[128,1536]{1,0:T(8,128)(2,1)S(1)} %join1.1.refs_8_.refs_9_.refs_7_), channel_id=1, source_target_pairs={{0,2},{1,3},{2,0},{3,1},{4,6},{5,7},{6,4},{7,5},{8,10},{9,11},{10,... | collective-permute-start | bytes 1179656 | tf_op jit(solution)/shard_map/ppermute | solution.py:22
  59.0 0.5 collective-permute-done.14.refs_7_
  59.6 0.9 %collective-permute-done.16.refs_10_.refs_6_ = bf16[128,1536]{1,0:T(8,128)(2,1)S(1)} collective-permute-done((bf16[128,1536]{1,0:T(8,128)(2,1)S(1)}, bf16[128,1536]{1,0:T(8,128)(2,1)S(1)}, u32[]{:S(2)}, u32[]{:S(2)}) %collective-permute-start.16) | collective-permute-done | bytes 393248 | tf_op jit(solution)/shard_map/ppermute | solution.py:22
  60.5 0.7 choose2.1
  61.2 0.9 collective-permute-start.17
  62.1 1.7 %collective-permute-start.23 = (bf16[96,1536]{1,0:T(8,128)(2,1)S(1)}, bf16[96,1536]{1,0:T(8,128)(2,1)S(1)}, u32[]{:S(2)}, u32[]{:S(2)}) collective-permute-start(bf16[96,1536]{1,0:T(8,128)(2,1)S(1)} %stack3.1.refs_2_), channel_id=1, source_target_pairs={{0,4},{4,0},{8,12},{12,8},{16,20},{20,16},{24,28},{28,24},{1,5},{5... | collective-permute-start | bytes 884744 | tf_op jit(solution)/shard_map/ppermute | solution.py:22
  63.9 3.1 %collective-permute-done.17.refs_1_ = bf16[64,1536]{1,0:T(8,128)(2,1)S(1)} collective-permute-done((bf16[64,1536]{1,0:T(8,128)(2,1)S(1)}, bf16[64,1536]{1,0:T(8,128)(2,1)S(1)}, u32[]{:S(2)}, u32[]{:S(2)}) %collective-permute-start.17) | collective-permute-done | bytes 196640 | tf_op jit(solution)/shard_map/ppermute | solution.py:22
  67.0 1.4 %collective-permute-start.20 = (bf16[128,1536]{1,0:T(8,128)(2,1)S(1)}, bf16[128,1536]{1,0:T(8,128)(2,1)S(1)}, u32[]{:S(2)}, u32[]{:S(2)}) collective-permute-start(bf16[128,1536]{1,0:T(8,128)(2,1)S(1)} %join2.1.refs_8_.refs_5_), channel_id=1, source_target_pairs={{0,2},{1,3},{2,0},{3,1},{4,6},{5,7},{6,4},{7,5},{8,10},{9,11},{10,... | collective-permute-start | bytes 1179656 | tf_op jit(solution)/shard_map/ppermute | solution.py:22
  68.4 0.5 collective-permute-done.23.refs_7_
  68.9 1.0 %collective-permute-done.24.refs_10_.refs_8_ = bf16[128,1536]{1,0:T(8,128)(2,1)S(1)} collective-permute-done((bf16[128,1536]{1,0:T(8,128)(2,1)S(1)}, bf16[128,1536]{1,0:T(8,128)(2,1)S(1)}, u32[]{:S(2)}, u32[]{:S(2)}) %collective-permute-start.24) | collective-permute-done | bytes 393248 | tf_op jit(solution)/shard_map/ppermute | solution.py:22
  69.9 0.7 choose3.1
  70.7 0.3 collective-permute-start.25
  71.0 2.0 %early.1 = (f32[256,1536]{1,0:T(8,128)S(1)}, f32[256,1536]{1,0:T(8,128)S(1)}) custom-call(bf16[512,1536]{1,0:T(8,128)(2,1)S(1)} %pad_maximum_fusion.refs_0_, f32[512,1]{1,0:T(8,128)S(1)} %bitcast.39, bf16[512,32]{1,0:T(8,128)(2,1)S(1)} %pad_maximum_fusion.1.refs_9_.refs_2_, f32[1,512]{1,0:T(1,128)S(1)} %constant_dynamic-update-slice_fusion.16.refs_10_.refs_3_, ...), custom_call_target="tpu_custom_call" | custom-call | flops 10000000000 | bytes 1 | tf_op jit(solution)/shard_map/early/pallas_call | solution.py:51
  73.0 3.4 %collective-permute-done.25.refs_1_ = bf16[64,1536]{1,0:T(8,128)(2,1)S(1)} collective-permute-done((bf16[64,1536]{1,0:T(8,128)(2,1)S(1)}, bf16[64,1536]{1,0:T(8,128)(2,1)S(1)}, u32[]{:S(2)}, u32[]{:S(2)}) %collective-permute-start.25) | collective-permute-done | bytes 196640 | tf_op jit(solution)/shard_map/ppermute | solution.py:22
  76.4 1.2 %collective-permute-start.26 = (bf16[128,1536]{1,0:T(8,128)(2,1)S(1)}, bf16[128,1536]{1,0:T(8,128)(2,1)S(1)}, u32[]{:S(2)}, u32[]{:S(2)}) collective-permute-start(bf16[128,1536]{1,0:T(8,128)(2,1)S(1)} %join3.1.refs_9_.refs_15_), channel_id=1, source_target_pairs={{0,2},{1,3},{2,0},{3,1},{4,6},{5,7},{6,4},{7,5},{8,10},{9,11},{10,... | collective-permute-start | bytes 1179656 | tf_op jit(solution)/shard_map/ppermute | solution.py:22
  77.7 0.5 collective-permute-start.27
  78.2 6.6 %collective-permute-done.26.refs_10_ = bf16[128,1536]{1,0:T(8,128)(2,1)S(1)} collective-permute-done((bf16[128,1536]{1,0:T(8,128)(2,1)S(1)}, bf16[128,1536]{1,0:T(8,128)(2,1)S(1)}, u32[]{:S(2)}, u32[]{:S(2)}) %collective-permute-start.26) | collective-permute-done | bytes 393248 | tf_op jit(solution)/shard_map/ppermute | solution.py:22
  84.8 1.7 %collective-permute-done.28.refs_12_ = bf16[128,1536]{1,0:T(8,128)(2,1)S(1)} collective-permute-done((bf16[128,1536]{1,0:T(8,128)(2,1)S(1)}, bf16[128,1536]{1,0:T(8,128)(2,1)S(1)}, u32[]{:S(2)}, u32[]{:S(2)}) %collective-permute-start.28) | collective-permute-done | bytes 393248 | tf_op jit(solution)/shard_map/ppermute | solution.py:22
  86.5 3.1 %last.1 = f32[256,1536]{1,0:T(8,128)} custom-call(bf16[256,1536]{1,0:T(8,128)(2,1)S(1)} %bitcast.37, f32[256,1]{1,0:T(8,128)S(1)} %copy.29.refs_4_.refs_1_, bf16[256,32]{1,0:T(8,128)(2,1)S(1)} %bitcast.42, f32[1,1024]{1,0:T(1,128)S(1)} %constant_dynamic-update-slice_fusion.refs_6_.refs_3_, s32[1,1024]{1,0:T(1,128)S(1)} %constant_dynamic-update-slice_fusion.8.refs_7_.refs_4_, ...), custom_call_target="tpu_custom_call" | custom-call | flops 10000000000 | bytes 1 | tf_op jit(solution)/shard_map/last/pallas_call | solution.py:51
  (137 shorter events, 4.1 us)
Async XLA Ops:
  0.0 13.8 %collective-permute-start.1 = (bf16[256,1536]{1,0:T(8,128)(2,1)}, bf16[256,1536]{1,0:T(8,128)(2,1)S(1)}, u32[]{:S(2)}, u32[]{:S(2)}) collective-permute-start(bf16[256,1536]{1,0:T(8,128)(2,1)} %bitcast.34), channel_id=1, source_target_pairs={{0,1},{1,0},{2,3},{3,2},{4,5},{5,4},{6,7},{7,6},{8,9},{9,8},{10,11... | collective-permute-start | bytes 2359304 | tf_op jit(solution)/shard_map/ppermute | solution.py:22
  0.5 1.1 %copy-start = (bf16[1,256,1536]{2,1,0:T(8,128)(2,1)S(1)}, bf16[1,256,1536]{2,1,0:T(8,128)(2,1)}, u32[]{:S(2)}) copy-start(bf16[1,256,1536]{2,1,0:T(8,128)(2,1)} %param.5) | copy-start | bytes 2359300
  1.7 5.9 %copy-start.5 = (s32[2,1,1,56]{3,2,1,0:T(1,128)S(1)}, s32[2,1,1,56]{3,2,1,0:T(1,128)}, u32[]{:S(2)}) copy-start(s32[2,1,1,56]{3,2,1,0:T(1,128)} %param.9) | copy-start | bytes 1348
  1.7 6.0 %copy-start.4 = (f32[1024]{0:T(1024)S(1)}, f32[1024]{0:T(1024)}, u32[]{:S(2)}) copy-start(f32[1024]{0:T(1024)} %param.7) | copy-start | bytes 12292
  1.7 6.2 %copy-start.2 = (s32[2,8]{1,0:T(2,128)S(1)}, s32[2,8]{1,0:T(2,128)}, u32[]{:S(2)}) copy-start(s32[2,8]{1,0:T(2,128)} %refs_1_.7) | copy-start | bytes 196
  1.7 6.4 %copy-start.3 = (f32[8]{0:T(128)S(1)}, f32[8]{0:T(128)}, u32[]{:S(2)}) copy-start(f32[8]{0:T(128)} %param.6) | copy-start | bytes 100
  2.3 13.2 %collective-permute-start.3 = (bf16[32,1536]{1,0:T(8,128)(2,1)S(1)}, bf16[32,1536]{1,0:T(8,128)(2,1)S(1)}, u32[]{:S(2)}, u32[]{:S(2)}) collective-permute-start(bf16[32,1536]{1,0:T(8,128)(2,1)S(1)} %slice.107), channel_id=1, source_target_pairs={{0,8},{4,12},{8,0},{12,4},{16,24},{20,28},{24,16},{28,20},{1,9},{5... | collective-permute-start | bytes 294920 | tf_op jit(solution)/shard_map/ppermute | solution.py:22
  5.0 10.7 %collective-permute-start.4 = (bf16[32,1536]{1,0:T(8,128)(2,1)S(1)}, bf16[32,1536]{1,0:T(8,128)(2,1)S(1)}, u32[]{:S(2)}, u32[]{:S(2)}) collective-permute-start(bf16[32,1536]{1,0:T(8,128)(2,1)S(1)} %get-tuple-element.34), channel_id=1, source_target_pairs={{0,16},{4,20},{8,24},{12,28},{16,0},{20,4},{24,8},{28,12},{1,17},{... | collective-permute-start | bytes 294920 | tf_op jit(solution)/shard_map/ppermute | solution.py:22
  7.6 8.2 %collective-permute-start.5 = (bf16[32,1536]{1,0:T(8,128)(2,1)S(1)}, bf16[32,1536]{1,0:T(8,128)(2,1)S(1)}, u32[]{:S(2)}, u32[]{:S(2)}) collective-permute-start(bf16[32,1536]{1,0:T(8,128)(2,1)S(1)} %get-tuple-element.35), channel_id=1, source_target_pairs={{0,24},{4,28},{8,16},{12,20},{16,8},{20,12},{24,0},{28,4},{1,25},{... | collective-permute-start | bytes 294920 | tf_op jit(solution)/shard_map/ppermute | solution.py:22
  7.6 5.8 %collective-permute-start = (s32[2,56]{1,0:T(2,128)S(1)}, s32[2,56]{1,0:T(2,128)S(1)}, u32[]{:S(2)}, u32[]{:S(2)}) collective-permute-start(s32[2,56]{1,0:T(2,128)S(1)} %bitcast.55), channel_id=1, source_target_pairs={{0,1},{1,0},{2,3},{3,2},{4,5},{5,4},{6,7},{7,6},{8,9},{9,8},{10,11... | collective-permute-start | bytes 1352 | tf_op jit(solution)/shard_map/ppermute | solution.py:22
  13.8 21.7 %collective-permute-start.2 = (bf16[128,1536]{1,0:T(8,128)(2,1)S(1)}, bf16[128,1536]{1,0:T(8,128)(2,1)S(1)}, u32[]{:S(2)}, u32[]{:S(2)}) collective-permute-start(bf16[128,1536]{1,0:T(8,128)(2,1)S(1)} %get-tuple-element.32.refs_3_.refs_2_), channel_id=1, source_target_pairs={{0,4},{4,0},{8,12},{12,8},{16,20},{20,16},{24,28},{28,24},{1,5},{5... | collective-permute-start | bytes 1179656 | tf_op jit(solution)/shard_map/ppermute | solution.py:22
  15.7 6.1 %copy-start.1 = (bf16[1,256,1536]{2,1,0:T(8,128)(2,1)S(1)}, bf16[1,256,1536]{2,1,0:T(8,128)(2,1)}, u32[]{:S(2)}) copy-start(bf16[1,256,1536]{2,1,0:T(8,128)(2,1)} %param.5) | copy-start | bytes 2359300
  15.8 15.9 %collective-permute-start.11 = (bf16[96,1536]{1,0:T(8,128)(2,1)S(1)}, bf16[96,1536]{1,0:T(8,128)(2,1)S(1)}, u32[]{:S(2)}, u32[]{:S(2)}) collective-permute-start(bf16[96,1536]{1,0:T(8,128)(2,1)S(1)} %stack0.1.refs_8_), channel_id=1, source_target_pairs={{0,4},{4,0},{8,12},{12,8},{16,20},{20,16},{24,28},{28,24},{1,5},{5... | collective-permute-start | bytes 884744 | tf_op jit(solution)/shard_map/ppermute | solution.py:22
  17.3 18.9 %collective-permute-start.10 = (bf16[32,1536]{1,0:T(8,128)(2,1)S(1)}, bf16[32,1536]{1,0:T(8,128)(2,1)S(1)}, u32[]{:S(2)}, u32[]{:S(2)}) collective-permute-start(bf16[32,1536]{1,0:T(8,128)(2,1)S(1)} %get-tuple-element.42), channel_id=1, source_target_pairs={{0,24},{4,28},{8,16},{12,20},{16,8},{20,12},{24,0},{28,4},{1,25},{... | collective-permute-start | bytes 294920 | tf_op jit(solution)/shard_map/ppermute | solution.py:22
  19.9 17.0 %collective-permute-start.9 = (bf16[32,1536]{1,0:T(8,128)(2,1)S(1)}, bf16[32,1536]{1,0:T(8,128)(2,1)S(1)}, u32[]{:S(2)}, u32[]{:S(2)}) collective-permute-start(bf16[32,1536]{1,0:T(8,128)(2,1)S(1)} %get-tuple-element.41), channel_id=1, source_target_pairs={{0,16},{4,20},{8,24},{12,28},{16,0},{20,4},{24,8},{28,12},{1,17},{... | collective-permute-start | bytes 294920 | tf_op jit(solution)/shard_map/ppermute | solution.py:22
  20.8 16.1 %collective-permute-start.6 = (bf16[96,1536]{1,0:T(8,128)(2,1)S(1)}, bf16[96,1536]{1,0:T(8,128)(2,1)S(1)}, u32[]{:S(2)}, u32[]{:S(2)}) collective-permute-start(bf16[96,1536]{1,0:T(8,128)(2,1)S(1)} %slice.106), channel_id=1, source_target_pairs={{0,8},{4,12},{8,0},{12,4},{16,24},{20,28},{24,16},{28,20},{1,9},{5... | collective-permute-start | bytes 884744 | tf_op jit(solution)/shard_map/ppermute | solution.py:22
  31.7 20.3 %collective-permute-start.8 = (bf16[32,1536]{1,0:T(8,128)(2,1)S(1)}, bf16[32,1536]{1,0:T(8,128)(2,1)S(1)}, u32[]{:S(2)}, u32[]{:S(2)}) collective-permute-start(bf16[32,1536]{1,0:T(8,128)(2,1)S(1)} %get-tuple-element.40), channel_id=1, source_target_pairs={{0,24},{4,28},{8,16},{12,20},{16,8},{20,12},{24,0},{28,4},{1,25},{... | collective-permute-start | bytes 294920 | tf_op jit(solution)/shard_map/ppermute | solution.py:22
  35.5 16.6 %collective-permute-start.7 = (bf16[32,1536]{1,0:T(8,128)(2,1)S(1)}, bf16[32,1536]{1,0:T(8,128)(2,1)S(1)}, u32[]{:S(2)}, u32[]{:S(2)}) collective-permute-start(bf16[32,1536]{1,0:T(8,128)(2,1)S(1)} %get-tuple-element.38), channel_id=1, source_target_pairs={{0,16},{4,20},{8,24},{12,28},{16,0},{20,4},{24,8},{28,12},{1,17},{... | collective-permute-start | bytes 294920 | tf_op jit(solution)/shard_map/ppermute | solution.py:22
  36.3 10.6 %collective-permute-start.13 = (bf16[64,1536]{1,0:T(8,128)(2,1)S(1)}, bf16[64,1536]{1,0:T(8,128)(2,1)S(1)}, u32[]{:S(2)}, u32[]{:S(2)}) collective-permute-start(bf16[64,1536]{1,0:T(8,128)(2,1)S(1)} %get-tuple-element.44), channel_id=1, source_target_pairs={{0,8},{4,12},{8,0},{12,4},{16,24},{20,28},{24,16},{28,20},{1,9},{5... | collective-permute-start | bytes 589832 | tf_op jit(solution)/shard_map/ppermute | solution.py:22
  36.9 12.7 %collective-permute-start.12 = (bf16[96,1536]{1,0:T(8,128)(2,1)S(1)}, bf16[96,1536]{1,0:T(8,128)(2,1)S(1)}, u32[]{:S(2)}, u32[]{:S(2)}) collective-permute-start(bf16[96,1536]{1,0:T(8,128)(2,1)S(1)} %stack1.1.refs_2_), channel_id=1, source_target_pairs={{0,4},{4,0},{8,12},{12,8},{16,20},{20,16},{24,28},{28,24},{1,5},{5... | collective-permute-start | bytes 884744 | tf_op jit(solution)/shard_map/ppermute | solution.py:22
  38.7 23.4 %collective-permute-start.18 = (bf16[32,1536]{1,0:T(8,128)(2,1)S(1)}, bf16[32,1536]{1,0:T(8,128)(2,1)S(1)}, u32[]{:S(2)}, u32[]{:S(2)}) collective-permute-start(bf16[32,1536]{1,0:T(8,128)(2,1)S(1)} %get-tuple-element.50), channel_id=1, source_target_pairs={{0,16},{4,20},{8,24},{12,28},{16,0},{20,4},{24,8},{28,12},{1,17},{... | collective-permute-start | bytes 294920 | tf_op jit(solution)/shard_map/ppermute | solution.py:22
  46.9 15.2 %collective-permute-start.19 = (bf16[32,1536]{1,0:T(8,128)(2,1)S(1)}, bf16[32,1536]{1,0:T(8,128)(2,1)S(1)}, u32[]{:S(2)}, u32[]{:S(2)}) collective-permute-start(bf16[32,1536]{1,0:T(8,128)(2,1)S(1)} %get-tuple-element.52), channel_id=1, source_target_pairs={{0,24},{4,28},{8,16},{12,20},{16,8},{20,12},{24,0},{28,4},{1,25},{... | collective-permute-start | bytes 294920 | tf_op jit(solution)/shard_map/ppermute | solution.py:22
  49.7 10.8 %collective-permute-start.16 = (bf16[128,1536]{1,0:T(8,128)(2,1)S(1)}, bf16[128,1536]{1,0:T(8,128)(2,1)S(1)}, u32[]{:S(2)}, u32[]{:S(2)}) collective-permute-start(bf16[128,1536]{1,0:T(8,128)(2,1)S(1)} %join0.1.refs_8_.refs_9_.refs_5_), channel_id=1, source_target_pairs={{0,2},{1,3},{2,0},{3,1},{4,6},{5,7},{6,4},{7,5},{8,10},{9,11},{10,... | collective-permute-start | bytes 1179656 | tf_op jit(solution)/shard_map/ppermute | solution.py:22
  52.0 5.8 %collective-permute-start.15 = (bf16[64,1536]{1,0:T(8,128)(2,1)S(1)}, bf16[64,1536]{1,0:T(8,128)(2,1)S(1)}, u32[]{:S(2)}, u32[]{:S(2)}) collective-permute-start(bf16[64,1536]{1,0:T(8,128)(2,1)S(1)} %get-tuple-element.46), channel_id=1, source_target_pairs={{0,8},{4,12},{8,0},{12,4},{16,24},{20,28},{24,16},{28,20},{1,9},{5... | collective-permute-start | bytes 589832 | tf_op jit(solution)/shard_map/ppermute | solution.py:22
  52.1 7.5 %collective-permute-start.14 = (bf16[96,1536]{1,0:T(8,128)(2,1)S(1)}, bf16[96,1536]{1,0:T(8,128)(2,1)S(1)}, u32[]{:S(2)}, u32[]{:S(2)}) collective-permute-start(bf16[96,1536]{1,0:T(8,128)(2,1)S(1)} %stack2.1.refs_2_), channel_id=1, source_target_pairs={{0,4},{4,0},{8,12},{12,8},{16,20},{20,16},{24,28},{28,24},{1,5},{5... | collective-permute-start | bytes 884744 | tf_op jit(solution)/shard_map/ppermute | solution.py:22
  57.8 12.1 %collective-permute-start.24 = (bf16[128,1536]{1,0:T(8,128)(2,1)S(1)}, bf16[128,1536]{1,0:T(8,128)(2,1)S(1)}, u32[]{:S(2)}, u32[]{:S(2)}) collective-permute-start(bf16[128,1536]{1,0:T(8,128)(2,1)S(1)} %join1.1.refs_8_.refs_9_.refs_7_), channel_id=1, source_target_pairs={{0,2},{1,3},{2,0},{3,1},{4,6},{5,7},{6,4},{7,5},{8,10},{9,11},{10,... | collective-permute-start | bytes 1179656 | tf_op jit(solution)/shard_map/ppermute | solution.py:22
  61.2 5.7 %collective-permute-start.17 = (bf16[64,1536]{1,0:T(8,128)(2,1)S(1)}, bf16[64,1536]{1,0:T(8,128)(2,1)S(1)}, u32[]{:S(2)}, u32[]{:S(2)}) collective-permute-start(bf16[64,1536]{1,0:T(8,128)(2,1)S(1)} %get-tuple-element.48), channel_id=1, source_target_pairs={{0,8},{4,12},{8,0},{12,4},{16,24},{20,28},{24,16},{28,20},{1,9},{5... | collective-permute-start | bytes 589832 | tf_op jit(solution)/shard_map/ppermute | solution.py:22
  62.1 6.8 %collective-permute-start.23 = (bf16[96,1536]{1,0:T(8,128)(2,1)S(1)}, bf16[96,1536]{1,0:T(8,128)(2,1)S(1)}, u32[]{:S(2)}, u32[]{:S(2)}) collective-permute-start(bf16[96,1536]{1,0:T(8,128)(2,1)S(1)} %stack3.1.refs_2_), channel_id=1, source_target_pairs={{0,4},{4,0},{8,12},{12,8},{16,20},{20,16},{24,28},{28,24},{1,5},{5... | collective-permute-start | bytes 884744 | tf_op jit(solution)/shard_map/ppermute | solution.py:22
  67.0 11.2 %collective-permute-start.20 = (bf16[128,1536]{1,0:T(8,128)(2,1)S(1)}, bf16[128,1536]{1,0:T(8,128)(2,1)S(1)}, u32[]{:S(2)}, u32[]{:S(2)}) collective-permute-start(bf16[128,1536]{1,0:T(8,128)(2,1)S(1)} %join2.1.refs_8_.refs_5_), channel_id=1, source_target_pairs={{0,2},{1,3},{2,0},{3,1},{4,6},{5,7},{6,4},{7,5},{8,10},{9,11},{10,... | collective-permute-start | bytes 1179656 | tf_op jit(solution)/shard_map/ppermute | solution.py:22
  70.7 5.7 %collective-permute-start.25 = (bf16[64,1536]{1,0:T(8,128)(2,1)S(1)}, bf16[64,1536]{1,0:T(8,128)(2,1)S(1)}, u32[]{:S(2)}, u32[]{:S(2)}) collective-permute-start(bf16[64,1536]{1,0:T(8,128)(2,1)S(1)} %get-tuple-element.54), channel_id=1, source_target_pairs={{0,8},{4,12},{8,0},{12,4},{16,24},{20,28},{24,16},{28,20},{1,9},{5... | collective-permute-start | bytes 589832 | tf_op jit(solution)/shard_map/ppermute | solution.py:22
  72.9 13.6 %collective-permute-start.29 = (f32[256,1536]{1,0:T(8,128)S(1)}, f32[256,1536]{1,0:T(8,128)S(1)}, u32[]{:S(2)}, u32[]{:S(2)}) collective-permute-start(f32[256,1536]{1,0:T(8,128)S(1)} %get-tuple-element.56), channel_id=1, source_target_pairs={{0,1},{1,0},{2,3},{3,2},{4,5},{5,4},{6,7},{7,6},{8,9},{9,8},{10,11... | collective-permute-start | bytes 4718600 | tf_op jit(solution)/shard_map/ppermute | solution.py:22
  76.4 8.3 %collective-permute-start.26 = (bf16[128,1536]{1,0:T(8,128)(2,1)S(1)}, bf16[128,1536]{1,0:T(8,128)(2,1)S(1)}, u32[]{:S(2)}, u32[]{:S(2)}) collective-permute-start(bf16[128,1536]{1,0:T(8,128)(2,1)S(1)} %join3.1.refs_9_.refs_15_), channel_id=1, source_target_pairs={{0,2},{1,3},{2,0},{3,1},{4,6},{5,7},{6,4},{7,5},{8,10},{9,11},{10,... | collective-permute-start | bytes 1179656 | tf_op jit(solution)/shard_map/ppermute | solution.py:22
  77.6 7.1 %collective-permute-start.21 = (bf16[128,1536]{1,0:T(8,128)(2,1)S(1)}, bf16[128,1536]{1,0:T(8,128)(2,1)S(1)}, u32[]{:S(2)}, u32[]{:S(2)}) collective-permute-start(bf16[128,1536]{1,0:T(8,128)(2,1)S(1)} %join2.1.refs_8_.refs_5_), channel_id=1, source_target_pairs={{0,1},{1,0},{2,3},{3,2},{4,5},{5,4},{6,7},{7,6},{8,9},{9,8},{10,11... | collective-permute-start | bytes 1179656 | tf_op jit(solution)/shard_map/ppermute | solution.py:22
  77.7 7.1 %collective-permute-start.27 = (bf16[128,1536]{1,0:T(8,128)(2,1)S(1)}, bf16[128,1536]{1,0:T(8,128)(2,1)S(1)}, u32[]{:S(2)}, u32[]{:S(2)}) collective-permute-start(bf16[128,1536]{1,0:T(8,128)(2,1)S(1)} %join3.1.refs_9_.refs_15_), channel_id=1, source_target_pairs={{0,1},{1,0},{2,3},{3,2},{4,5},{5,4},{6,7},{7,6},{8,9},{9,8},{10,11... | collective-permute-start | bytes 1179656 | tf_op jit(solution)/shard_map/ppermute | solution.py:22
  78.2 6.6 %collective-permute-start.22 = (bf16[128,1536]{1,0:T(8,128)(2,1)S(1)}, bf16[128,1536]{1,0:T(8,128)(2,1)S(1)}, u32[]{:S(2)}, u32[]{:S(2)}) collective-permute-start(bf16[128,1536]{1,0:T(8,128)(2,1)S(1)} %collective-permute-done.20.refs_6_), channel_id=1, source_target_pairs={{0,1},{1,0},{2,3},{3,2},{4,5},{5,4},{6,7},{7,6},{8,9},{9,8},{10,11... | collective-permute-start | bytes 1179656 | tf_op jit(solution)/shard_map/ppermute | solution.py:22
  84.8 1.7 %collective-permute-start.28 = (bf16[128,1536]{1,0:T(8,128)(2,1)S(1)}, bf16[128,1536]{1,0:T(8,128)(2,1)S(1)}, u32[]{:S(2)}, u32[]{:S(2)}) collective-permute-start(bf16[128,1536]{1,0:T(8,128)(2,1)S(1)} %collective-permute-done.26.refs_10_), channel_id=1, source_target_pairs={{0,1},{1,0},{2,3},{3,2},{4,5},{5,4},{6,7},{7,6},{8,9},{9,8},{10,11... | collective-permute-start | bytes 1179656 | tf_op jit(solution)/shard_map/ppermute | solution.py:22

commit v3 on v2

--- a/solution.py
+++ b/solution.py
@@ -7,12 +7,18 @@
 
 TILE = 64
 SHARES = (2, 2, 2, 2)
-PACE = 2
-FL, BY = 10**10, 1
-NEAR_FIRST = 1
+FGROUPS = ((0,), (1,), (2,), (3,))
+FGATE = {2: "c0", 3: "s2"}
+FNEED = {2: "c1", 3: "c2"}
+NEAR_FIRST, NGATE = 2, "s1"
+BSTART, BNEED = "s0", "j0"
+XNEED = "j1"
+SETNEED = "s1"
+EARLY = 1
 TAIL = 2
-XWAIT = 2
-GATE = 0
+ORDER = "s"
+FL, FK, BY = 10**10, 1, 1
+WS, WJ, WC = 10**10, 10**10, 10**10
 VMEM = pl.BlockSpec(memory_space=pltpu.VMEM)
 SMEM = pl.BlockSpec(memory_space=pltpu.SMEM)
 ANY = pl.BlockSpec(memory_space=pl.ANY)
@@ -41,7 +47,7 @@
     def __init__(self):
         self.last = []
 
-    def call(self, kernel, smem, arrays, outs, name, waits=()):
+    def call(self, kernel, smem, arrays, outs, name, waits=(), weight=None):
         waits = [*self.last, *waits]
         count = len(smem) + len(arrays)
 
@@ -54,7 +60,7 @@
             in_specs=[SMEM] * len(smem) + [VMEM] * len(arrays) + [ANY] * len(waits),
             out_specs=(VMEM,) * len(outs),
             compiler_params=pltpu.CompilerParams(vmem_limit_bytes=40 * 1024 * 1024),
-            cost_estimate=pl.CostEstimate(flops=FL, bytes_accessed=BY, transcendentals=0),
+            cost_estimate=pl.CostEstimate(flops=weight or FL, bytes_accessed=BY, transcendentals=0),
             name=name,
         )(*smem, *arrays, *waits)
         self.last = [result[0]]
@@ -106,6 +112,8 @@
     count = len(shares)
     edges = [piece * sum(shares[:c]) // sum(shares) for c in range(count + 1)]
     spans = list(zip(edges[:-1], edges[1:]))
+    far_groups = FGROUPS if count == sum(map(len, FGROUPS)) else [(c,) for c in range(count)]
+    far_spans = [(edges[g[0]], edges[g[-1] + 1]) for g in far_groups]
     x_order = [m for m in range(virt_count) if not m & 1]
 
     def block(n):
@@ -120,10 +128,10 @@
             at = pl.multiple_of((ids_ref[1] ^ m) * piece, piece)
             data = own_ref[pl.ds(at, piece), :]
             out_refs[m][...] = data
-            for c, (lo, hi) in enumerate(spans):
+            for c, (lo, hi) in enumerate(far_spans):
                 out_refs[places + c * places + m][...] = data[lo:hi]
 
-    cuts = chain.call(cut, [ids], [own], [block(piece)] * places + [block(hi - lo) for lo, hi in spans for _ in range(places)], "cut")
+    cuts = chain.call(cut, [ids], [own], [block(piece)] * places + [block(hi - lo) for lo, hi in far_spans for _ in range(places)], "cut")
     turned = cuts[:places]
 
     def start_far(c, *deps):
@@ -133,20 +141,19 @@
 
     lists = tile_lists[:, 0, 0]
     lists_beside = send(lists, "virt", 1)
-    beside = send(own, "virt", 1) if count > TAIL else None
     far = {0: start_far(0)}
-    near = []
-    for m in range(1, places):
-        split = edges[NEAR_FIRST] if count > 1 else piece
-        first = send(turned[m][:split], "occ", m * unit)
-        near.append([(0, first)])
     own_side = {}
     for mask in column_masks:
         for m in [0, *own_side]:
-            mine = own_side[m] if m else after(turned[0], *([lists_beside, beside] if count > TAIL else []))
-            own_side[m ^ mask] = send(mine, "occ", mask)
-    for c in range(1, min(PACE, count)):
-        far[c] = start_far(c)
+            own_side[m ^ mask] = send(own_side[m] if m else turned[0], "occ", mask)
+    near = []
+    for m in range(1, places):
+        split = edges[min(NEAR_FIRST, count)]
+        first = send(turned[m][:split], "occ", m * unit)
+        near.append([(0, first)])
+    for c in range(1, len(far_groups)):
+        if c not in FGATE:
+            far[c] = start_far(c)
 
     partner_energy = jnp.take(occupied_energy, jnp.take(partner_list, myself, axis=1), axis=0)
     own_energy = lax.dynamic_index_in_dim(occupied_energy, myself, 0, False)
@@ -173,8 +180,9 @@
     early = list(range(count - TAIL))
     late = list(range(max(count - TAIL, 0), count))
     full_order = x_order + [m ^ 1 for m in x_order]
-    set_last = (gap_left[:slice_rows], table[:slice_rows], column(right, full_order, late), column(key, full_order, late))
-    set_early = (gap_left, table, column(right, x_order, early), column(key, x_order, early)) if early else ()
+    sets = {c: (gap_left[:slice_rows], table[:slice_rows], column(right, full_order, [c]), column(key, full_order, [c])) for c in late}
+    if early:
+        sets[0] = (gap_left, table, column(right, x_order, early), column(key, x_order, early))
 
     def add_part(left, sides, row_refs, added, outs, name, waits=()):
         arrays = [left, *sides, *row_refs, *added]
@@ -183,41 +191,54 @@
             part_kernel(*refs, row_count=len(row_refs), added=len(added))
 
         shapes = [jax.ShapeDtypeStruct((n, aux), jnp.float32) for n in outs]
-        return chain.call(kernel, [], arrays, shapes, name, waits)
+        return chain.call(kernel, [], arrays, shapes, name, waits, FK)
 
     far_masks = [half ^ (m * unit) for m in range(places)]
     near_masks = [m * unit for m in range(1, places)]
     group = near_masks + far_masks
-    side, got, local, value, wide = {}, {}, {}, {}, {}
+    masks, side, got, local, value, wide = {}, {}, {}, {}, {}, {}
+
+    def needed(kind, t):
+        label = f"{kind}{t}"
+        found = []
+        for g, at in FNEED.items():
+            if at == label and g in far:
+                found += far[g]
+        if BNEED == label and beside is not None:
+            found.append(beside)
+        if kind == XNEED[0] and t - int(XNEED[1]) in wide:
+            found += wide[t - int(XNEED[1])]
+        if SETNEED == label:
+            found += [v for sides in sets.values() for v in sides]
+        return found
 
     def near_of(t, m):
         at, value = [(at, v) for at, v in near[m] if at <= spans[t][0]][-1]
         return value, spans[t][0] - at
 
+    def far_of(t):
+        g = [i for i, chunks in enumerate(far_groups) if t in chunks][0]
+        return [(v, spans[t][0] - far_spans[g][0]) for v in far[g]]
+
     def stack_side(t):
         lo, hi = spans[t]
         rows = hi - lo
-        nears = [near_of(t, m) for m in range(places - 1)]
-
+        parts = [near_of(t, m) for m in range(places - 1)] + far_of(t)
+        masks[t] = list(group)
         def kernel(*refs):
             *in_refs, out_ref = refs
             for i, ref in enumerate(in_refs):
-                at = nears[i][1] if i < len(nears) else 0
+                at = parts[i][1]
                 out_ref[i * rows : (i + 1) * rows, :] = ref[at : at + rows, :]
 
-        waits = [*set_last, *set_early] if t == 0 else []
-        arrays = [v for v, _ in nears] + far[t]
-        out = chain.call(kernel, [], arrays, [block(len(group) * rows)], f"stack{t}", waits)[0]
-        if t == 0 and count > 1:
-            for m in range(1, places):
-                split = edges[NEAR_FIRST]
-                near[m - 1].append((split, send(after(turned[m][split:], out), "occ", m * unit)))
+        waits = needed("s", t)
+        arrays = [v for v, _ in parts]
+        out = chain.call(kernel, [], arrays, [block(len(parts) * rows)], f"stack{t}", waits, WS)[0]
         stacked = {0: out}
         for mask in column_masks:
             for m in list(stacked):
                 stacked[m ^ mask] = send(stacked[m], "occ", mask)
         side[t] = {col: v for col, v in stacked.items() if col}
-        return out
 
     def choose(t):
         lo, hi = spans[t]
@@ -225,10 +246,10 @@
         sources = [(0, turned[0], lo)]
         sources += [(m, v, lo) for m, v in own_side.items()]
         sources += [(m, *near_of(t, i)) for i, m in enumerate(near_masks)]
-        sources += [(m, v, 0) for m, v in zip(far_masks, far[t])]
+        sources += [(m, *v) for m, v in zip(far_masks, far_of(t))]
         arrays = [v for _, v, _ in sources]
         for col, v in side[t].items():
-            sources += [(m ^ col, len(arrays), i * rows) for i, m in enumerate(group)]
+            sources += [(m ^ col, len(arrays), i * rows) for i, m in enumerate(masks[t])]
             arrays.append(v)
 
         def kernel(ids_ref, partner_ref, *refs):
@@ -243,14 +264,15 @@
                         def _(ref=ref, at=at, k=k, m=m):
                             out_refs[m][k * rows : (k + 1) * rows, :] = ref[at : at + rows, :]
 
-        waits = wide[t - XWAIT] if t >= XWAIT else []
-        outs = chain.call(kernel, [ids, partner_list], arrays, [block(pairings * rows)] * places, f"choose{t}", waits)
+        waits = needed("c", t)
+        outs = chain.call(kernel, [ids, partner_list], arrays, [block(pairings * rows)] * places, f"choose{t}", waits, WC)
         local[t] = outs[0]
         got[t] = [send(outs[m], "occ", m * unit) for m in range(1, places)]
         return outs[0]
 
     def join(t, waits=()):
         rows = spans[t][1] - spans[t][0]
+        waits = needed("j", t)
 
         def kernel(*refs):
             *in_refs, out_ref = refs
@@ -260,7 +282,7 @@
                     out_ref[at : at + rows, :] = ref[k * rows : (k + 1) * rows, :]
 
         value[t] = chain.call(
-            kernel, [], [local[t], *got[t]], [block(pairings * places * rows)], f"join{t}", waits
+            kernel, [], [local[t], *got[t]], [block(pairings * places * rows)], f"join{t}", waits, WJ
         )[0]
         ready = {0: value[t]}
         mask = virt_count // 2
@@ -271,26 +293,48 @@
         wide[t] = [ready[m] for m in x_order]
 
     added = []
-    for t in range(count):
-        stack_side(t)
-        if GATE == 0 and t + PACE < count:
-            far[t + PACE] = start_far(t + PACE, *chain.last)
-        if t:
-            join(t - 1)
-        if GATE == 1 and t + PACE < count:
-            far[t + PACE] = start_far(t + PACE, *chain.last)
-        choose(t)
-        if GATE == 2 and t + PACE < count:
-            far[t + PACE] = start_far(t + PACE, *chain.last)
-    if early:
+    def add_early():
         lefts = jnp.concatenate([own, beside], axis=0)
         mine, other = add_part(
-            lefts, set_early, [v for c in early for v in wide[c]], [], [slice_rows] * 2, "early"
+            lefts, sets[0], [v for c in early for v in wide[c]], [], [slice_rows] * 2, "early"
         )
-        added = [mine, send(other, "virt", 1)]
+        return [mine, send(other, "virt", 1)]
+
+    def full(c):
+        return wide[c] + [send(w, "virt", 1) for w in wide[c]]
+
+    def gate(kind, t):
+        nonlocal beside
+        if BSTART == f"{kind}{t}" and early:
+            beside = send(after(own, *chain.last), "virt", 1)
+        if NGATE == f"{kind}{t}" and NEAR_FIRST < count:
+            split = edges[NEAR_FIRST]
+            for m in range(1, places):
+                near[m - 1].append((split, send(after(turned[m][split:], *chain.last), "occ", m * unit)))
+        for g, at in FGATE.items():
+            if at == f"{kind}{t}" and g < len(far_groups):
+                far[g] = start_far(g, *chain.last)
+
+    beside = None
+    for t in range(count):
+        steps = [("s", t)] + [("j", t - 1)] * (t > 0)
+        if ORDER[t % len(ORDER)] == "j":
+            steps = steps[::-1]
+        for kind, c in steps:
+            (stack_side if kind == "s" else join)(c)
+            gate(kind, c)
+        if t == count - 1 and EARLY == 0 and early:
+            added = add_early()
+        choose(t)
+        gate("c", t)
+    if early and EARLY == 1:
+        added = add_early()
     join(count - 1)
-    final = [v for c in late for v in wide[c] + [send(w, "virt", 1) for w in wide[c]]]
-    return add_part(own, set_last, final, added, [slice_rows], "last")[0][None]
+    if early and EARLY == 2:
+        added = add_early()
+    for c in late:
+        added = add_part(own, sets[c], full(c), added, [slice_rows], f"late{c}")
+    return added[0][None]
 
 
 def solution(mesh):

time: 89.8 us -> 83.6 us (0.931)
  waiting for transfers between devices: 37.7 us -> 32.2 us
  starting transfers between devices: 35.3 us -> 31.3 us
  Pallas kernels: 8.92 us -> 10.6 us
  local copies, waits for them, and re-layouts: 5.59 us -> 7.15 us
    ppermute x30, waiting for transfers between devices: 37.7 us -> 32.2 us  [send(): lax.ppermute(value, axis, [(i, i ^ mask) for i in range(lax.axis_size(axi...]
    ppermute x30, starting transfers between devices: 35.3 us -> 31.3 us  [send(): lax.ppermute(value, axis, [(i, i ^ mask) for i in range(lax.axis_size(axi...]
    pallas_call x15 -> x16, Pallas kernels: 8.92 us -> 10.6 us  [call(): pl.pallas_call(run, out_shape=tuple(outs), in_specs=[SMEM] * len(smem) +...]
    unnamed x34 -> x38, local copies, waits for them, and re-layouts: 1.46 us -> 2.34 us
  transfers between devices with their start and end apart: 30 -> 30, of which waited for: 12 -> 13; matrix products, arithmetic and copies ran while one was open for 7% -> 7% of each run, Pallas kernels for 6% -> 9%
where the time goes in v3:
time: 83.6 us; the launch traced here: 83.3 us
  waiting for transfers between devices  32.2 us (39%)
  starting transfers between devices  31.3 us (37%)
  Pallas kernels  10.6 us (13%)
  local copies, waits for them, and re-layouts  7.15 us (9%)
  other arithmetic  1.6 us (2%)
    ppermute x30, waiting for transfers between devices, send(): lax.ppermute(value, axis, [(i, i ^ mask) for i in range(lax.axis_size(axi...  32.2 us
    ppermute x30, starting transfers between devices, send(): lax.ppermute(value, axis, [(i, i ^ mask) for i in range(lax.axis_size(axi...  31.3 us
    pallas_call x16, Pallas kernels, call(): pl.pallas_call(run, out_shape=tuple(outs), in_specs=[SMEM] * len(smem) +...  10.6 us
    unnamed x38, local copies, waits for them, and re-layouts  2.34 us
    another operation x24, local copies, waits for them, and re-layouts, column(): x[m, :, :, slice(*spans[c])].reshape(1, -1)  1.98 us
  transfers between devices with their start and end apart: 30, of which 13 were waited for; matrix products, arithmetic and copies ran while one was open for 7% of the time, Pallas kernels for 9%

profile of v3, /device:TPU:0, one launch (start us, length us, event | category | flops | bytes accessed | tf_op | source)
XLA Modules:
  0.0 83.3 jit_solution(10904538810122873421)
XLA Ops:
  0.1 1.1 %copy-done = bf16[1,256,1536]{2,1,0:T(8,128)(2,1)S(1)} copy-done((bf16[1,256,1536]{2,1,0:T(8,128)(2,1)S(1)}, bf16[1,256,1536]{2,1,0:T(8,128)(2,1)}, u32[]{:S(2)}) %copy-start) | copy-done | bytes 786456
  1.2 0.7 cut.1
  1.9 0.7 fusion.6
  2.6 3.0 %collective-permute-start.1 = (bf16[64,1536]{1,0:T(8,128)(2,1)S(1)}, bf16[64,1536]{1,0:T(8,128)(2,1)S(1)}, u32[]{:S(2)}, u32[]{:S(2)}) collective-permute-start(bf16[64,1536]{1,0:T(8,128)(2,1)S(1)} %get-tuple-element.70), channel_id=1, source_target_pairs={{0,8},{4,12},{8,0},{12,4},{16,24},{20,28},{24,16},{28,20},{1,9},{5... | collective-permute-start | bytes 589832 | tf_op jit(solution)/shard_map/ppermute | solution.py:28
  5.6 2.6 %collective-permute-start.4 = (bf16[32,1536]{1,0:T(8,128)(2,1)S(1)}, bf16[32,1536]{1,0:T(8,128)(2,1)S(1)}, u32[]{:S(2)}, u32[]{:S(2)}) collective-permute-start(bf16[32,1536]{1,0:T(8,128)(2,1)S(1)} %get-tuple-element.35), channel_id=1, source_target_pairs={{0,16},{4,20},{8,24},{12,28},{16,0},{20,4},{24,8},{28,12},{1,17},{... | collective-permute-start | bytes 294920 | tf_op jit(solution)/shard_map/ppermute | solution.py:28
  8.2 1.7 %collective-permute-start = (bf16[128,1536]{1,0:T(8,128)(2,1)S(1)}, bf16[128,1536]{1,0:T(8,128)(2,1)S(1)}, u32[]{:S(2)}, u32[]{:S(2)}) collective-permute-start(bf16[128,1536]{1,0:T(8,128)(2,1)S(1)} %get-tuple-element.31.refs_3_.refs_2_), channel_id=1, source_target_pairs={{0,4},{4,0},{8,12},{12,8},{16,20},{20,16},{24,28},{28,24},{1,5},{5... | collective-permute-start | bytes 1179656 | tf_op jit(solution)/shard_map/ppermute | solution.py:28
  10.4 0.6 dynamic_slice.4
  11.0 0.6 gather_fusion
  14.3 0.6 fusion.3
  15.3 1.8 %collective-permute-start.2 = (bf16[32,1536]{1,0:T(8,128)(2,1)S(1)}, bf16[32,1536]{1,0:T(8,128)(2,1)}, u32[]{:S(2)}, u32[]{:S(2)}) collective-permute-start(bf16[32,1536]{1,0:T(8,128)(2,1)S(1)} %get-tuple-element.33), channel_id=1, source_target_pairs={{0,16},{4,20},{8,24},{12,28},{16,0},{20,4},{24,8},{28,12},{1,17},{... | collective-permute-start | bytes 294920 | tf_op jit(solution)/shard_map/ppermute | solution.py:28
  17.1 2.0 %collective-permute-start.3 = (bf16[32,1536]{1,0:T(8,128)(2,1)S(1)}, bf16[32,1536]{1,0:T(8,128)(2,1)}, u32[]{:S(2)}, u32[]{:S(2)}) collective-permute-start(bf16[32,1536]{1,0:T(8,128)(2,1)S(1)} %get-tuple-element.34), channel_id=1, source_target_pairs={{0,24},{4,28},{8,16},{12,20},{16,8},{20,12},{24,0},{28,4},{1,25},{... | collective-permute-start | bytes 294920 | tf_op jit(solution)/shard_map/ppermute | solution.py:28
  19.1 1.4 %collective-permute-start.6 = (bf16[96,1536]{1,0:T(8,128)(2,1)S(1)}, bf16[96,1536]{1,0:T(8,128)(2,1)S(1)}, u32[]{:S(2)}, u32[]{:S(2)}) collective-permute-start(bf16[96,1536]{1,0:T(8,128)(2,1)S(1)} %stack0.1.refs_8_), channel_id=1, source_target_pairs={{0,4},{4,0},{8,12},{12,8},{16,20},{20,16},{24,28},{28,24},{1,5},{5... | collective-permute-start | bytes 884744 | tf_op jit(solution)/shard_map/ppermute | solution.py:28
  21.3 7.0 %collective-permute-done.6.refs_7_ = bf16[96,1536]{1,0:T(8,128)(2,1)S(1)} collective-permute-done((bf16[96,1536]{1,0:T(8,128)(2,1)S(1)}, bf16[96,1536]{1,0:T(8,128)(2,1)S(1)}, u32[]{:S(2)}, u32[]{:S(2)}) %collective-permute-start.6) | collective-permute-done | bytes 294944 | tf_op jit(solution)/shard_map/ppermute | solution.py:28
  28.3 0.9 %copy-done.4 = bf16[32,1536]{1,0:T(8,128)(2,1)S(1)} copy-done((bf16[32,1536]{1,0:T(8,128)(2,1)S(1)}, bf16[32,1536]{1,0:T(8,128)(2,1)}, u32[]{:S(2)}) %copy-start.4) | copy-done | bytes 98328
  29.2 0.7 choose0.1
  30.0 1.0 %collective-permute-start.12 = (bf16[64,1536]{1,0:T(8,128)(2,1)S(1)}, bf16[64,1536]{1,0:T(8,128)(2,1)S(1)}, u32[]{:S(2)}, u32[]{:S(2)}) collective-permute-start(bf16[64,1536]{1,0:T(8,128)(2,1)S(1)} %get-tuple-element.44), channel_id=1, source_target_pairs={{0,8},{4,12},{8,0},{12,4},{16,24},{20,28},{24,16},{28,20},{1,9},{5... | collective-permute-start | bytes 589832 | tf_op jit(solution)/shard_map/ppermute | solution.py:28
  31.0 2.1 %collective-permute-start.10 = (bf16[32,1536]{1,0:T(8,128)(2,1)S(1)}, bf16[32,1536]{1,0:T(8,128)(2,1)S(1)}, u32[]{:S(2)}, u32[]{:S(2)}) collective-permute-start(bf16[32,1536]{1,0:T(8,128)(2,1)S(1)} %get-tuple-element.43), channel_id=1, source_target_pairs={{0,24},{4,28},{8,16},{12,20},{16,8},{20,12},{24,0},{28,4},{1,25},{... | collective-permute-start | bytes 294920 | tf_op jit(solution)/shard_map/ppermute | solution.py:28
  33.2 0.4 collective-permute-start.9
  33.5 1.0 %stack1.1.refs_2_ = bf16[96,1536]{1,0:T(8,128)(2,1)S(1)} custom-call(bf16[64,1536]{1,0:T(8,128)(2,1)S(1)} %collective-permute-done.1.refs_0_.refs_4_, bf16[32,1536]{1,0:T(8,128)(2,1)} %collective-permute-done.2.refs_1_.refs_5_, bf16[32,1536]{1,0:T(8,128)(2,1)} %collective-permute-done.3.refs_2_.refs_6_, ...), custom_call_target="tpu_custom_call" | custom-call | flops 10000000000 | bytes 1 | tf_op jit(solution)/shard_map/stack1/pallas_call | solution.py:57
  34.5 0.6 collective-permute-start.11
  35.1 3.4 %collective-permute-done.12.refs_1_ = bf16[64,1536]{1,0:T(8,128)(2,1)S(1)} collective-permute-done((bf16[64,1536]{1,0:T(8,128)(2,1)S(1)}, bf16[64,1536]{1,0:T(8,128)(2,1)S(1)}, u32[]{:S(2)}, u32[]{:S(2)}) %collective-permute-start.12) | collective-permute-done | bytes 196640 | tf_op jit(solution)/shard_map/ppermute | solution.py:28
  38.5 0.3 collective-permute-start.8
  38.9 1.6 %collective-permute-start.18 = (bf16[128,1536]{1,0:T(8,128)(2,1)S(1)}, bf16[128,1536]{1,0:T(8,128)(2,1)S(1)}, u32[]{:S(2)}, u32[]{:S(2)}) collective-permute-start(bf16[128,1536]{1,0:T(8,128)(2,1)S(1)} %join0.1.refs_8_.refs_3_.refs_5_), channel_id=1, source_target_pairs={{0,2},{1,3},{2,0},{3,1},{4,6},{5,7},{6,4},{7,5},{8,10},{9,11},{10,... | collective-permute-start | bytes 1179656 | tf_op jit(solution)/shard_map/ppermute | solution.py:28
  40.5 0.7 collective-permute-done.10.refs_10_.refs_2_.refs_6_
  41.1 0.6 collective-permute-done.9.refs_9_.refs_1_.refs_5_
  41.7 0.4 collective-permute-done.11.refs_7_
  42.1 1.1 %choose1.1 = (bf16[64,1536]{1,0:T(8,128)(2,1)S(1)}, bf16[64,1536]{1,0:T(8,128)(2,1)S(1)}) custom-call(s32[2]{0:T(128)S(1)} %pad_add_fusion.refs_0_, s32[2,8]{1,0:T(2,128)S(1)} %copy-done.2, bf16[128,1536]{1,0:T(8,128)(2,1)S(1)} %get-tuple-element.31.refs_3_.refs_2_, bf16[128,1536]{1,0:T(8,128)(2,1)S(1)} %collective-permute-done.refs_3_, ...), custom_call_target="tpu_custom_call" | custom-call | flops 10000000000 | bytes 1 | tf_op jit(solution)/shard_map/choose1/pallas_call | solution.py:57
  43.2 1.9 %collective-permute-start.17 = (bf16[64,1536]{1,0:T(8,128)(2,1)S(1)}, bf16[64,1536]{1,0:T(8,128)(2,1)S(1)}, u32[]{:S(2)}, u32[]{:S(2)}) collective-permute-start(bf16[64,1536]{1,0:T(8,128)(2,1)S(1)} %get-tuple-element.50), channel_id=1, source_target_pairs={{0,8},{4,12},{8,0},{12,4},{16,24},{20,28},{24,16},{28,20},{1,9},{5... | collective-permute-start | bytes 589832 | tf_op jit(solution)/shard_map/ppermute | solution.py:28
  45.2 0.2 collective-permute-done.8.refs_0_.refs_4_
  45.6 1.9 %collective-permute-start.15 = (bf16[32,1536]{1,0:T(8,128)(2,1)S(1)}, bf16[32,1536]{1,0:T(8,128)(2,1)S(1)}, u32[]{:S(2)}, u32[]{:S(2)}) collective-permute-start(bf16[32,1536]{1,0:T(8,128)(2,1)S(1)} %get-tuple-element.49), channel_id=1, source_target_pairs={{0,24},{4,28},{8,16},{12,20},{16,8},{20,12},{24,0},{28,4},{1,25},{... | collective-permute-start | bytes 294920 | tf_op jit(solution)/shard_map/ppermute | solution.py:28
  47.5 3.1 %collective-permute-done.17.refs_1_ = bf16[64,1536]{1,0:T(8,128)(2,1)S(1)} collective-permute-done((bf16[64,1536]{1,0:T(8,128)(2,1)S(1)}, bf16[64,1536]{1,0:T(8,128)(2,1)S(1)}, u32[]{:S(2)}, u32[]{:S(2)}) %collective-permute-start.17) | collective-permute-done | bytes 196640 | tf_op jit(solution)/shard_map/ppermute | solution.py:28
  50.6 1.6 %collective-permute-start.21 = (bf16[128,1536]{1,0:T(8,128)(2,1)S(1)}, bf16[128,1536]{1,0:T(8,128)(2,1)S(1)}, u32[]{:S(2)}, u32[]{:S(2)}) collective-permute-start(bf16[128,1536]{1,0:T(8,128)(2,1)S(1)} %join1.1.refs_8_.refs_3_.refs_7_), channel_id=1, source_target_pairs={{0,2},{1,3},{2,0},{3,1},{4,6},{5,7},{6,4},{7,5},{8,10},{9,11},{10,... | collective-permute-start | bytes 1179656 | tf_op jit(solution)/shard_map/ppermute | solution.py:28
  52.2 0.8 %collective-permute-done.15.refs_10_.refs_2_.refs_6_ = bf16[32,1536]{1,0:T(8,128)(2,1)S(1)} collective-permute-done((bf16[32,1536]{1,0:T(8,128)(2,1)S(1)}, bf16[32,1536]{1,0:T(8,128)(2,1)S(1)}, u32[]{:S(2)}, u32[]{:S(2)}) %collective-permute-start.15) | collective-permute-done | bytes 98336 | tf_op jit(solution)/shard_map/ppermute | solution.py:28
  53.0 2.1 %collective-permute-done.14.refs_9_.refs_1_.refs_5_ = bf16[32,1536]{1,0:T(8,128)(2,1)S(1)} collective-permute-done((bf16[32,1536]{1,0:T(8,128)(2,1)S(1)}, bf16[32,1536]{1,0:T(8,128)(2,1)S(1)}, u32[]{:S(2)}, u32[]{:S(2)}) %collective-permute-start.14) | collective-permute-done | bytes 98336 | tf_op jit(solution)/shard_map/ppermute | solution.py:28
  55.1 0.7 choose2.1
  55.9 1.9 %collective-permute-start.19 = (bf16[96,1536]{1,0:T(8,128)(2,1)S(1)}, bf16[96,1536]{1,0:T(8,128)(2,1)S(1)}, u32[]{:S(2)}, u32[]{:S(2)}) collective-permute-start(bf16[96,1536]{1,0:T(8,128)(2,1)S(1)} %stack3.1.refs_2_), channel_id=1, source_target_pairs={{0,4},{4,0},{8,12},{12,8},{16,20},{20,16},{24,28},{28,24},{1,5},{5... | collective-permute-start | bytes 884744 | tf_op jit(solution)/shard_map/ppermute | solution.py:28
  57.9 3.7 %collective-permute-done.20.refs_1_ = bf16[64,1536]{1,0:T(8,128)(2,1)S(1)} collective-permute-done((bf16[64,1536]{1,0:T(8,128)(2,1)S(1)}, bf16[64,1536]{1,0:T(8,128)(2,1)S(1)}, u32[]{:S(2)}, u32[]{:S(2)}) %collective-permute-start.20) | collective-permute-done | bytes 196640 | tf_op jit(solution)/shard_map/ppermute | solution.py:28
  61.6 1.6 %collective-permute-start.23 = (bf16[128,1536]{1,0:T(8,128)(2,1)S(1)}, bf16[128,1536]{1,0:T(8,128)(2,1)S(1)}, u32[]{:S(2)}, u32[]{:S(2)}) collective-permute-start(bf16[128,1536]{1,0:T(8,128)(2,1)S(1)} %join2.1.refs_8_.refs_3_.refs_5_), channel_id=1, source_target_pairs={{0,2},{1,3},{2,0},{3,1},{4,6},{5,7},{6,4},{7,5},{8,10},{9,11},{10,... | collective-permute-start | bytes 1179656 | tf_op jit(solution)/shard_map/ppermute | solution.py:28
  63.2 0.7 choose3.1
  63.9 1.6 %collective-permute-start.22 = (bf16[64,1536]{1,0:T(8,128)(2,1)S(1)}, bf16[64,1536]{1,0:T(8,128)(2,1)S(1)}, u32[]{:S(2)}, u32[]{:S(2)}) collective-permute-start(bf16[64,1536]{1,0:T(8,128)(2,1)S(1)} %get-tuple-element.54), channel_id=1, source_target_pairs={{0,8},{4,12},{8,0},{12,4},{16,24},{20,28},{24,16},{28,20},{1,9},{5... | collective-permute-start | bytes 589832 | tf_op jit(solution)/shard_map/ppermute | solution.py:28
  65.6 2.0 %early.1 = (f32[256,1536]{1,0:T(8,128)S(1)}, f32[256,1536]{1,0:T(8,128)S(1)}) custom-call(bf16[512,1536]{1,0:T(8,128)(2,1)S(1)} %pad_maximum_fusion.refs_0_, f32[512,1]{1,0:T(8,128)S(1)} %bitcast.45, bf16[512,32]{1,0:T(8,128)(2,1)S(1)} %pad_maximum_fusion.1.refs_13_.refs_2_, f32[1,512]{1,0:T(1,128)S(1)} %constant_dynamic-update-slice_fusion.16.refs_14_.refs_3_, ...), custom_call_target="tpu_custom_call" | custom-call | flops 1 | bytes 1 | tf_op jit(solution)/shard_map/early/pallas_call | solution.py:57
  67.7 1.9 %collective-permute-done.22.refs_1_ = bf16[64,1536]{1,0:T(8,128)(2,1)S(1)} collective-permute-done((bf16[64,1536]{1,0:T(8,128)(2,1)S(1)}, bf16[64,1536]{1,0:T(8,128)(2,1)S(1)}, u32[]{:S(2)}, u32[]{:S(2)}) %collective-permute-start.22) | collective-permute-done | bytes 196640 | tf_op jit(solution)/shard_map/ppermute | solution.py:28
  69.7 1.3 %collective-permute-start.24 = (bf16[128,1536]{1,0:T(8,128)(2,1)S(1)}, bf16[128,1536]{1,0:T(8,128)(2,1)S(1)}, u32[]{:S(2)}, u32[]{:S(2)}) collective-permute-start(bf16[128,1536]{1,0:T(8,128)(2,1)S(1)} %join3.1.refs_11_.refs_5_), channel_id=1, source_target_pairs={{0,2},{1,3},{2,0},{3,1},{4,6},{5,7},{6,4},{7,5},{8,10},{9,11},{10,... | collective-permute-start | bytes 1179656 | tf_op jit(solution)/shard_map/ppermute | solution.py:28
  71.0 0.5 collective-permute-start.28
  71.5 7.8 %collective-permute-done.24.refs_6_ = bf16[128,1536]{1,0:T(8,128)(2,1)S(1)} collective-permute-done((bf16[128,1536]{1,0:T(8,128)(2,1)S(1)}, bf16[128,1536]{1,0:T(8,128)(2,1)S(1)}, u32[]{:S(2)}, u32[]{:S(2)}) %collective-permute-start.24) | collective-permute-done | bytes 393248 | tf_op jit(solution)/shard_map/ppermute | solution.py:28
  79.3 1.2 %late2.1.refs_9_.refs_10_ = f32[256,1536]{1,0:T(8,128)S(1)} custom-call(bf16[256,1536]{1,0:T(8,128)(2,1)S(1)} %bitcast.37, f32[256,1]{1,0:T(8,128)S(1)} %copy.35.refs_4_.refs_8_.refs_1_, bf16[256,32]{1,0:T(8,128)(2,1)S(1)} %bitcast.42, f32[1,512]{1,0:T(1,128)S(1)} %get-tuple-element.97.refs_6_.refs_3_, s32[1,512]{1,0:T(1,128)S(1)} %get-tuple-element.99.refs_7_.refs_4_, ...), custom_call_target="tpu_custom_call" | custom-call | flops 1 | bytes 1 | tf_op jit(solution)/shard_map/late2/pallas_call | solution.py:57
  80.5 0.5 collective-permute-done.26.refs_8_
  81.0 2.3 %late3.1 = f32[256,1536]{1,0:T(8,128)} custom-call(bf16[256,1536]{1,0:T(8,128)(2,1)S(1)} %bitcast.38, f32[256,1]{1,0:T(8,128)S(1)} %copy.35.refs_4_.refs_8_.refs_1_, bf16[256,32]{1,0:T(8,128)(2,1)S(1)} %bitcast.43, f32[1,512]{1,0:T(1,128)S(1)} %get-tuple-element.96.refs_10_.refs_3_, s32[1,512]{1,0:T(1,128)S(1)} %get-tuple-element.98.refs_11_.refs_4_, ...), custom_call_target="tpu_custom_call" | custom-call | flops 1 | bytes 1 | tf_op jit(solution)/shard_map/late3/pallas_call | solution.py:57
  (141 shorter events, 4.8 us)
Async XLA Ops:
  0.1 1.1 %copy-start = (bf16[1,256,1536]{2,1,0:T(8,128)(2,1)S(1)}, bf16[1,256,1536]{2,1,0:T(8,128)(2,1)}, u32[]{:S(2)}) copy-start(bf16[1,256,1536]{2,1,0:T(8,128)(2,1)} %param.5) | copy-start | bytes 2359300
  1.2 8.7 %copy-start.8 = (s32[2,1,1,56]{3,2,1,0:T(1,128)S(1)}, s32[2,1,1,56]{3,2,1,0:T(1,128)}, u32[]{:S(2)}) copy-start(s32[2,1,1,56]{3,2,1,0:T(1,128)} %param.9) | copy-start | bytes 1348
  1.2 8.8 %copy-start.6 = (f32[1024]{0:T(1024)S(1)}, f32[1024]{0:T(1024)}, u32[]{:S(2)}) copy-start(f32[1024]{0:T(1024)} %param.7) | copy-start | bytes 12292
  1.2 9.0 %copy-start.2 = (s32[2,8]{1,0:T(2,128)S(1)}, s32[2,8]{1,0:T(2,128)}, u32[]{:S(2)}) copy-start(s32[2,8]{1,0:T(2,128)} %refs_1_.7) | copy-start | bytes 196
  1.2 9.2 %copy-start.5 = (f32[8]{0:T(128)S(1)}, f32[8]{0:T(128)}, u32[]{:S(2)}) copy-start(f32[8]{0:T(128)} %param.6) | copy-start | bytes 100
  2.6 16.5 %collective-permute-start.1 = (bf16[64,1536]{1,0:T(8,128)(2,1)S(1)}, bf16[64,1536]{1,0:T(8,128)(2,1)S(1)}, u32[]{:S(2)}, u32[]{:S(2)}) collective-permute-start(bf16[64,1536]{1,0:T(8,128)(2,1)S(1)} %get-tuple-element.70), channel_id=1, source_target_pairs={{0,8},{4,12},{8,0},{12,4},{16,24},{20,28},{24,16},{28,20},{1,9},{5... | collective-permute-start | bytes 589832 | tf_op jit(solution)/shard_map/ppermute | solution.py:28
  5.6 9.7 %collective-permute-start.4 = (bf16[32,1536]{1,0:T(8,128)(2,1)S(1)}, bf16[32,1536]{1,0:T(8,128)(2,1)S(1)}, u32[]{:S(2)}, u32[]{:S(2)}) collective-permute-start(bf16[32,1536]{1,0:T(8,128)(2,1)S(1)} %get-tuple-element.35), channel_id=1, source_target_pairs={{0,16},{4,20},{8,24},{12,28},{16,0},{20,4},{24,8},{28,12},{1,17},{... | collective-permute-start | bytes 294920 | tf_op jit(solution)/shard_map/ppermute | solution.py:28
  8.2 8.9 %collective-permute-start.5 = (bf16[32,1536]{1,0:T(8,128)(2,1)S(1)}, bf16[32,1536]{1,0:T(8,128)(2,1)S(1)}, u32[]{:S(2)}, u32[]{:S(2)}) collective-permute-start(bf16[32,1536]{1,0:T(8,128)(2,1)S(1)} %get-tuple-element.36), channel_id=1, source_target_pairs={{0,24},{4,28},{8,16},{12,20},{16,8},{20,12},{24,0},{28,4},{1,25},{... | collective-permute-start | bytes 294920 | tf_op jit(solution)/shard_map/ppermute | solution.py:28
  8.2 13.1 %collective-permute-start = (bf16[128,1536]{1,0:T(8,128)(2,1)S(1)}, bf16[128,1536]{1,0:T(8,128)(2,1)S(1)}, u32[]{:S(2)}, u32[]{:S(2)}) collective-permute-start(bf16[128,1536]{1,0:T(8,128)(2,1)S(1)} %get-tuple-element.31.refs_3_.refs_2_), channel_id=1, source_target_pairs={{0,4},{4,0},{8,12},{12,8},{16,20},{20,16},{24,28},{28,24},{1,5},{5... | collective-permute-start | bytes 1179656 | tf_op jit(solution)/shard_map/ppermute | solution.py:28
  9.9 10.9 %collective-permute-start.7 = (s32[2,56]{1,0:T(2,128)S(1)}, s32[2,56]{1,0:T(2,128)S(1)}, u32[]{:S(2)}, u32[]{:S(2)}) collective-permute-start(s32[2,56]{1,0:T(2,128)S(1)} %bitcast.58), channel_id=1, source_target_pairs={{0,1},{1,0},{2,3},{3,2},{4,5},{5,4},{6,7},{7,6},{8,9},{9,8},{10,11... | collective-permute-start | bytes 1352 | tf_op jit(solution)/shard_map/ppermute | solution.py:28
  15.3 17.8 %collective-permute-start.2 = (bf16[32,1536]{1,0:T(8,128)(2,1)S(1)}, bf16[32,1536]{1,0:T(8,128)(2,1)}, u32[]{:S(2)}, u32[]{:S(2)}) collective-permute-start(bf16[32,1536]{1,0:T(8,128)(2,1)S(1)} %get-tuple-element.33), channel_id=1, source_target_pairs={{0,16},{4,20},{8,24},{12,28},{16,0},{20,4},{24,8},{28,12},{1,17},{... | collective-permute-start | bytes 294920 | tf_op jit(solution)/shard_map/ppermute | solution.py:28
  17.1 2.1 %copy-start.3 = (bf16[32,1536]{1,0:T(8,128)(2,1)}, bf16[32,1536]{1,0:T(8,128)(2,1)S(1)}, u32[]{:S(2)}) copy-start(bf16[32,1536]{1,0:T(8,128)(2,1)S(1)} %collective-permute-done.5.refs_2_.refs_6_) | copy-start | bytes 294916
  17.1 4.2 %copy-start.1 = (bf16[1,256,1536]{2,1,0:T(8,128)(2,1)S(1)}, bf16[1,256,1536]{2,1,0:T(8,128)(2,1)}, u32[]{:S(2)}) copy-start(bf16[1,256,1536]{2,1,0:T(8,128)(2,1)} %param.5) | copy-start | bytes 2359300
  17.1 16.5 %collective-permute-start.3 = (bf16[32,1536]{1,0:T(8,128)(2,1)S(1)}, bf16[32,1536]{1,0:T(8,128)(2,1)}, u32[]{:S(2)}, u32[]{:S(2)}) collective-permute-start(bf16[32,1536]{1,0:T(8,128)(2,1)S(1)} %get-tuple-element.34), channel_id=1, source_target_pairs={{0,24},{4,28},{8,16},{12,20},{16,8},{20,12},{24,0},{28,4},{1,25},{... | collective-permute-start | bytes 294920 | tf_op jit(solution)/shard_map/ppermute | solution.py:28
  19.1 9.2 %collective-permute-start.6 = (bf16[96,1536]{1,0:T(8,128)(2,1)S(1)}, bf16[96,1536]{1,0:T(8,128)(2,1)S(1)}, u32[]{:S(2)}, u32[]{:S(2)}) collective-permute-start(bf16[96,1536]{1,0:T(8,128)(2,1)S(1)} %stack0.1.refs_8_), channel_id=1, source_target_pairs={{0,4},{4,0},{8,12},{12,8},{16,20},{20,16},{24,28},{28,24},{1,5},{5... | collective-permute-start | bytes 884744 | tf_op jit(solution)/shard_map/ppermute | solution.py:28
  21.3 17.6 %collective-permute-start.13 = (bf16[256,1536]{1,0:T(8,128)(2,1)S(1)}, bf16[256,1536]{1,0:T(8,128)(2,1)S(1)}, u32[]{:S(2)}, u32[]{:S(2)}) collective-permute-start(bf16[256,1536]{1,0:T(8,128)(2,1)S(1)} %bitcast.35), channel_id=1, source_target_pairs={{0,1},{1,0},{2,3},{3,2},{4,5},{5,4},{6,7},{7,6},{8,9},{9,8},{10,11... | collective-permute-start | bytes 2359304 | tf_op jit(solution)/shard_map/ppermute | solution.py:28
  28.3 0.9 %copy-start.4 = (bf16[32,1536]{1,0:T(8,128)(2,1)S(1)}, bf16[32,1536]{1,0:T(8,128)(2,1)}, u32[]{:S(2)}) copy-start(bf16[32,1536]{1,0:T(8,128)(2,1)} %copy-done.3) | copy-start | bytes 294916
  30.0 8.5 %collective-permute-start.12 = (bf16[64,1536]{1,0:T(8,128)(2,1)S(1)}, bf16[64,1536]{1,0:T(8,128)(2,1)S(1)}, u32[]{:S(2)}, u32[]{:S(2)}) collective-permute-start(bf16[64,1536]{1,0:T(8,128)(2,1)S(1)} %get-tuple-element.44), channel_id=1, source_target_pairs={{0,8},{4,12},{8,0},{12,4},{16,24},{20,28},{24,16},{28,20},{1,9},{5... | collective-permute-start | bytes 589832 | tf_op jit(solution)/shard_map/ppermute | solution.py:28
  31.0 10.1 %collective-permute-start.10 = (bf16[32,1536]{1,0:T(8,128)(2,1)S(1)}, bf16[32,1536]{1,0:T(8,128)(2,1)S(1)}, u32[]{:S(2)}, u32[]{:S(2)}) collective-permute-start(bf16[32,1536]{1,0:T(8,128)(2,1)S(1)} %get-tuple-element.43), channel_id=1, source_target_pairs={{0,24},{4,28},{8,16},{12,20},{16,8},{20,12},{24,0},{28,4},{1,25},{... | collective-permute-start | bytes 294920 | tf_op jit(solution)/shard_map/ppermute | solution.py:28
  33.2 8.6 %collective-permute-start.9 = (bf16[32,1536]{1,0:T(8,128)(2,1)S(1)}, bf16[32,1536]{1,0:T(8,128)(2,1)S(1)}, u32[]{:S(2)}, u32[]{:S(2)}) collective-permute-start(bf16[32,1536]{1,0:T(8,128)(2,1)S(1)} %get-tuple-element.41), channel_id=1, source_target_pairs={{0,16},{4,20},{8,24},{12,28},{16,0},{20,4},{24,8},{28,12},{1,17},{... | collective-permute-start | bytes 294920 | tf_op jit(solution)/shard_map/ppermute | solution.py:28
  33.5 5.0 %copy-start.7 = (bf16[64,1536]{1,0:T(8,128)(2,1)S(1)}, bf16[64,1536]{1,0:T(8,128)(2,1)}, u32[]{:S(2)}) copy-start(bf16[64,1536]{1,0:T(8,128)(2,1)} %get-tuple-element.38) | copy-start | bytes 589828
  34.5 7.5 %collective-permute-start.11 = (bf16[96,1536]{1,0:T(8,128)(2,1)S(1)}, bf16[96,1536]{1,0:T(8,128)(2,1)S(1)}, u32[]{:S(2)}, u32[]{:S(2)}) collective-permute-start(bf16[96,1536]{1,0:T(8,128)(2,1)S(1)} %stack1.1.refs_2_), channel_id=1, source_target_pairs={{0,4},{4,0},{8,12},{12,8},{16,20},{20,16},{24,28},{28,24},{1,5},{5... | collective-permute-start | bytes 884744 | tf_op jit(solution)/shard_map/ppermute | solution.py:28
  38.5 6.9 %collective-permute-start.8 = (bf16[64,1536]{1,0:T(8,128)(2,1)S(1)}, bf16[64,1536]{1,0:T(8,128)(2,1)S(1)}, u32[]{:S(2)}, u32[]{:S(2)}) collective-permute-start(bf16[64,1536]{1,0:T(8,128)(2,1)S(1)} %copy-done.7), channel_id=1, source_target_pairs={{0,8},{4,12},{8,0},{12,4},{16,24},{20,28},{24,16},{28,20},{1,9},{5... | collective-permute-start | bytes 589832 | tf_op jit(solution)/shard_map/ppermute | solution.py:28
  38.9 11.7 %collective-permute-start.18 = (bf16[128,1536]{1,0:T(8,128)(2,1)S(1)}, bf16[128,1536]{1,0:T(8,128)(2,1)S(1)}, u32[]{:S(2)}, u32[]{:S(2)}) collective-permute-start(bf16[128,1536]{1,0:T(8,128)(2,1)S(1)} %join0.1.refs_8_.refs_3_.refs_5_), channel_id=1, source_target_pairs={{0,2},{1,3},{2,0},{3,1},{4,6},{5,7},{6,4},{7,5},{8,10},{9,11},{10,... | collective-permute-start | bytes 1179656 | tf_op jit(solution)/shard_map/ppermute | solution.py:28
  43.2 7.3 %collective-permute-start.17 = (bf16[64,1536]{1,0:T(8,128)(2,1)S(1)}, bf16[64,1536]{1,0:T(8,128)(2,1)S(1)}, u32[]{:S(2)}, u32[]{:S(2)}) collective-permute-start(bf16[64,1536]{1,0:T(8,128)(2,1)S(1)} %get-tuple-element.50), channel_id=1, source_target_pairs={{0,8},{4,12},{8,0},{12,4},{16,24},{20,28},{24,16},{28,20},{1,9},{5... | collective-permute-start | bytes 589832 | tf_op jit(solution)/shard_map/ppermute | solution.py:28
  45.4 9.7 %collective-permute-start.16 = (bf16[96,1536]{1,0:T(8,128)(2,1)S(1)}, bf16[96,1536]{1,0:T(8,128)(2,1)S(1)}, u32[]{:S(2)}, u32[]{:S(2)}) collective-permute-start(bf16[96,1536]{1,0:T(8,128)(2,1)S(1)} %stack2.1.refs_2_), channel_id=1, source_target_pairs={{0,4},{4,0},{8,12},{12,8},{16,20},{20,16},{24,28},{28,24},{1,5},{5... | collective-permute-start | bytes 884744 | tf_op jit(solution)/shard_map/ppermute | solution.py:28
  45.6 7.4 %collective-permute-start.15 = (bf16[32,1536]{1,0:T(8,128)(2,1)S(1)}, bf16[32,1536]{1,0:T(8,128)(2,1)S(1)}, u32[]{:S(2)}, u32[]{:S(2)}) collective-permute-start(bf16[32,1536]{1,0:T(8,128)(2,1)S(1)} %get-tuple-element.49), channel_id=1, source_target_pairs={{0,24},{4,28},{8,16},{12,20},{16,8},{20,12},{24,0},{28,4},{1,25},{... | collective-permute-start | bytes 294920 | tf_op jit(solution)/shard_map/ppermute | solution.py:28
  47.5 7.6 %collective-permute-start.14 = (bf16[32,1536]{1,0:T(8,128)(2,1)S(1)}, bf16[32,1536]{1,0:T(8,128)(2,1)S(1)}, u32[]{:S(2)}, u32[]{:S(2)}) collective-permute-start(bf16[32,1536]{1,0:T(8,128)(2,1)S(1)} %get-tuple-element.47), channel_id=1, source_target_pairs={{0,16},{4,20},{8,24},{12,28},{16,0},{20,4},{24,8},{28,12},{1,17},{... | collective-permute-start | bytes 294920 | tf_op jit(solution)/shard_map/ppermute | solution.py:28
  50.6 11.0 %collective-permute-start.21 = (bf16[128,1536]{1,0:T(8,128)(2,1)S(1)}, bf16[128,1536]{1,0:T(8,128)(2,1)S(1)}, u32[]{:S(2)}, u32[]{:S(2)}) collective-permute-start(bf16[128,1536]{1,0:T(8,128)(2,1)S(1)} %join1.1.refs_8_.refs_3_.refs_7_), channel_id=1, source_target_pairs={{0,2},{1,3},{2,0},{3,1},{4,6},{5,7},{6,4},{7,5},{8,10},{9,11},{10,... | collective-permute-start | bytes 1179656 | tf_op jit(solution)/shard_map/ppermute | solution.py:28
  55.8 5.7 %collective-permute-start.20 = (bf16[64,1536]{1,0:T(8,128)(2,1)S(1)}, bf16[64,1536]{1,0:T(8,128)(2,1)S(1)}, u32[]{:S(2)}, u32[]{:S(2)}) collective-permute-start(bf16[64,1536]{1,0:T(8,128)(2,1)S(1)} %get-tuple-element.52), channel_id=1, source_target_pairs={{0,8},{4,12},{8,0},{12,4},{16,24},{20,28},{24,16},{28,20},{1,9},{5... | collective-permute-start | bytes 589832 | tf_op jit(solution)/shard_map/ppermute | solution.py:28
  55.9 7.2 %collective-permute-start.19 = (bf16[96,1536]{1,0:T(8,128)(2,1)S(1)}, bf16[96,1536]{1,0:T(8,128)(2,1)S(1)}, u32[]{:S(2)}, u32[]{:S(2)}) collective-permute-start(bf16[96,1536]{1,0:T(8,128)(2,1)S(1)} %stack3.1.refs_2_), channel_id=1, source_target_pairs={{0,4},{4,0},{8,12},{12,8},{16,20},{20,16},{24,28},{28,24},{1,5},{5... | collective-permute-start | bytes 884744 | tf_op jit(solution)/shard_map/ppermute | solution.py:28
  61.6 8.1 %collective-permute-start.23 = (bf16[128,1536]{1,0:T(8,128)(2,1)S(1)}, bf16[128,1536]{1,0:T(8,128)(2,1)S(1)}, u32[]{:S(2)}, u32[]{:S(2)}) collective-permute-start(bf16[128,1536]{1,0:T(8,128)(2,1)S(1)} %join2.1.refs_8_.refs_3_.refs_5_), channel_id=1, source_target_pairs={{0,2},{1,3},{2,0},{3,1},{4,6},{5,7},{6,4},{7,5},{8,10},{9,11},{10,... | collective-permute-start | bytes 1179656 | tf_op jit(solution)/shard_map/ppermute | solution.py:28
  63.9 5.7 %collective-permute-start.22 = (bf16[64,1536]{1,0:T(8,128)(2,1)S(1)}, bf16[64,1536]{1,0:T(8,128)(2,1)S(1)}, u32[]{:S(2)}, u32[]{:S(2)}) collective-permute-start(bf16[64,1536]{1,0:T(8,128)(2,1)S(1)} %get-tuple-element.54), channel_id=1, source_target_pairs={{0,8},{4,12},{8,0},{12,4},{16,24},{20,28},{24,16},{28,20},{1,9},{5... | collective-permute-start | bytes 589832 | tf_op jit(solution)/shard_map/ppermute | solution.py:28
  67.6 11.7 %collective-permute-start.29 = (f32[256,1536]{1,0:T(8,128)S(1)}, f32[256,1536]{1,0:T(8,128)S(1)}, u32[]{:S(2)}, u32[]{:S(2)}) collective-permute-start(f32[256,1536]{1,0:T(8,128)S(1)} %get-tuple-element.56), channel_id=1, source_target_pairs={{0,1},{1,0},{2,3},{3,2},{4,5},{5,4},{6,7},{7,6},{8,9},{9,8},{10,11... | collective-permute-start | bytes 4718600 | tf_op jit(solution)/shard_map/ppermute | solution.py:28
  69.7 9.6 %collective-permute-start.24 = (bf16[128,1536]{1,0:T(8,128)(2,1)S(1)}, bf16[128,1536]{1,0:T(8,128)(2,1)S(1)}, u32[]{:S(2)}, u32[]{:S(2)}) collective-permute-start(bf16[128,1536]{1,0:T(8,128)(2,1)S(1)} %join3.1.refs_11_.refs_5_), channel_id=1, source_target_pairs={{0,2},{1,3},{2,0},{3,1},{4,6},{5,7},{6,4},{7,5},{8,10},{9,11},{10,... | collective-permute-start | bytes 1179656 | tf_op jit(solution)/shard_map/ppermute | solution.py:28
  71.0 8.3 %collective-permute-start.27 = (bf16[128,1536]{1,0:T(8,128)(2,1)S(1)}, bf16[128,1536]{1,0:T(8,128)(2,1)S(1)}, u32[]{:S(2)}, u32[]{:S(2)}) collective-permute-start(bf16[128,1536]{1,0:T(8,128)(2,1)S(1)} %join2.1.refs_8_.refs_3_.refs_5_), channel_id=1, source_target_pairs={{0,1},{1,0},{2,3},{3,2},{4,5},{5,4},{6,7},{7,6},{8,9},{9,8},{10,11... | collective-permute-start | bytes 1179656 | tf_op jit(solution)/shard_map/ppermute | solution.py:28
  71.0 8.3 %collective-permute-start.28 = (bf16[128,1536]{1,0:T(8,128)(2,1)S(1)}, bf16[128,1536]{1,0:T(8,128)(2,1)S(1)}, u32[]{:S(2)}, u32[]{:S(2)}) collective-permute-start(bf16[128,1536]{1,0:T(8,128)(2,1)S(1)} %collective-permute-done.23.refs_4_.refs_6_), channel_id=1, source_target_pairs={{0,1},{1,0},{2,3},{3,2},{4,5},{5,4},{6,7},{7,6},{8,9},{9,8},{10,11... | collective-permute-start | bytes 1179656 | tf_op jit(solution)/shard_map/ppermute | solution.py:28
  71.5 9.0 %collective-permute-start.25 = (bf16[128,1536]{1,0:T(8,128)(2,1)S(1)}, bf16[128,1536]{1,0:T(8,128)(2,1)S(1)}, u32[]{:S(2)}, u32[]{:S(2)}) collective-permute-start(bf16[128,1536]{1,0:T(8,128)(2,1)S(1)} %join3.1.refs_11_.refs_5_), channel_id=1, source_target_pairs={{0,1},{1,0},{2,3},{3,2},{4,5},{5,4},{6,7},{7,6},{8,9},{9,8},{10,11... | collective-permute-start | bytes 1179656 | tf_op jit(solution)/shard_map/ppermute | solution.py:28
  79.3 1.7 %collective-permute-start.26 = (bf16[128,1536]{1,0:T(8,128)(2,1)S(1)}, bf16[128,1536]{1,0:T(8,128)(2,1)S(1)}, u32[]{:S(2)}, u32[]{:S(2)}) collective-permute-start(bf16[128,1536]{1,0:T(8,128)(2,1)S(1)} %collective-permute-done.24.refs_6_), channel_id=1, source_target_pairs={{0,1},{1,0},{2,3},{3,2},{4,5},{5,4},{6,7},{7,6},{8,9},{9,8},{10,11... | collective-permute-start | bytes 1179656 | tf_op jit(solution)/shard_map/ppermute | solution.py:28

commit v4 on v3

--- a/solution.py
+++ b/solution.py
@@ -8,16 +8,21 @@
 TILE = 64
 SHARES = (2, 2, 2, 2)
 FGROUPS = ((0,), (1,), (2,), (3,))
-FGATE = {2: "c0", 3: "s2"}
-FNEED = {2: "c1", 3: "c2"}
-NEAR_FIRST, NGATE = 2, "s1"
+FGATE = {1: "s0", 2: "s1", 3: "c1"}
+FNEED = {}
+NEAR_FIRST, NGATE = 2, "c0"
 BSTART, BNEED = "s0", "j0"
 XNEED = "j1"
-SETNEED = "s1"
-EARLY = 1
+SETNEED = "s0"
+EARLY = 2
+PGATE = "none"
+CGATE = True
+PCUTS = (128, 128)
+PTYPE = jnp.bfloat16
 TAIL = 2
 ORDER = "s"
 FL, FK, BY = 10**10, 1, 1
+FE = 10**10
 WS, WJ, WC = 10**10, 10**10, 10**10
 VMEM = pl.BlockSpec(memory_space=pltpu.VMEM)
 SMEM = pl.BlockSpec(memory_space=pltpu.SMEM)
@@ -83,11 +88,13 @@
     gap = gap_ref[...] + right_ref[...]
     amplitude = jnp.where(listed > 0.5, scores / gap, 0.0).astype(jnp.bfloat16)
     part = jnp.dot(amplitude, rows, preferred_element_type=jnp.float32)
-    for ref in added_refs:
-        part += ref[...]
+    if added_refs:
+        part += added_refs[0][...]
+        if len(added_refs) > 1:
+            part += jnp.concatenate([r[...].astype(jnp.float32) for r in added_refs[1:]], axis=0)
     at = 0
     for ref in out_refs:
-        ref[...] = part[at : at + ref.shape[0]]
+        ref[...] = part[at : at + ref.shape[0]].astype(ref.dtype)
         at += ref.shape[0]
 
 
@@ -190,8 +197,8 @@
         def kernel(*refs):
             part_kernel(*refs, row_count=len(row_refs), added=len(added))
 
-        shapes = [jax.ShapeDtypeStruct((n, aux), jnp.float32) for n in outs]
-        return chain.call(kernel, [], arrays, shapes, name, waits, FK)
+        shapes = [jax.ShapeDtypeStruct((n, aux), PTYPE if i else jnp.float32) for i, n in enumerate(outs)]
+        return chain.call(kernel, [], arrays, shapes, name, waits, FE if name == "early" else FK)
 
     far_masks = [half ^ (m * unit) for m in range(places)]
     near_masks = [m * unit for m in range(1, places)]
@@ -292,16 +299,17 @@
             mask //= 2
         wide[t] = [ready[m] for m in x_order]
 
-    added = []
+    added, fulls, held_back = [], {}, []
     def add_early():
         lefts = jnp.concatenate([own, beside], axis=0)
-        mine, other = add_part(
-            lefts, sets[0], [v for c in early for v in wide[c]], [], [slice_rows] * 2, "early"
+        return add_part(
+            lefts, sets[0], [v for c in early for v in wide[c]], [], [slice_rows, *PCUTS], "early"
         )
-        return [mine, send(other, "virt", 1)]
 
     def full(c):
-        return wide[c] + [send(w, "virt", 1) for w in wide[c]]
+        if c not in fulls:
+            fulls[c] = wide[c] + [send(after(w, *held_back), "virt", 1) for w in wide[c]]
+        return fulls[c]
 
     def gate(kind, t):
         nonlocal beside
@@ -332,6 +340,12 @@
     join(count - 1)
     if early and EARLY == 2:
         added = add_early()
+    if early:
+        held_back = chain.last if CGATE else []
+        mine, *others = added
+        if PGATE == "j":
+            others = [after(v, *chain.last) for v in others]
+        added = [mine] + [send(v, "virt", 1) for v in others]
     for c in late:
         added = add_part(own, sets[c], full(c), added, [slice_rows], f"late{c}")
     return added[0][None]

time: 83.6 us -> 80.3 us (0.961)
  waiting for transfers between devices: 32.2 us -> 28.2 us
  starting transfers between devices: 31.3 us -> 35.1 us
  local copies, waits for them, and re-layouts: 7.15 us -> 5.57 us
  Pallas kernels: 10.6 us -> 9.27 us
    ppermute x30 -> x31, waiting for transfers between devices: 32.2 us -> 28.2 us  [send(): lax.ppermute(value, axis, [(i, i ^ mask) for i in range(lax.axis_size(axi...]
    ppermute x30 -> x31, starting transfers between devices: 31.3 us -> 35.1 us  [send(): lax.ppermute(value, axis, [(i, i ^ mask) for i in range(lax.axis_size(axi...]
    pallas_call x16, Pallas kernels: 10.6 us -> 9.27 us  [call(): pl.pallas_call(run, out_shape=tuple(outs), in_specs=[SMEM] * len(smem) +...]
    unnamed x38 -> x32, local copies, waits for them, and re-layouts: 2.34 us -> 1.44 us
  transfers between devices with their start and end apart: 30 -> 31, of which waited for: 13 -> 14; matrix products, arithmetic and copies ran while one was open for 7% -> 7% of each run, Pallas kernels for 9% -> 8%
where the time goes in v4:
time: 80.3 us; the launch traced here: 80.2 us
  starting transfers between devices  35.1 us (44%)
  waiting for transfers between devices  28.2 us (35%)
  Pallas kernels  9.27 us (12%)
  local copies, waits for them, and re-layouts  5.57 us (7%)
  other arithmetic  1.62 us (2%)
    ppermute x31, starting transfers between devices, send(): lax.ppermute(value, axis, [(i, i ^ mask) for i in range(lax.axis_size(axi...  35.1 us
    ppermute x31, waiting for transfers between devices, send(): lax.ppermute(value, axis, [(i, i ^ mask) for i in range(lax.axis_size(axi...  28.2 us
    pallas_call x16, Pallas kernels, call(): pl.pallas_call(run, out_shape=tuple(outs), in_specs=[SMEM] * len(smem) +...  9.27 us
    another operation x24, local copies, waits for them, and re-layouts, column(): x[m, :, :, slice(*spans[c])].reshape(1, -1)  1.98 us
  transfers between devices with their start and end apart: 31, of which 14 were waited for; matrix products, arithmetic and copies ran while one was open for 7% of the time, Pallas kernels for 8%

profile of v4, /device:TPU:0, one launch (start us, length us, event | category | flops | bytes accessed | tf_op | source)
XLA Modules:
  0.0 80.2 jit_solution(6873664897772245983)
XLA Ops:
  0.1 1.1 %copy-done = bf16[1,256,1536]{2,1,0:T(8,128)(2,1)S(1)} copy-done((bf16[1,256,1536]{2,1,0:T(8,128)(2,1)S(1)}, bf16[1,256,1536]{2,1,0:T(8,128)(2,1)}, u32[]{:S(2)}) %copy-start) | copy-done | bytes 786456
  1.2 0.7 cut.1
  1.9 3.1 %collective-permute-start.1 = (bf16[64,1536]{1,0:T(8,128)(2,1)S(1)}, bf16[64,1536]{1,0:T(8,128)(2,1)S(1)}, u32[]{:S(2)}, u32[]{:S(2)}) collective-permute-start(bf16[64,1536]{1,0:T(8,128)(2,1)S(1)} %get-tuple-element.84), channel_id=1, source_target_pairs={{0,8},{4,12},{8,0},{12,4},{16,24},{20,28},{24,16},{28,20},{1,9},{5... | collective-permute-start | bytes 589832 | tf_op jit(solution)/shard_map/ppermute | solution.py:33
  5.0 2.6 %collective-permute-start.2 = (bf16[32,1536]{1,0:T(8,128)(2,1)S(1)}, bf16[32,1536]{1,0:T(8,128)(2,1)S(1)}, u32[]{:S(2)}, u32[]{:S(2)}) collective-permute-start(bf16[32,1536]{1,0:T(8,128)(2,1)S(1)} %get-tuple-element.40), channel_id=1, source_target_pairs={{0,16},{4,20},{8,24},{12,28},{16,0},{20,4},{24,8},{28,12},{1,17},{... | collective-permute-start | bytes 294920 | tf_op jit(solution)/shard_map/ppermute | solution.py:33
  7.6 1.7 %collective-permute-start = (bf16[128,1536]{1,0:T(8,128)(2,1)S(1)}, bf16[128,1536]{1,0:T(8,128)(2,1)S(1)}, u32[]{:S(2)}, u32[]{:S(2)}) collective-permute-start(bf16[128,1536]{1,0:T(8,128)(2,1)S(1)} %get-tuple-element.38.refs_3_.refs_2_), channel_id=1, source_target_pairs={{0,4},{4,0},{8,12},{12,8},{16,20},{20,16},{24,28},{28,24},{1,5},{5... | collective-permute-start | bytes 1179656 | tf_op jit(solution)/shard_map/ppermute | solution.py:33
  9.8 0.6 dynamic_slice.4
  10.4 0.6 gather_fusion
  13.7 0.7 fusion.3
  15.5 0.9 %collective-permute-done.3.refs_2_.refs_6_ = bf16[32,1536]{1,0:T(8,128)(2,1)S(1)} collective-permute-done((bf16[32,1536]{1,0:T(8,128)(2,1)S(1)}, bf16[32,1536]{1,0:T(8,128)(2,1)S(1)}, u32[]{:S(2)}, u32[]{:S(2)}) %collective-permute-start.3) | collective-permute-done | bytes 98336 | tf_op jit(solution)/shard_map/ppermute | solution.py:33
  16.4 1.6 %collective-permute-start.5 = (bf16[96,1536]{1,0:T(8,128)(2,1)S(1)}, bf16[96,1536]{1,0:T(8,128)(2,1)S(1)}, u32[]{:S(2)}, u32[]{:S(2)}) collective-permute-start(bf16[96,1536]{1,0:T(8,128)(2,1)S(1)} %stack0.1.refs_8_), channel_id=1, source_target_pairs={{0,4},{4,0},{8,12},{12,8},{16,20},{20,16},{24,28},{28,24},{1,5},{5... | collective-permute-start | bytes 884744 | tf_op jit(solution)/shard_map/ppermute | solution.py:33
  18.0 1.7 %collective-permute-start.8 = (bf16[32,1536]{1,0:T(8,128)(2,1)S(1)}, bf16[32,1536]{1,0:T(8,128)(2,1)S(1)}, u32[]{:S(2)}, u32[]{:S(2)}) collective-permute-start(bf16[32,1536]{1,0:T(8,128)(2,1)S(1)} %get-tuple-element.48), channel_id=1, source_target_pairs={{0,24},{4,28},{8,16},{12,20},{16,8},{20,12},{24,0},{28,4},{1,25},{... | collective-permute-start | bytes 294920 | tf_op jit(solution)/shard_map/ppermute | solution.py:33
  19.7 0.7 collective-permute-start.7
  20.4 5.1 %collective-permute-done.5.refs_7_ = bf16[96,1536]{1,0:T(8,128)(2,1)S(1)} collective-permute-done((bf16[96,1536]{1,0:T(8,128)(2,1)S(1)}, bf16[96,1536]{1,0:T(8,128)(2,1)S(1)}, u32[]{:S(2)}, u32[]{:S(2)}) %collective-permute-start.5) | collective-permute-done | bytes 294944 | tf_op jit(solution)/shard_map/ppermute | solution.py:33
  25.5 0.7 choose0.1
  26.2 1.0 %collective-permute-start.10 = (bf16[64,1536]{1,0:T(8,128)(2,1)S(1)}, bf16[64,1536]{1,0:T(8,128)(2,1)S(1)}, u32[]{:S(2)}, u32[]{:S(2)}) collective-permute-start(bf16[64,1536]{1,0:T(8,128)(2,1)S(1)} %get-tuple-element.49), channel_id=1, source_target_pairs={{0,8},{4,12},{8,0},{12,4},{16,24},{20,28},{24,16},{28,20},{1,9},{5... | collective-permute-start | bytes 589832 | tf_op jit(solution)/shard_map/ppermute | solution.py:33
  27.2 1.0 %collective-permute-done.7.refs_1_.refs_5_ = bf16[32,1536]{1,0:T(8,128)(2,1)S(1)} collective-permute-done((bf16[32,1536]{1,0:T(8,128)(2,1)S(1)}, bf16[32,1536]{1,0:T(8,128)(2,1)S(1)}, u32[]{:S(2)}, u32[]{:S(2)}) %collective-permute-start.7) | collective-permute-done | bytes 98336 | tf_op jit(solution)/shard_map/ppermute | solution.py:33
  28.2 1.3 %collective-permute-start.9 = (bf16[96,1536]{1,0:T(8,128)(2,1)S(1)}, bf16[96,1536]{1,0:T(8,128)(2,1)S(1)}, u32[]{:S(2)}, u32[]{:S(2)}) collective-permute-start(bf16[96,1536]{1,0:T(8,128)(2,1)S(1)} %stack1.1.refs_2_), channel_id=1, source_target_pairs={{0,4},{4,0},{8,12},{12,8},{16,20},{20,16},{24,28},{28,24},{1,5},{5... | collective-permute-start | bytes 884744 | tf_op jit(solution)/shard_map/ppermute | solution.py:33
  29.5 2.8 %collective-permute-start.14 = (bf16[32,1536]{1,0:T(8,128)(2,1)S(1)}, bf16[32,1536]{1,0:T(8,128)(2,1)S(1)}, u32[]{:S(2)}, u32[]{:S(2)}) collective-permute-start(bf16[32,1536]{1,0:T(8,128)(2,1)S(1)} %get-tuple-element.56), channel_id=1, source_target_pairs={{0,16},{4,20},{8,24},{12,28},{16,0},{20,4},{24,8},{28,12},{1,17},{... | collective-permute-start | bytes 294920 | tf_op jit(solution)/shard_map/ppermute | solution.py:33
  32.5 0.6 collective-permute-start.6
  33.1 2.1 %collective-permute-start.18 = (bf16[128,1536]{1,0:T(8,128)(2,1)S(1)}, bf16[128,1536]{1,0:T(8,128)(2,1)S(1)}, u32[]{:S(2)}, u32[]{:S(2)}) collective-permute-start(bf16[128,1536]{1,0:T(8,128)(2,1)S(1)} %join0.1.refs_8_.refs_3_.refs_5_), channel_id=1, source_target_pairs={{0,2},{1,3},{2,0},{3,1},{4,6},{5,7},{6,4},{7,5},{8,10},{9,11},{10,... | collective-permute-start | bytes 1179656 | tf_op jit(solution)/shard_map/ppermute | solution.py:33
  35.3 1.1 %collective-permute-done.9.refs_7_ = bf16[96,1536]{1,0:T(8,128)(2,1)S(1)} collective-permute-done((bf16[96,1536]{1,0:T(8,128)(2,1)S(1)}, bf16[96,1536]{1,0:T(8,128)(2,1)S(1)}, u32[]{:S(2)}, u32[]{:S(2)}) %collective-permute-start.9) | collective-permute-done | bytes 294944 | tf_op jit(solution)/shard_map/ppermute | solution.py:33
  36.3 0.7 choose1.1
  37.1 1.0 %collective-permute-start.17 = (bf16[64,1536]{1,0:T(8,128)(2,1)S(1)}, bf16[64,1536]{1,0:T(8,128)(2,1)S(1)}, u32[]{:S(2)}, u32[]{:S(2)}) collective-permute-start(bf16[64,1536]{1,0:T(8,128)(2,1)S(1)} %get-tuple-element.59), channel_id=1, source_target_pairs={{0,8},{4,12},{8,0},{12,4},{16,24},{20,28},{24,16},{28,20},{1,9},{5... | collective-permute-start | bytes 589832 | tf_op jit(solution)/shard_map/ppermute | solution.py:33
  38.1 1.5 %collective-permute-done.14.refs_1_.refs_5_ = bf16[32,1536]{1,0:T(8,128)(2,1)S(1)} collective-permute-done((bf16[32,1536]{1,0:T(8,128)(2,1)S(1)}, bf16[32,1536]{1,0:T(8,128)(2,1)S(1)}, u32[]{:S(2)}, u32[]{:S(2)}) %collective-permute-start.14) | collective-permute-done | bytes 98336 | tf_op jit(solution)/shard_map/ppermute | solution.py:33
  39.6 0.5 collective-permute-done.15.refs_2_.refs_6_
  40.1 2.5 %collective-permute-done.6.refs_0_.refs_4_ = bf16[64,1536]{1,0:T(8,128)(2,1)S(1)} collective-permute-done((bf16[64,1536]{1,0:T(8,128)(2,1)S(1)}, bf16[64,1536]{1,0:T(8,128)(2,1)S(1)}, u32[]{:S(2)}, u32[]{:S(2)}) %collective-permute-start.6) | collective-permute-done | bytes 196640 | tf_op jit(solution)/shard_map/ppermute | solution.py:33
  42.6 2.3 %collective-permute-start.16 = (bf16[96,1536]{1,0:T(8,128)(2,1)S(1)}, bf16[96,1536]{1,0:T(8,128)(2,1)S(1)}, u32[]{:S(2)}, u32[]{:S(2)}) collective-permute-start(bf16[96,1536]{1,0:T(8,128)(2,1)S(1)} %stack2.1.refs_2_), channel_id=1, source_target_pairs={{0,4},{4,0},{8,12},{12,8},{16,20},{20,16},{24,28},{28,24},{1,5},{5... | collective-permute-start | bytes 884744 | tf_op jit(solution)/shard_map/ppermute | solution.py:33
  44.8 4.0 %collective-permute-start.13 = (bf16[32,1536]{1,0:T(8,128)(2,1)S(1)}, bf16[32,1536]{1,0:T(8,128)(2,1)S(1)}, u32[]{:S(2)}, u32[]{:S(2)}) collective-permute-start(bf16[32,1536]{1,0:T(8,128)(2,1)S(1)} %get-tuple-element.54), channel_id=1, source_target_pairs={{0,24},{4,28},{8,16},{12,20},{16,8},{20,12},{24,0},{28,4},{1,25},{... | collective-permute-start | bytes 294920 | tf_op jit(solution)/shard_map/ppermute | solution.py:33
  48.9 1.6 %collective-permute-start.21 = (bf16[128,1536]{1,0:T(8,128)(2,1)S(1)}, bf16[128,1536]{1,0:T(8,128)(2,1)S(1)}, u32[]{:S(2)}, u32[]{:S(2)}) collective-permute-start(bf16[128,1536]{1,0:T(8,128)(2,1)S(1)} %join1.1.refs_8_.refs_3_.refs_7_), channel_id=1, source_target_pairs={{0,2},{1,3},{2,0},{3,1},{4,6},{5,7},{6,4},{7,5},{8,10},{9,11},{10,... | collective-permute-start | bytes 1179656 | tf_op jit(solution)/shard_map/ppermute | solution.py:33
  50.5 0.7 choose2.1
  51.2 0.7 collective-permute-start.20
  52.0 2.4 %collective-permute-done.12.refs_1_.refs_5_ = bf16[32,1536]{1,0:T(8,128)(2,1)S(1)} collective-permute-done((bf16[32,1536]{1,0:T(8,128)(2,1)S(1)}, bf16[32,1536]{1,0:T(8,128)(2,1)S(1)}, u32[]{:S(2)}, u32[]{:S(2)}) %collective-permute-start.12) | collective-permute-done | bytes 98336 | tf_op jit(solution)/shard_map/ppermute | solution.py:33
  54.4 0.9 %collective-permute-start.19 = (bf16[96,1536]{1,0:T(8,128)(2,1)S(1)}, bf16[96,1536]{1,0:T(8,128)(2,1)S(1)}, u32[]{:S(2)}, u32[]{:S(2)}) collective-permute-start(bf16[96,1536]{1,0:T(8,128)(2,1)S(1)} %stack3.1.refs_2_), channel_id=1, source_target_pairs={{0,4},{4,0},{8,12},{12,8},{16,20},{20,16},{24,28},{28,24},{1,5},{5... | collective-permute-start | bytes 884744 | tf_op jit(solution)/shard_map/ppermute | solution.py:33
  55.4 1.6 %collective-permute-done.20.refs_1_ = bf16[64,1536]{1,0:T(8,128)(2,1)S(1)} collective-permute-done((bf16[64,1536]{1,0:T(8,128)(2,1)S(1)}, bf16[64,1536]{1,0:T(8,128)(2,1)S(1)}, u32[]{:S(2)}, u32[]{:S(2)}) %collective-permute-start.20) | collective-permute-done | bytes 196640 | tf_op jit(solution)/shard_map/ppermute | solution.py:33
  57.0 0.4 collective-permute-done.21.refs_4_.refs_8_
  57.4 1.6 %collective-permute-start.23 = (bf16[128,1536]{1,0:T(8,128)(2,1)S(1)}, bf16[128,1536]{1,0:T(8,128)(2,1)S(1)}, u32[]{:S(2)}, u32[]{:S(2)}) collective-permute-start(bf16[128,1536]{1,0:T(8,128)(2,1)S(1)} %join2.1.refs_8_.refs_3_.refs_5_), channel_id=1, source_target_pairs={{0,2},{1,3},{2,0},{3,1},{4,6},{5,7},{6,4},{7,5},{8,10},{9,11},{10,... | collective-permute-start | bytes 1179656 | tf_op jit(solution)/shard_map/ppermute | solution.py:33
  59.0 2.2 %collective-permute-done.19.refs_7_ = bf16[96,1536]{1,0:T(8,128)(2,1)S(1)} collective-permute-done((bf16[96,1536]{1,0:T(8,128)(2,1)S(1)}, bf16[96,1536]{1,0:T(8,128)(2,1)S(1)}, u32[]{:S(2)}, u32[]{:S(2)}) %collective-permute-start.19) | collective-permute-done | bytes 294944 | tf_op jit(solution)/shard_map/ppermute | solution.py:33
  61.2 0.7 choose3.1
  62.2 5.5 %collective-permute-done.22.refs_1_ = bf16[64,1536]{1,0:T(8,128)(2,1)S(1)} collective-permute-done((bf16[64,1536]{1,0:T(8,128)(2,1)S(1)}, bf16[64,1536]{1,0:T(8,128)(2,1)S(1)}, u32[]{:S(2)}, u32[]{:S(2)}) %collective-permute-start.22) | collective-permute-done | bytes 196640 | tf_op jit(solution)/shard_map/ppermute | solution.py:33
  67.7 2.0 %collective-permute-start.24 = (bf16[128,1536]{1,0:T(8,128)(2,1)S(1)}, bf16[128,1536]{1,0:T(8,128)(2,1)S(1)}, u32[]{:S(2)}, u32[]{:S(2)}) collective-permute-start(bf16[128,1536]{1,0:T(8,128)(2,1)S(1)} %join3.1.refs_9_.refs_5_), channel_id=1, source_target_pairs={{0,2},{1,3},{2,0},{3,1},{4,6},{5,7},{6,4},{7,5},{8,10},{9,11},{10,... | collective-permute-start | bytes 1179656 | tf_op jit(solution)/shard_map/ppermute | solution.py:33
  69.7 2.0 %early.1 = (f32[256,1536]{1,0:T(8,128)S(1)}, bf16[128,1536]{1,0:T(8,128)(2,1)S(1)}, bf16[128,1536]{1,0:T(8,128)(2,1)S(1)}) custom-call(bf16[512,1536]{1,0:T(8,128)(2,1)S(1)} %pad_maximum_fusion.refs_0_, f32[512,1]{1,0:T(8,128)S(1)} %bitcast.45, bf16[512,32]{1,0:T(8,128)(2,1)S(1)} %pad_maximum_fusion.1.refs_13_.refs_2_, ...), custom_call_target="tpu_custom_call" | custom-call | flops 10000000000 | bytes 1 | tf_op jit(solution)/shard_map/early/pallas_call | solution.py:62
  71.8 0.5 collective-permute-start.27
  72.3 0.4 collective-permute-start.30
  72.8 2.8 %collective-permute-done.24.refs_6_ = bf16[128,1536]{1,0:T(8,128)(2,1)S(1)} collective-permute-done((bf16[128,1536]{1,0:T(8,128)(2,1)S(1)}, bf16[128,1536]{1,0:T(8,128)(2,1)S(1)}, u32[]{:S(2)}, u32[]{:S(2)}) %collective-permute-start.24) | collective-permute-done | bytes 393248 | tf_op jit(solution)/shard_map/ppermute | solution.py:33
  75.6 0.5 collective-permute-start.26
  76.1 1.2 %late2.1.refs_9_.refs_10_ = f32[256,1536]{1,0:T(8,128)S(1)} custom-call(bf16[256,1536]{1,0:T(8,128)(2,1)S(1)} %bitcast.37, f32[256,1]{1,0:T(8,128)S(1)} %copy.35.refs_4_.refs_8_.refs_1_, bf16[256,32]{1,0:T(8,128)(2,1)S(1)} %bitcast.42, f32[1,512]{1,0:T(1,128)S(1)} %get-tuple-element.111.refs_6_.refs_3_, s32[1,512]{1,0:T(1,128)S(1)} %get-tuple-element.113.refs_7_.refs_4_, ...), custom_call_target="tpu_custom_call" | custom-call | flops 1 | bytes 1 | tf_op jit(solution)/shard_map/late2/pallas_call | solution.py:62
  77.3 0.6 collective-permute-done.26.refs_8_
  77.9 2.3 %late3.1 = f32[256,1536]{1,0:T(8,128)} custom-call(bf16[256,1536]{1,0:T(8,128)(2,1)S(1)} %bitcast.38, f32[256,1]{1,0:T(8,128)S(1)} %copy.35.refs_4_.refs_8_.refs_1_, bf16[256,32]{1,0:T(8,128)(2,1)S(1)} %bitcast.43, f32[1,512]{1,0:T(1,128)S(1)} %get-tuple-element.110.refs_10_.refs_3_, s32[1,512]{1,0:T(1,128)S(1)} %get-tuple-element.112.refs_11_.refs_4_, ...), custom_call_target="tpu_custom_call" | custom-call | flops 1 | bytes 1 | tf_op jit(solution)/shard_map/late3/pallas_call | solution.py:62
  (137 shorter events, 4.9 us)
Async XLA Ops:
  0.1 1.1 %copy-start = (bf16[1,256,1536]{2,1,0:T(8,128)(2,1)S(1)}, bf16[1,256,1536]{2,1,0:T(8,128)(2,1)}, u32[]{:S(2)}) copy-start(bf16[1,256,1536]{2,1,0:T(8,128)(2,1)} %param.5) | copy-start | bytes 2359300
  1.2 6.4 %copy-start.5 = (s32[2,1,1,56]{3,2,1,0:T(1,128)S(1)}, s32[2,1,1,56]{3,2,1,0:T(1,128)}, u32[]{:S(2)}) copy-start(s32[2,1,1,56]{3,2,1,0:T(1,128)} %param.9) | copy-start | bytes 1348
  1.2 8.1 %copy-start.4 = (f32[1024]{0:T(1024)S(1)}, f32[1024]{0:T(1024)}, u32[]{:S(2)}) copy-start(f32[1024]{0:T(1024)} %param.7) | copy-start | bytes 12292
  1.2 8.4 %copy-start.2 = (s32[2,8]{1,0:T(2,128)S(1)}, s32[2,8]{1,0:T(2,128)}, u32[]{:S(2)}) copy-start(s32[2,8]{1,0:T(2,128)} %refs_1_.7) | copy-start | bytes 196
  1.2 8.6 %copy-start.3 = (f32[8]{0:T(128)S(1)}, f32[8]{0:T(128)}, u32[]{:S(2)}) copy-start(f32[8]{0:T(128)} %param.6) | copy-start | bytes 100
  1.9 14.5 %collective-permute-start.1 = (bf16[64,1536]{1,0:T(8,128)(2,1)S(1)}, bf16[64,1536]{1,0:T(8,128)(2,1)S(1)}, u32[]{:S(2)}, u32[]{:S(2)}) collective-permute-start(bf16[64,1536]{1,0:T(8,128)(2,1)S(1)} %get-tuple-element.84), channel_id=1, source_target_pairs={{0,8},{4,12},{8,0},{12,4},{16,24},{20,28},{24,16},{28,20},{1,9},{5... | collective-permute-start | bytes 589832 | tf_op jit(solution)/shard_map/ppermute | solution.py:33
  5.0 10.5 %collective-permute-start.2 = (bf16[32,1536]{1,0:T(8,128)(2,1)S(1)}, bf16[32,1536]{1,0:T(8,128)(2,1)S(1)}, u32[]{:S(2)}, u32[]{:S(2)}) collective-permute-start(bf16[32,1536]{1,0:T(8,128)(2,1)S(1)} %get-tuple-element.40), channel_id=1, source_target_pairs={{0,16},{4,20},{8,24},{12,28},{16,0},{20,4},{24,8},{28,12},{1,17},{... | collective-permute-start | bytes 294920 | tf_op jit(solution)/shard_map/ppermute | solution.py:33
  7.6 8.8 %collective-permute-start.3 = (bf16[32,1536]{1,0:T(8,128)(2,1)S(1)}, bf16[32,1536]{1,0:T(8,128)(2,1)S(1)}, u32[]{:S(2)}, u32[]{:S(2)}) collective-permute-start(bf16[32,1536]{1,0:T(8,128)(2,1)S(1)} %get-tuple-element.41), channel_id=1, source_target_pairs={{0,24},{4,28},{8,16},{12,20},{16,8},{20,12},{24,0},{28,4},{1,25},{... | collective-permute-start | bytes 294920 | tf_op jit(solution)/shard_map/ppermute | solution.py:33
  7.6 7.5 %collective-permute-start.4 = (s32[2,56]{1,0:T(2,128)S(1)}, s32[2,56]{1,0:T(2,128)S(1)}, u32[]{:S(2)}, u32[]{:S(2)}) collective-permute-start(s32[2,56]{1,0:T(2,128)S(1)} %bitcast.58), channel_id=1, source_target_pairs={{0,1},{1,0},{2,3},{3,2},{4,5},{5,4},{6,7},{7,6},{8,9},{9,8},{10,11... | collective-permute-start | bytes 1352 | tf_op jit(solution)/shard_map/ppermute | solution.py:33
  7.6 12.8 %collective-permute-start = (bf16[128,1536]{1,0:T(8,128)(2,1)S(1)}, bf16[128,1536]{1,0:T(8,128)(2,1)S(1)}, u32[]{:S(2)}, u32[]{:S(2)}) collective-permute-start(bf16[128,1536]{1,0:T(8,128)(2,1)S(1)} %get-tuple-element.38.refs_3_.refs_2_), channel_id=1, source_target_pairs={{0,4},{4,0},{8,12},{12,8},{16,20},{20,16},{24,28},{28,24},{1,5},{5... | collective-permute-start | bytes 1179656 | tf_op jit(solution)/shard_map/ppermute | solution.py:33
  16.4 3.9 %copy-start.1 = (bf16[1,256,1536]{2,1,0:T(8,128)(2,1)S(1)}, bf16[1,256,1536]{2,1,0:T(8,128)(2,1)}, u32[]{:S(2)}) copy-start(bf16[1,256,1536]{2,1,0:T(8,128)(2,1)} %param.5) | copy-start | bytes 2359300
  16.4 9.0 %collective-permute-start.5 = (bf16[96,1536]{1,0:T(8,128)(2,1)S(1)}, bf16[96,1536]{1,0:T(8,128)(2,1)S(1)}, u32[]{:S(2)}, u32[]{:S(2)}) collective-permute-start(bf16[96,1536]{1,0:T(8,128)(2,1)S(1)} %stack0.1.refs_8_), channel_id=1, source_target_pairs={{0,4},{4,0},{8,12},{12,8},{16,20},{20,16},{24,28},{28,24},{1,5},{5... | collective-permute-start | bytes 884744 | tf_op jit(solution)/shard_map/ppermute | solution.py:33
  18.0 9.1 %collective-permute-start.8 = (bf16[32,1536]{1,0:T(8,128)(2,1)S(1)}, bf16[32,1536]{1,0:T(8,128)(2,1)S(1)}, u32[]{:S(2)}, u32[]{:S(2)}) collective-permute-start(bf16[32,1536]{1,0:T(8,128)(2,1)S(1)} %get-tuple-element.48), channel_id=1, source_target_pairs={{0,24},{4,28},{8,16},{12,20},{16,8},{20,12},{24,0},{28,4},{1,25},{... | collective-permute-start | bytes 294920 | tf_op jit(solution)/shard_map/ppermute | solution.py:33
  19.7 8.5 %collective-permute-start.7 = (bf16[32,1536]{1,0:T(8,128)(2,1)S(1)}, bf16[32,1536]{1,0:T(8,128)(2,1)S(1)}, u32[]{:S(2)}, u32[]{:S(2)}) collective-permute-start(bf16[32,1536]{1,0:T(8,128)(2,1)S(1)} %get-tuple-element.46), channel_id=1, source_target_pairs={{0,16},{4,20},{8,24},{12,28},{16,0},{20,4},{24,8},{28,12},{1,17},{... | collective-permute-start | bytes 294920 | tf_op jit(solution)/shard_map/ppermute | solution.py:33
  20.4 12.7 %collective-permute-start.11 = (bf16[256,1536]{1,0:T(8,128)(2,1)S(1)}, bf16[256,1536]{1,0:T(8,128)(2,1)S(1)}, u32[]{:S(2)}, u32[]{:S(2)}) collective-permute-start(bf16[256,1536]{1,0:T(8,128)(2,1)S(1)} %bitcast.35), channel_id=1, source_target_pairs={{0,1},{1,0},{2,3},{3,2},{4,5},{5,4},{6,7},{7,6},{8,9},{9,8},{10,11... | collective-permute-start | bytes 2359304 | tf_op jit(solution)/shard_map/ppermute | solution.py:33
  26.2 6.3 %collective-permute-start.10 = (bf16[64,1536]{1,0:T(8,128)(2,1)S(1)}, bf16[64,1536]{1,0:T(8,128)(2,1)S(1)}, u32[]{:S(2)}, u32[]{:S(2)}) collective-permute-start(bf16[64,1536]{1,0:T(8,128)(2,1)S(1)} %get-tuple-element.49), channel_id=1, source_target_pairs={{0,8},{4,12},{8,0},{12,4},{16,24},{20,28},{24,16},{28,20},{1,9},{5... | collective-permute-start | bytes 589832 | tf_op jit(solution)/shard_map/ppermute | solution.py:33
  28.2 8.1 %collective-permute-start.9 = (bf16[96,1536]{1,0:T(8,128)(2,1)S(1)}, bf16[96,1536]{1,0:T(8,128)(2,1)S(1)}, u32[]{:S(2)}, u32[]{:S(2)}) collective-permute-start(bf16[96,1536]{1,0:T(8,128)(2,1)S(1)} %stack1.1.refs_2_), channel_id=1, source_target_pairs={{0,4},{4,0},{8,12},{12,8},{16,20},{20,16},{24,28},{28,24},{1,5},{5... | collective-permute-start | bytes 884744 | tf_op jit(solution)/shard_map/ppermute | solution.py:33
  29.5 10.1 %collective-permute-start.14 = (bf16[32,1536]{1,0:T(8,128)(2,1)S(1)}, bf16[32,1536]{1,0:T(8,128)(2,1)S(1)}, u32[]{:S(2)}, u32[]{:S(2)}) collective-permute-start(bf16[32,1536]{1,0:T(8,128)(2,1)S(1)} %get-tuple-element.56), channel_id=1, source_target_pairs={{0,16},{4,20},{8,24},{12,28},{16,0},{20,4},{24,8},{28,12},{1,17},{... | collective-permute-start | bytes 294920 | tf_op jit(solution)/shard_map/ppermute | solution.py:33
  32.3 7.8 %collective-permute-start.15 = (bf16[32,1536]{1,0:T(8,128)(2,1)S(1)}, bf16[32,1536]{1,0:T(8,128)(2,1)S(1)}, u32[]{:S(2)}, u32[]{:S(2)}) collective-permute-start(bf16[32,1536]{1,0:T(8,128)(2,1)S(1)} %get-tuple-element.58), channel_id=1, source_target_pairs={{0,24},{4,28},{8,16},{12,20},{16,8},{20,12},{24,0},{28,4},{1,25},{... | collective-permute-start | bytes 294920 | tf_op jit(solution)/shard_map/ppermute | solution.py:33
  32.5 10.1 %collective-permute-start.6 = (bf16[64,1536]{1,0:T(8,128)(2,1)S(1)}, bf16[64,1536]{1,0:T(8,128)(2,1)S(1)}, u32[]{:S(2)}, u32[]{:S(2)}) collective-permute-start(bf16[64,1536]{1,0:T(8,128)(2,1)S(1)} %get-tuple-element.43), channel_id=1, source_target_pairs={{0,8},{4,12},{8,0},{12,4},{16,24},{20,28},{24,16},{28,20},{1,9},{5... | collective-permute-start | bytes 589832 | tf_op jit(solution)/shard_map/ppermute | solution.py:33
  33.1 15.8 %collective-permute-start.18 = (bf16[128,1536]{1,0:T(8,128)(2,1)S(1)}, bf16[128,1536]{1,0:T(8,128)(2,1)S(1)}, u32[]{:S(2)}, u32[]{:S(2)}) collective-permute-start(bf16[128,1536]{1,0:T(8,128)(2,1)S(1)} %join0.1.refs_8_.refs_3_.refs_5_), channel_id=1, source_target_pairs={{0,2},{1,3},{2,0},{3,1},{4,6},{5,7},{6,4},{7,5},{8,10},{9,11},{10,... | collective-permute-start | bytes 1179656 | tf_op jit(solution)/shard_map/ppermute | solution.py:33
  37.1 11.8 %collective-permute-start.17 = (bf16[64,1536]{1,0:T(8,128)(2,1)S(1)}, bf16[64,1536]{1,0:T(8,128)(2,1)S(1)}, u32[]{:S(2)}, u32[]{:S(2)}) collective-permute-start(bf16[64,1536]{1,0:T(8,128)(2,1)S(1)} %get-tuple-element.59), channel_id=1, source_target_pairs={{0,8},{4,12},{8,0},{12,4},{16,24},{20,28},{24,16},{28,20},{1,9},{5... | collective-permute-start | bytes 589832 | tf_op jit(solution)/shard_map/ppermute | solution.py:33
  42.6 7.9 %collective-permute-start.16 = (bf16[96,1536]{1,0:T(8,128)(2,1)S(1)}, bf16[96,1536]{1,0:T(8,128)(2,1)S(1)}, u32[]{:S(2)}, u32[]{:S(2)}) collective-permute-start(bf16[96,1536]{1,0:T(8,128)(2,1)S(1)} %stack2.1.refs_2_), channel_id=1, source_target_pairs={{0,4},{4,0},{8,12},{12,8},{16,20},{20,16},{24,28},{28,24},{1,5},{5... | collective-permute-start | bytes 884744 | tf_op jit(solution)/shard_map/ppermute | solution.py:33
  44.8 7.1 %collective-permute-start.13 = (bf16[32,1536]{1,0:T(8,128)(2,1)S(1)}, bf16[32,1536]{1,0:T(8,128)(2,1)S(1)}, u32[]{:S(2)}, u32[]{:S(2)}) collective-permute-start(bf16[32,1536]{1,0:T(8,128)(2,1)S(1)} %get-tuple-element.54), channel_id=1, source_target_pairs={{0,24},{4,28},{8,16},{12,20},{16,8},{20,12},{24,0},{28,4},{1,25},{... | collective-permute-start | bytes 294920 | tf_op jit(solution)/shard_map/ppermute | solution.py:33
  48.9 5.5 %collective-permute-start.12 = (bf16[32,1536]{1,0:T(8,128)(2,1)S(1)}, bf16[32,1536]{1,0:T(8,128)(2,1)S(1)}, u32[]{:S(2)}, u32[]{:S(2)}) collective-permute-start(bf16[32,1536]{1,0:T(8,128)(2,1)S(1)} %get-tuple-element.52), channel_id=1, source_target_pairs={{0,16},{4,20},{8,24},{12,28},{16,0},{20,4},{24,8},{28,12},{1,17},{... | collective-permute-start | bytes 294920 | tf_op jit(solution)/shard_map/ppermute | solution.py:33
  48.9 8.4 %collective-permute-start.21 = (bf16[128,1536]{1,0:T(8,128)(2,1)S(1)}, bf16[128,1536]{1,0:T(8,128)(2,1)S(1)}, u32[]{:S(2)}, u32[]{:S(2)}) collective-permute-start(bf16[128,1536]{1,0:T(8,128)(2,1)S(1)} %join1.1.refs_8_.refs_3_.refs_7_), channel_id=1, source_target_pairs={{0,2},{1,3},{2,0},{3,1},{4,6},{5,7},{6,4},{7,5},{8,10},{9,11},{10,... | collective-permute-start | bytes 1179656 | tf_op jit(solution)/shard_map/ppermute | solution.py:33
  51.2 5.7 %collective-permute-start.20 = (bf16[64,1536]{1,0:T(8,128)(2,1)S(1)}, bf16[64,1536]{1,0:T(8,128)(2,1)S(1)}, u32[]{:S(2)}, u32[]{:S(2)}) collective-permute-start(bf16[64,1536]{1,0:T(8,128)(2,1)S(1)} %get-tuple-element.61), channel_id=1, source_target_pairs={{0,8},{4,12},{8,0},{12,4},{16,24},{20,28},{24,16},{28,20},{1,9},{5... | collective-permute-start | bytes 589832 | tf_op jit(solution)/shard_map/ppermute | solution.py:33
  54.4 6.8 %collective-permute-start.19 = (bf16[96,1536]{1,0:T(8,128)(2,1)S(1)}, bf16[96,1536]{1,0:T(8,128)(2,1)S(1)}, u32[]{:S(2)}, u32[]{:S(2)}) collective-permute-start(bf16[96,1536]{1,0:T(8,128)(2,1)S(1)} %stack3.1.refs_2_), channel_id=1, source_target_pairs={{0,4},{4,0},{8,12},{12,8},{16,20},{20,16},{24,28},{28,24},{1,5},{5... | collective-permute-start | bytes 884744 | tf_op jit(solution)/shard_map/ppermute | solution.py:33
  57.4 10.3 %collective-permute-start.23 = (bf16[128,1536]{1,0:T(8,128)(2,1)S(1)}, bf16[128,1536]{1,0:T(8,128)(2,1)S(1)}, u32[]{:S(2)}, u32[]{:S(2)}) collective-permute-start(bf16[128,1536]{1,0:T(8,128)(2,1)S(1)} %join2.1.refs_8_.refs_3_.refs_5_), channel_id=1, source_target_pairs={{0,2},{1,3},{2,0},{3,1},{4,6},{5,7},{6,4},{7,5},{8,10},{9,11},{10,... | collective-permute-start | bytes 1179656 | tf_op jit(solution)/shard_map/ppermute | solution.py:33
  62.0 5.7 %collective-permute-start.22 = (bf16[64,1536]{1,0:T(8,128)(2,1)S(1)}, bf16[64,1536]{1,0:T(8,128)(2,1)S(1)}, u32[]{:S(2)}, u32[]{:S(2)}) collective-permute-start(bf16[64,1536]{1,0:T(8,128)(2,1)S(1)} %get-tuple-element.63), channel_id=1, source_target_pairs={{0,8},{4,12},{8,0},{12,4},{16,24},{20,28},{24,16},{28,20},{1,9},{5... | collective-permute-start | bytes 589832 | tf_op jit(solution)/shard_map/ppermute | solution.py:33
  67.7 7.8 %collective-permute-start.24 = (bf16[128,1536]{1,0:T(8,128)(2,1)S(1)}, bf16[128,1536]{1,0:T(8,128)(2,1)S(1)}, u32[]{:S(2)}, u32[]{:S(2)}) collective-permute-start(bf16[128,1536]{1,0:T(8,128)(2,1)S(1)} %join3.1.refs_9_.refs_5_), channel_id=1, source_target_pairs={{0,2},{1,3},{2,0},{3,1},{4,6},{5,7},{6,4},{7,5},{8,10},{9,11},{10,... | collective-permute-start | bytes 1179656 | tf_op jit(solution)/shard_map/ppermute | solution.py:33
  71.7 3.9 %collective-permute-start.28 = (bf16[128,1536]{1,0:T(8,128)(2,1)S(1)}, bf16[128,1536]{1,0:T(8,128)(2,1)S(1)}, u32[]{:S(2)}, u32[]{:S(2)}) collective-permute-start(bf16[128,1536]{1,0:T(8,128)(2,1)S(1)} %collective-permute-done.23.refs_4_.refs_6_), channel_id=1, source_target_pairs={{0,1},{1,0},{2,3},{3,2},{4,5},{5,4},{6,7},{7,6},{8,9},{9,8},{10,11... | collective-permute-start | bytes 1179656 | tf_op jit(solution)/shard_map/ppermute | solution.py:33
  71.8 4.3 %collective-permute-start.27 = (bf16[128,1536]{1,0:T(8,128)(2,1)S(1)}, bf16[128,1536]{1,0:T(8,128)(2,1)S(1)}, u32[]{:S(2)}, u32[]{:S(2)}) collective-permute-start(bf16[128,1536]{1,0:T(8,128)(2,1)S(1)} %join2.1.refs_8_.refs_3_.refs_5_), channel_id=1, source_target_pairs={{0,1},{1,0},{2,3},{3,2},{4,5},{5,4},{6,7},{7,6},{8,9},{9,8},{10,11... | collective-permute-start | bytes 1179656 | tf_op jit(solution)/shard_map/ppermute | solution.py:33
  72.3 3.8 %collective-permute-start.29 = (bf16[128,1536]{1,0:T(8,128)(2,1)S(1)}, bf16[128,1536]{1,0:T(8,128)(2,1)S(1)}, u32[]{:S(2)}, u32[]{:S(2)}) collective-permute-start(bf16[128,1536]{1,0:T(8,128)(2,1)S(1)} %get-tuple-element.69), channel_id=1, source_target_pairs={{0,1},{1,0},{2,3},{3,2},{4,5},{5,4},{6,7},{7,6},{8,9},{9,8},{10,11... | collective-permute-start | bytes 1179656 | tf_op jit(solution)/shard_map/ppermute | solution.py:33
  72.3 3.8 %collective-permute-start.30 = (bf16[128,1536]{1,0:T(8,128)(2,1)S(1)}, bf16[128,1536]{1,0:T(8,128)(2,1)S(1)}, u32[]{:S(2)}, u32[]{:S(2)}) collective-permute-start(bf16[128,1536]{1,0:T(8,128)(2,1)S(1)} %get-tuple-element.70), channel_id=1, source_target_pairs={{0,1},{1,0},{2,3},{3,2},{4,5},{5,4},{6,7},{7,6},{8,9},{9,8},{10,11... | collective-permute-start | bytes 1179656 | tf_op jit(solution)/shard_map/ppermute | solution.py:33
  75.6 1.7 %collective-permute-start.25 = (bf16[128,1536]{1,0:T(8,128)(2,1)S(1)}, bf16[128,1536]{1,0:T(8,128)(2,1)S(1)}, u32[]{:S(2)}, u32[]{:S(2)}) collective-permute-start(bf16[128,1536]{1,0:T(8,128)(2,1)S(1)} %join3.1.refs_9_.refs_5_), channel_id=1, source_target_pairs={{0,1},{1,0},{2,3},{3,2},{4,5},{5,4},{6,7},{7,6},{8,9},{9,8},{10,11... | collective-permute-start | bytes 1179656 | tf_op jit(solution)/shard_map/ppermute | solution.py:33
  75.6 2.3 %collective-permute-start.26 = (bf16[128,1536]{1,0:T(8,128)(2,1)S(1)}, bf16[128,1536]{1,0:T(8,128)(2,1)S(1)}, u32[]{:S(2)}, u32[]{:S(2)}) collective-permute-start(bf16[128,1536]{1,0:T(8,128)(2,1)S(1)} %collective-permute-done.24.refs_6_), channel_id=1, source_target_pairs={{0,1},{1,0},{2,3},{3,2},{4,5},{5,4},{6,7},{7,6},{8,9},{9,8},{10,11... | collective-permute-start | bytes 1179656 | tf_op jit(solution)/shard_map/ppermute | solution.py:33

commit v5 on v4

--- a/solution.py
+++ b/solution.py
@@ -17,9 +17,10 @@
 EARLY = 2
 PGATE = "none"
 CGATE = True
-PCUTS = (128, 128)
+PCUTS = 2
+STREAM = 3
 PTYPE = jnp.bfloat16
-TAIL = 2
+TAIL = 1
 ORDER = "s"
 FL, FK, BY = 10**10, 1, 1
 FE = 10**10
@@ -52,7 +53,7 @@
     def __init__(self):
         self.last = []
 
-    def call(self, kernel, smem, arrays, outs, name, waits=(), weight=None):
+    def call(self, kernel, smem, arrays, outs, name, waits=(), weight=None, out_spec=VMEM, scratch=()):
         waits = [*self.last, *waits]
         count = len(smem) + len(arrays)
 
@@ -63,7 +64,8 @@
             run,
             out_shape=tuple(outs),
             in_specs=[SMEM] * len(smem) + [VMEM] * len(arrays) + [ANY] * len(waits),
-            out_specs=(VMEM,) * len(outs),
+            out_specs=(out_spec,) * len(outs),
+            scratch_shapes=list(scratch),
             compiler_params=pltpu.CompilerParams(vmem_limit_bytes=40 * 1024 * 1024),
             cost_estimate=pl.CostEstimate(flops=weight or FL, bytes_accessed=BY, transcendentals=0),
             name=name,
@@ -72,7 +74,7 @@
         return result
 
 
-def part_kernel(*refs, row_count, added):
+def part_kernel(*refs, row_count, added, stream):
     left_ref, gap_ref, table_ref, right_ref, key_ref = refs[:5]
     row_refs = refs[5 : 5 + row_count]
     added_refs = refs[5 + row_count : 5 + row_count + added]
@@ -87,6 +89,24 @@
     listed = jnp.dot(table_ref[...], one_hot, preferred_element_type=jnp.float32)
     gap = gap_ref[...] + right_ref[...]
     amplitude = jnp.where(listed > 0.5, scores / gap, 0.0).astype(jnp.bfloat16)
+    if stream:
+        out_ref, hold_ref, sems = out_refs
+        width = hold_ref.shape[-1]
+        copies = []
+        for i in range(hold_ref.shape[0]):
+            columns = slice(i * width, (i + 1) * width)
+            part = jnp.dot(amplitude, rows[:, columns], preferred_element_type=jnp.float32)
+            if added_refs:
+                part += added_refs[0][:, columns]
+                if len(added_refs) > 1:
+                    other = [r[:, columns].astype(jnp.float32) for r in added_refs[1:]]
+                    part += jnp.concatenate(other, axis=0)
+            hold_ref[i] = part
+            copies.append(pltpu.make_async_copy(hold_ref.at[i], out_ref.at[:, columns], sems.at[i]))
+            copies[-1].start()
+        for copy in copies:
+            copy.wait()
+        return
     part = jnp.dot(amplitude, rows, preferred_element_type=jnp.float32)
     if added_refs:
         part += added_refs[0][...]
@@ -191,14 +211,21 @@
     if early:
         sets[0] = (gap_left, table, column(right, x_order, early), column(key, x_order, early))
 
-    def add_part(left, sides, row_refs, added, outs, name, waits=()):
+    def add_part(left, sides, row_refs, added, outs, name, stream=0):
         arrays = [left, *sides, *row_refs, *added]
 
         def kernel(*refs):
-            part_kernel(*refs, row_count=len(row_refs), added=len(added))
+            part_kernel(*refs, row_count=len(row_refs), added=len(added), stream=stream)
 
         shapes = [jax.ShapeDtypeStruct((n, aux), PTYPE if i else jnp.float32) for i, n in enumerate(outs)]
-        return chain.call(kernel, [], arrays, shapes, name, waits, FE if name == "early" else FK)
+        weight = FE if name == "early" else FK
+        if stream:
+            scratch = [
+                pltpu.VMEM((stream, left.shape[0], aux // stream), jnp.float32),
+                pltpu.SemaphoreType.DMA((stream,)),
+            ]
+            return chain.call(kernel, [], arrays, shapes, name, (), weight, ANY, scratch)
+        return chain.call(kernel, [], arrays, shapes, name, (), weight)
 
     far_masks = [half ^ (m * unit) for m in range(places)]
     near_masks = [m * unit for m in range(1, places)]
@@ -303,7 +330,7 @@
     def add_early():
         lefts = jnp.concatenate([own, beside], axis=0)
         return add_part(
-            lefts, sets[0], [v for c in early for v in wide[c]], [], [slice_rows, *PCUTS], "early"
+            lefts, sets[0], [v for c in early for v in wide[c]], [], [slice_rows] + [slice_rows // PCUTS] * PCUTS, "early"
         )
 
     def full(c):
@@ -347,7 +374,8 @@
             others = [after(v, *chain.last) for v in others]
         added = [mine] + [send(v, "virt", 1) for v in others]
     for c in late:
-        added = add_part(own, sets[c], full(c), added, [slice_rows], f"late{c}")
+        stream = STREAM if c == late[-1] else 0
+        added = add_part(own, sets[c], full(c), added, [slice_rows], f"late{c}", stream)
     return added[0][None]
 
 

time: 80.3 us -> 79.5 us (0.990)
  waiting for transfers between devices: 28.2 us -> 29.3 us
  starting transfers between devices: 35.1 us -> 34.1 us
    ppermute x31 -> x29, waiting for transfers between devices: 28.2 us -> 29.3 us  [send(): lax.ppermute(value, axis, [(i, i ^ mask) for i in range(lax.axis_size(axi...]
    ppermute x31 -> x29, starting transfers between devices: 35.1 us -> 34.1 us  [send(): lax.ppermute(value, axis, [(i, i ^ mask) for i in range(lax.axis_size(axi...]
    pallas_call x16 -> x15, Pallas kernels: 9.27 us -> 8.73 us  [call(): pl.pallas_call(run, out_shape=tuple(outs), in_specs=[SMEM] * len(smem) +...]
    another operation x24 -> x20, local copies, waits for them, and re-layouts: 1.98 us -> 1.65 us  [column(): x[m, :, :, slice(*spans[c])].reshape(1, -1)]
  transfers between devices with their start and end apart: 31 -> 29, of which waited for: 14 -> 14; matrix products, arithmetic and copies ran while one was open for 7% -> 7% of each run, Pallas kernels for 8% -> 8%
where the time goes in v5:
time: 79.5 us; the launch traced here: 79.4 us
  starting transfers between devices  34.1 us (43%)
  waiting for transfers between devices  29.3 us (37%)
  Pallas kernels  8.73 us (11%)
  local copies, waits for them, and re-layouts  5.2 us (7%)
  other arithmetic  1.63 us (2%)
    ppermute x29, starting transfers between devices, send(): lax.ppermute(value, axis, [(i, i ^ mask) for i in range(lax.axis_size(axi...  34.1 us
    ppermute x29, waiting for transfers between devices, send(): lax.ppermute(value, axis, [(i, i ^ mask) for i in range(lax.axis_size(axi...  29.3 us
    pallas_call x15, Pallas kernels, call(): pl.pallas_call(run, out_shape=tuple(outs), in_specs=[SMEM] * len(smem) +...  8.73 us
    another operation x20, local copies, waits for them, and re-layouts, column(): x[m, :, :, slice(*spans[c])].reshape(1, -1)  1.65 us
  transfers between devices with their start and end apart: 29, of which 14 were waited for; matrix products, arithmetic and copies ran while one was open for 7% of the time, Pallas kernels for 8%

profile of v5, /device:TPU:0, one launch (start us, length us, event | category | flops | bytes accessed | tf_op | source)
XLA Modules:
  0.0 79.4 jit_solution(14685002351669120506)
XLA Ops:
  0.1 1.1 %copy-done = bf16[1,256,1536]{2,1,0:T(8,128)(2,1)S(1)} copy-done((bf16[1,256,1536]{2,1,0:T(8,128)(2,1)S(1)}, bf16[1,256,1536]{2,1,0:T(8,128)(2,1)}, u32[]{:S(2)}) %copy-start) | copy-done | bytes 786456
  1.2 0.7 cut.1
  1.9 3.1 %collective-permute-start.1 = (bf16[64,1536]{1,0:T(8,128)(2,1)S(1)}, bf16[64,1536]{1,0:T(8,128)(2,1)S(1)}, u32[]{:S(2)}, u32[]{:S(2)}) collective-permute-start(bf16[64,1536]{1,0:T(8,128)(2,1)S(1)} %get-tuple-element.80), channel_id=1, source_target_pairs={{0,8},{4,12},{8,0},{12,4},{16,24},{20,28},{24,16},{28,20},{1,9},{5... | collective-permute-start | bytes 589832 | tf_op jit(solution)/shard_map/ppermute | solution.py:34
  5.0 2.6 %collective-permute-start.2 = (bf16[32,1536]{1,0:T(8,128)(2,1)S(1)}, bf16[32,1536]{1,0:T(8,128)(2,1)S(1)}, u32[]{:S(2)}, u32[]{:S(2)}) collective-permute-start(bf16[32,1536]{1,0:T(8,128)(2,1)S(1)} %get-tuple-element.38), channel_id=1, source_target_pairs={{0,16},{4,20},{8,24},{12,28},{16,0},{20,4},{24,8},{28,12},{1,17},{... | collective-permute-start | bytes 294920 | tf_op jit(solution)/shard_map/ppermute | solution.py:34
  7.6 1.7 %collective-permute-start = (bf16[128,1536]{1,0:T(8,128)(2,1)S(1)}, bf16[128,1536]{1,0:T(8,128)(2,1)S(1)}, u32[]{:S(2)}, u32[]{:S(2)}) collective-permute-start(bf16[128,1536]{1,0:T(8,128)(2,1)S(1)} %get-tuple-element.36.refs_3_.refs_2_), channel_id=1, source_target_pairs={{0,4},{4,0},{8,12},{12,8},{16,20},{20,16},{24,28},{28,24},{1,5},{5... | collective-permute-start | bytes 1179656 | tf_op jit(solution)/shard_map/ppermute | solution.py:34
  10.8 0.2 fusion.5
  11.0 0.6 dynamic_slice.4
  11.6 0.6 gather_fusion
  13.4 0.7 fusion.3
  14.2 0.1 copy.31
  15.1 1.3 %collective-permute-done.3.refs_2_.refs_6_ = bf16[32,1536]{1,0:T(8,128)(2,1)S(1)} collective-permute-done((bf16[32,1536]{1,0:T(8,128)(2,1)S(1)}, bf16[32,1536]{1,0:T(8,128)(2,1)S(1)}, u32[]{:S(2)}, u32[]{:S(2)}) %collective-permute-start.3) | collective-permute-done | bytes 98336 | tf_op jit(solution)/shard_map/ppermute | solution.py:34
  16.4 1.6 %collective-permute-start.5 = (bf16[96,1536]{1,0:T(8,128)(2,1)S(1)}, bf16[96,1536]{1,0:T(8,128)(2,1)S(1)}, u32[]{:S(2)}, u32[]{:S(2)}) collective-permute-start(bf16[96,1536]{1,0:T(8,128)(2,1)S(1)} %stack0.1.refs_8_), channel_id=1, source_target_pairs={{0,4},{4,0},{8,12},{12,8},{16,20},{20,16},{24,28},{28,24},{1,5},{5... | collective-permute-start | bytes 884744 | tf_op jit(solution)/shard_map/ppermute | solution.py:34
  18.0 1.5 %collective-permute-start.8 = (bf16[32,1536]{1,0:T(8,128)(2,1)S(1)}, bf16[32,1536]{1,0:T(8,128)(2,1)S(1)}, u32[]{:S(2)}, u32[]{:S(2)}) collective-permute-start(bf16[32,1536]{1,0:T(8,128)(2,1)S(1)} %get-tuple-element.46), channel_id=1, source_target_pairs={{0,24},{4,28},{8,16},{12,20},{16,8},{20,12},{24,0},{28,4},{1,25},{... | collective-permute-start | bytes 294920 | tf_op jit(solution)/shard_map/ppermute | solution.py:34
  19.6 0.8 collective-permute-start.7
  20.4 5.1 %collective-permute-done.5.refs_7_ = bf16[96,1536]{1,0:T(8,128)(2,1)S(1)} collective-permute-done((bf16[96,1536]{1,0:T(8,128)(2,1)S(1)}, bf16[96,1536]{1,0:T(8,128)(2,1)S(1)}, u32[]{:S(2)}, u32[]{:S(2)}) %collective-permute-start.5) | collective-permute-done | bytes 294944 | tf_op jit(solution)/shard_map/ppermute | solution.py:34
  25.5 0.7 choose0.1
  26.2 1.0 %collective-permute-start.10 = (bf16[64,1536]{1,0:T(8,128)(2,1)S(1)}, bf16[64,1536]{1,0:T(8,128)(2,1)S(1)}, u32[]{:S(2)}, u32[]{:S(2)}) collective-permute-start(bf16[64,1536]{1,0:T(8,128)(2,1)S(1)} %get-tuple-element.47), channel_id=1, source_target_pairs={{0,8},{4,12},{8,0},{12,4},{16,24},{20,28},{24,16},{28,20},{1,9},{5... | collective-permute-start | bytes 589832 | tf_op jit(solution)/shard_map/ppermute | solution.py:34
  27.2 1.0 %collective-permute-done.7.refs_1_.refs_5_ = bf16[32,1536]{1,0:T(8,128)(2,1)S(1)} collective-permute-done((bf16[32,1536]{1,0:T(8,128)(2,1)S(1)}, bf16[32,1536]{1,0:T(8,128)(2,1)S(1)}, u32[]{:S(2)}, u32[]{:S(2)}) %collective-permute-start.7) | collective-permute-done | bytes 98336 | tf_op jit(solution)/shard_map/ppermute | solution.py:34
  28.2 0.9 %collective-permute-start.9 = (bf16[96,1536]{1,0:T(8,128)(2,1)S(1)}, bf16[96,1536]{1,0:T(8,128)(2,1)S(1)}, u32[]{:S(2)}, u32[]{:S(2)}) collective-permute-start(bf16[96,1536]{1,0:T(8,128)(2,1)S(1)} %stack1.1.refs_2_), channel_id=1, source_target_pairs={{0,4},{4,0},{8,12},{12,8},{16,20},{20,16},{24,28},{28,24},{1,5},{5... | collective-permute-start | bytes 884744 | tf_op jit(solution)/shard_map/ppermute | solution.py:34
  29.1 3.2 %collective-permute-start.14 = (bf16[32,1536]{1,0:T(8,128)(2,1)S(1)}, bf16[32,1536]{1,0:T(8,128)(2,1)S(1)}, u32[]{:S(2)}, u32[]{:S(2)}) collective-permute-start(bf16[32,1536]{1,0:T(8,128)(2,1)S(1)} %get-tuple-element.54), channel_id=1, source_target_pairs={{0,16},{4,20},{8,24},{12,28},{16,0},{20,4},{24,8},{28,12},{1,17},{... | collective-permute-start | bytes 294920 | tf_op jit(solution)/shard_map/ppermute | solution.py:34
  32.3 0.2 collective-permute-start.15
  32.5 0.6 collective-permute-start.6
  33.1 2.1 %collective-permute-start.18 = (bf16[128,1536]{1,0:T(8,128)(2,1)S(1)}, bf16[128,1536]{1,0:T(8,128)(2,1)S(1)}, u32[]{:S(2)}, u32[]{:S(2)}) collective-permute-start(bf16[128,1536]{1,0:T(8,128)(2,1)S(1)} %join0.1.refs_8_.refs_3_.refs_5_), channel_id=1, source_target_pairs={{0,2},{1,3},{2,0},{3,1},{4,6},{5,7},{6,4},{7,5},{8,10},{9,11},{10,... | collective-permute-start | bytes 1179656 | tf_op jit(solution)/shard_map/ppermute | solution.py:34
  35.3 1.0 %collective-permute-done.9.refs_7_ = bf16[96,1536]{1,0:T(8,128)(2,1)S(1)} collective-permute-done((bf16[96,1536]{1,0:T(8,128)(2,1)S(1)}, bf16[96,1536]{1,0:T(8,128)(2,1)S(1)}, u32[]{:S(2)}, u32[]{:S(2)}) %collective-permute-start.9) | collective-permute-done | bytes 294944 | tf_op jit(solution)/shard_map/ppermute | solution.py:34
  36.3 0.7 choose1.1
  37.0 1.1 %collective-permute-start.17 = (bf16[64,1536]{1,0:T(8,128)(2,1)S(1)}, bf16[64,1536]{1,0:T(8,128)(2,1)S(1)}, u32[]{:S(2)}, u32[]{:S(2)}) collective-permute-start(bf16[64,1536]{1,0:T(8,128)(2,1)S(1)} %get-tuple-element.57), channel_id=1, source_target_pairs={{0,8},{4,12},{8,0},{12,4},{16,24},{20,28},{24,16},{28,20},{1,9},{5... | collective-permute-start | bytes 589832 | tf_op jit(solution)/shard_map/ppermute | solution.py:34
  38.1 1.5 %collective-permute-done.14.refs_1_.refs_5_ = bf16[32,1536]{1,0:T(8,128)(2,1)S(1)} collective-permute-done((bf16[32,1536]{1,0:T(8,128)(2,1)S(1)}, bf16[32,1536]{1,0:T(8,128)(2,1)S(1)}, u32[]{:S(2)}, u32[]{:S(2)}) %collective-permute-start.14) | collective-permute-done | bytes 98336 | tf_op jit(solution)/shard_map/ppermute | solution.py:34
  39.6 0.5 collective-permute-done.15.refs_2_.refs_6_
  40.1 2.5 %collective-permute-done.6.refs_0_.refs_4_ = bf16[64,1536]{1,0:T(8,128)(2,1)S(1)} collective-permute-done((bf16[64,1536]{1,0:T(8,128)(2,1)S(1)}, bf16[64,1536]{1,0:T(8,128)(2,1)S(1)}, u32[]{:S(2)}, u32[]{:S(2)}) %collective-permute-start.6) | collective-permute-done | bytes 196640 | tf_op jit(solution)/shard_map/ppermute | solution.py:34
  42.6 2.1 %collective-permute-start.16 = (bf16[96,1536]{1,0:T(8,128)(2,1)S(1)}, bf16[96,1536]{1,0:T(8,128)(2,1)S(1)}, u32[]{:S(2)}, u32[]{:S(2)}) collective-permute-start(bf16[96,1536]{1,0:T(8,128)(2,1)S(1)} %stack2.1.refs_2_), channel_id=1, source_target_pairs={{0,4},{4,0},{8,12},{12,8},{16,20},{20,16},{24,28},{28,24},{1,5},{5... | collective-permute-start | bytes 884744 | tf_op jit(solution)/shard_map/ppermute | solution.py:34
  44.8 4.1 %collective-permute-start.13 = (bf16[32,1536]{1,0:T(8,128)(2,1)S(1)}, bf16[32,1536]{1,0:T(8,128)(2,1)S(1)}, u32[]{:S(2)}, u32[]{:S(2)}) collective-permute-start(bf16[32,1536]{1,0:T(8,128)(2,1)S(1)} %get-tuple-element.52), channel_id=1, source_target_pairs={{0,24},{4,28},{8,16},{12,20},{16,8},{20,12},{24,0},{28,4},{1,25},{... | collective-permute-start | bytes 294920 | tf_op jit(solution)/shard_map/ppermute | solution.py:34
  48.9 1.6 %collective-permute-start.21 = (bf16[128,1536]{1,0:T(8,128)(2,1)S(1)}, bf16[128,1536]{1,0:T(8,128)(2,1)S(1)}, u32[]{:S(2)}, u32[]{:S(2)}) collective-permute-start(bf16[128,1536]{1,0:T(8,128)(2,1)S(1)} %join1.1.refs_8_.refs_3_.refs_7_), channel_id=1, source_target_pairs={{0,2},{1,3},{2,0},{3,1},{4,6},{5,7},{6,4},{7,5},{8,10},{9,11},{10,... | collective-permute-start | bytes 1179656 | tf_op jit(solution)/shard_map/ppermute | solution.py:34
  50.5 0.7 choose2.1
  51.2 0.7 collective-permute-start.20
  52.0 2.4 %collective-permute-done.12.refs_1_.refs_5_ = bf16[32,1536]{1,0:T(8,128)(2,1)S(1)} collective-permute-done((bf16[32,1536]{1,0:T(8,128)(2,1)S(1)}, bf16[32,1536]{1,0:T(8,128)(2,1)S(1)}, u32[]{:S(2)}, u32[]{:S(2)}) %collective-permute-start.12) | collective-permute-done | bytes 98336 | tf_op jit(solution)/shard_map/ppermute | solution.py:34
  54.4 0.9 %collective-permute-start.19 = (bf16[96,1536]{1,0:T(8,128)(2,1)S(1)}, bf16[96,1536]{1,0:T(8,128)(2,1)S(1)}, u32[]{:S(2)}, u32[]{:S(2)}) collective-permute-start(bf16[96,1536]{1,0:T(8,128)(2,1)S(1)} %stack3.1.refs_2_), channel_id=1, source_target_pairs={{0,4},{4,0},{8,12},{12,8},{16,20},{20,16},{24,28},{28,24},{1,5},{5... | collective-permute-start | bytes 884744 | tf_op jit(solution)/shard_map/ppermute | solution.py:34
  55.4 1.6 %collective-permute-done.20.refs_1_ = bf16[64,1536]{1,0:T(8,128)(2,1)S(1)} collective-permute-done((bf16[64,1536]{1,0:T(8,128)(2,1)S(1)}, bf16[64,1536]{1,0:T(8,128)(2,1)S(1)}, u32[]{:S(2)}, u32[]{:S(2)}) %collective-permute-start.20) | collective-permute-done | bytes 196640 | tf_op jit(solution)/shard_map/ppermute | solution.py:34
  57.0 0.4 collective-permute-done.21.refs_4_.refs_8_
  57.4 1.6 %collective-permute-start.23 = (bf16[128,1536]{1,0:T(8,128)(2,1)S(1)}, bf16[128,1536]{1,0:T(8,128)(2,1)S(1)}, u32[]{:S(2)}, u32[]{:S(2)}) collective-permute-start(bf16[128,1536]{1,0:T(8,128)(2,1)S(1)} %join2.1.refs_8_.refs_3_.refs_9_), channel_id=1, source_target_pairs={{0,2},{1,3},{2,0},{3,1},{4,6},{5,7},{6,4},{7,5},{8,10},{9,11},{10,... | collective-permute-start | bytes 1179656 | tf_op jit(solution)/shard_map/ppermute | solution.py:34
  59.0 2.2 %collective-permute-done.19.refs_7_ = bf16[96,1536]{1,0:T(8,128)(2,1)S(1)} collective-permute-done((bf16[96,1536]{1,0:T(8,128)(2,1)S(1)}, bf16[96,1536]{1,0:T(8,128)(2,1)S(1)}, u32[]{:S(2)}, u32[]{:S(2)}) %collective-permute-start.19) | collective-permute-done | bytes 294944 | tf_op jit(solution)/shard_map/ppermute | solution.py:34
  61.2 0.7 choose3.1
  62.2 5.5 %collective-permute-done.22.refs_1_ = bf16[64,1536]{1,0:T(8,128)(2,1)S(1)} collective-permute-done((bf16[64,1536]{1,0:T(8,128)(2,1)S(1)}, bf16[64,1536]{1,0:T(8,128)(2,1)S(1)}, u32[]{:S(2)}, u32[]{:S(2)}) %collective-permute-start.22) | collective-permute-done | bytes 196640 | tf_op jit(solution)/shard_map/ppermute | solution.py:34
  67.7 2.0 %collective-permute-start.24 = (bf16[128,1536]{1,0:T(8,128)(2,1)S(1)}, bf16[128,1536]{1,0:T(8,128)(2,1)S(1)}, u32[]{:S(2)}, u32[]{:S(2)}) collective-permute-start(bf16[128,1536]{1,0:T(8,128)(2,1)S(1)} %join3.1.refs_11_.refs_5_), channel_id=1, source_target_pairs={{0,2},{1,3},{2,0},{3,1},{4,6},{5,7},{6,4},{7,5},{8,10},{9,11},{10,... | collective-permute-start | bytes 1179656 | tf_op jit(solution)/shard_map/ppermute | solution.py:34
  69.7 2.9 %early.1 = (f32[256,1536]{1,0:T(8,128)S(1)}, bf16[128,1536]{1,0:T(8,128)(2,1)S(1)}, bf16[128,1536]{1,0:T(8,128)(2,1)S(1)}) custom-call(bf16[512,1536]{1,0:T(8,128)(2,1)S(1)} %pad_maximum_fusion.refs_0_, f32[512,1]{1,0:T(8,128)S(1)} %bitcast.42, bf16[512,32]{1,0:T(8,128)(2,1)S(1)} %pad_maximum_fusion.1.refs_9_.refs_2_, ...), custom_call_target="tpu_custom_call" | custom-call | flops 10000000000 | bytes 1 | tf_op jit(solution)/shard_map/early/pallas_call | solution.py:63
  72.6 0.5 collective-permute-start.27
  73.2 2.3 %collective-permute-done.24.refs_6_ = bf16[128,1536]{1,0:T(8,128)(2,1)S(1)} collective-permute-done((bf16[128,1536]{1,0:T(8,128)(2,1)S(1)}, bf16[128,1536]{1,0:T(8,128)(2,1)S(1)}, u32[]{:S(2)}, u32[]{:S(2)}) %collective-permute-start.24) | collective-permute-done | bytes 393248 | tf_op jit(solution)/shard_map/ppermute | solution.py:34
  75.6 1.7 %collective-permute-done.26.refs_8_ = bf16[128,1536]{1,0:T(8,128)(2,1)S(1)} collective-permute-done((bf16[128,1536]{1,0:T(8,128)(2,1)S(1)}, bf16[128,1536]{1,0:T(8,128)(2,1)S(1)}, u32[]{:S(2)}, u32[]{:S(2)}) %collective-permute-start.26) | collective-permute-done | bytes 393248 | tf_op jit(solution)/shard_map/ppermute | solution.py:34
  77.3 2.1 %late3.1 = f32[256,1536]{1,0:T(8,128)} custom-call(bf16[256,1536]{1,0:T(8,128)(2,1)S(1)} %bitcast.37, f32[256,1]{1,0:T(8,128)S(1)} %copy.29.refs_4_.refs_1_, bf16[256,32]{1,0:T(8,128)(2,1)S(1)} %bitcast.40, f32[1,512]{1,0:T(1,128)S(1)} %get-tuple-element.102.refs_6_.refs_3_, s32[1,512]{1,0:T(1,128)S(1)} %get-tuple-element.104.refs_7_.refs_4_, ...), custom_call_target="tpu_custom_call" | custom-call | flops 1 | bytes 1 | tf_op jit(solution)/shard_map/late3/pallas_call | solution.py:63
  (124 shorter events, 4.0 us)
Async XLA Ops:
  0.1 1.1 %copy-start = (bf16[1,256,1536]{2,1,0:T(8,128)(2,1)S(1)}, bf16[1,256,1536]{2,1,0:T(8,128)(2,1)}, u32[]{:S(2)}) copy-start(bf16[1,256,1536]{2,1,0:T(8,128)(2,1)} %param.5) | copy-start | bytes 2359300
  1.2 6.4 %copy-start.5 = (s32[2,1,1,56]{3,2,1,0:T(1,128)S(1)}, s32[2,1,1,56]{3,2,1,0:T(1,128)}, u32[]{:S(2)}) copy-start(s32[2,1,1,56]{3,2,1,0:T(1,128)} %param.9) | copy-start | bytes 1348
  1.2 8.1 %copy-start.4 = (f32[1024]{0:T(1024)S(1)}, f32[1024]{0:T(1024)}, u32[]{:S(2)}) copy-start(f32[1024]{0:T(1024)} %param.7) | copy-start | bytes 12292
  1.2 9.5 %copy-start.2 = (s32[2,8]{1,0:T(2,128)S(1)}, s32[2,8]{1,0:T(2,128)}, u32[]{:S(2)}) copy-start(s32[2,8]{1,0:T(2,128)} %refs_1_.7) | copy-start | bytes 196
  1.2 9.8 %copy-start.3 = (f32[8]{0:T(128)S(1)}, f32[8]{0:T(128)}, u32[]{:S(2)}) copy-start(f32[8]{0:T(128)} %param.6) | copy-start | bytes 100
  1.9 14.5 %collective-permute-start.1 = (bf16[64,1536]{1,0:T(8,128)(2,1)S(1)}, bf16[64,1536]{1,0:T(8,128)(2,1)S(1)}, u32[]{:S(2)}, u32[]{:S(2)}) collective-permute-start(bf16[64,1536]{1,0:T(8,128)(2,1)S(1)} %get-tuple-element.80), channel_id=1, source_target_pairs={{0,8},{4,12},{8,0},{12,4},{16,24},{20,28},{24,16},{28,20},{1,9},{5... | collective-permute-start | bytes 589832 | tf_op jit(solution)/shard_map/ppermute | solution.py:34
  5.0 10.1 %collective-permute-start.2 = (bf16[32,1536]{1,0:T(8,128)(2,1)S(1)}, bf16[32,1536]{1,0:T(8,128)(2,1)S(1)}, u32[]{:S(2)}, u32[]{:S(2)}) collective-permute-start(bf16[32,1536]{1,0:T(8,128)(2,1)S(1)} %get-tuple-element.38), channel_id=1, source_target_pairs={{0,16},{4,20},{8,24},{12,28},{16,0},{20,4},{24,8},{28,12},{1,17},{... | collective-permute-start | bytes 294920 | tf_op jit(solution)/shard_map/ppermute | solution.py:34
  7.6 8.8 %collective-permute-start.3 = (bf16[32,1536]{1,0:T(8,128)(2,1)S(1)}, bf16[32,1536]{1,0:T(8,128)(2,1)S(1)}, u32[]{:S(2)}, u32[]{:S(2)}) collective-permute-start(bf16[32,1536]{1,0:T(8,128)(2,1)S(1)} %get-tuple-element.39), channel_id=1, source_target_pairs={{0,24},{4,28},{8,16},{12,20},{16,8},{20,12},{24,0},{28,4},{1,25},{... | collective-permute-start | bytes 294920 | tf_op jit(solution)/shard_map/ppermute | solution.py:34
  7.6 7.1 %collective-permute-start.4 = (s32[2,56]{1,0:T(2,128)S(1)}, s32[2,56]{1,0:T(2,128)S(1)}, u32[]{:S(2)}, u32[]{:S(2)}) collective-permute-start(s32[2,56]{1,0:T(2,128)S(1)} %bitcast.55), channel_id=1, source_target_pairs={{0,1},{1,0},{2,3},{3,2},{4,5},{5,4},{6,7},{7,6},{8,9},{9,8},{10,11... | collective-permute-start | bytes 1352 | tf_op jit(solution)/shard_map/ppermute | solution.py:34
  7.6 12.8 %collective-permute-start = (bf16[128,1536]{1,0:T(8,128)(2,1)S(1)}, bf16[128,1536]{1,0:T(8,128)(2,1)S(1)}, u32[]{:S(2)}, u32[]{:S(2)}) collective-permute-start(bf16[128,1536]{1,0:T(8,128)(2,1)S(1)} %get-tuple-element.36.refs_3_.refs_2_), channel_id=1, source_target_pairs={{0,4},{4,0},{8,12},{12,8},{16,20},{20,16},{24,28},{28,24},{1,5},{5... | collective-permute-start | bytes 1179656 | tf_op jit(solution)/shard_map/ppermute | solution.py:34
  16.4 3.9 %copy-start.1 = (bf16[1,256,1536]{2,1,0:T(8,128)(2,1)S(1)}, bf16[1,256,1536]{2,1,0:T(8,128)(2,1)}, u32[]{:S(2)}) copy-start(bf16[1,256,1536]{2,1,0:T(8,128)(2,1)} %param.5) | copy-start | bytes 2359300
  16.4 9.0 %collective-permute-start.5 = (bf16[96,1536]{1,0:T(8,128)(2,1)S(1)}, bf16[96,1536]{1,0:T(8,128)(2,1)S(1)}, u32[]{:S(2)}, u32[]{:S(2)}) collective-permute-start(bf16[96,1536]{1,0:T(8,128)(2,1)S(1)} %stack0.1.refs_8_), channel_id=1, source_target_pairs={{0,4},{4,0},{8,12},{12,8},{16,20},{20,16},{24,28},{28,24},{1,5},{5... | collective-permute-start | bytes 884744 | tf_op jit(solution)/shard_map/ppermute | solution.py:34
  18.0 9.1 %collective-permute-start.8 = (bf16[32,1536]{1,0:T(8,128)(2,1)S(1)}, bf16[32,1536]{1,0:T(8,128)(2,1)S(1)}, u32[]{:S(2)}, u32[]{:S(2)}) collective-permute-start(bf16[32,1536]{1,0:T(8,128)(2,1)S(1)} %get-tuple-element.46), channel_id=1, source_target_pairs={{0,24},{4,28},{8,16},{12,20},{16,8},{20,12},{24,0},{28,4},{1,25},{... | collective-permute-start | bytes 294920 | tf_op jit(solution)/shard_map/ppermute | solution.py:34
  19.6 8.6 %collective-permute-start.7 = (bf16[32,1536]{1,0:T(8,128)(2,1)S(1)}, bf16[32,1536]{1,0:T(8,128)(2,1)S(1)}, u32[]{:S(2)}, u32[]{:S(2)}) collective-permute-start(bf16[32,1536]{1,0:T(8,128)(2,1)S(1)} %get-tuple-element.44), channel_id=1, source_target_pairs={{0,16},{4,20},{8,24},{12,28},{16,0},{20,4},{24,8},{28,12},{1,17},{... | collective-permute-start | bytes 294920 | tf_op jit(solution)/shard_map/ppermute | solution.py:34
  20.4 12.7 %collective-permute-start.11 = (bf16[256,1536]{1,0:T(8,128)(2,1)S(1)}, bf16[256,1536]{1,0:T(8,128)(2,1)S(1)}, u32[]{:S(2)}, u32[]{:S(2)}) collective-permute-start(bf16[256,1536]{1,0:T(8,128)(2,1)S(1)} %bitcast.35), channel_id=1, source_target_pairs={{0,1},{1,0},{2,3},{3,2},{4,5},{5,4},{6,7},{7,6},{8,9},{9,8},{10,11... | collective-permute-start | bytes 2359304 | tf_op jit(solution)/shard_map/ppermute | solution.py:34
  26.2 6.3 %collective-permute-start.10 = (bf16[64,1536]{1,0:T(8,128)(2,1)S(1)}, bf16[64,1536]{1,0:T(8,128)(2,1)S(1)}, u32[]{:S(2)}, u32[]{:S(2)}) collective-permute-start(bf16[64,1536]{1,0:T(8,128)(2,1)S(1)} %get-tuple-element.47), channel_id=1, source_target_pairs={{0,8},{4,12},{8,0},{12,4},{16,24},{20,28},{24,16},{28,20},{1,9},{5... | collective-permute-start | bytes 589832 | tf_op jit(solution)/shard_map/ppermute | solution.py:34
  28.2 8.1 %collective-permute-start.9 = (bf16[96,1536]{1,0:T(8,128)(2,1)S(1)}, bf16[96,1536]{1,0:T(8,128)(2,1)S(1)}, u32[]{:S(2)}, u32[]{:S(2)}) collective-permute-start(bf16[96,1536]{1,0:T(8,128)(2,1)S(1)} %stack1.1.refs_2_), channel_id=1, source_target_pairs={{0,4},{4,0},{8,12},{12,8},{16,20},{20,16},{24,28},{28,24},{1,5},{5... | collective-permute-start | bytes 884744 | tf_op jit(solution)/shard_map/ppermute | solution.py:34
  29.1 10.5 %collective-permute-start.14 = (bf16[32,1536]{1,0:T(8,128)(2,1)S(1)}, bf16[32,1536]{1,0:T(8,128)(2,1)S(1)}, u32[]{:S(2)}, u32[]{:S(2)}) collective-permute-start(bf16[32,1536]{1,0:T(8,128)(2,1)S(1)} %get-tuple-element.54), channel_id=1, source_target_pairs={{0,16},{4,20},{8,24},{12,28},{16,0},{20,4},{24,8},{28,12},{1,17},{... | collective-permute-start | bytes 294920 | tf_op jit(solution)/shard_map/ppermute | solution.py:34
  32.3 7.8 %collective-permute-start.15 = (bf16[32,1536]{1,0:T(8,128)(2,1)S(1)}, bf16[32,1536]{1,0:T(8,128)(2,1)S(1)}, u32[]{:S(2)}, u32[]{:S(2)}) collective-permute-start(bf16[32,1536]{1,0:T(8,128)(2,1)S(1)} %get-tuple-element.56), channel_id=1, source_target_pairs={{0,24},{4,28},{8,16},{12,20},{16,8},{20,12},{24,0},{28,4},{1,25},{... | collective-permute-start | bytes 294920 | tf_op jit(solution)/shard_map/ppermute | solution.py:34
  32.5 10.1 %collective-permute-start.6 = (bf16[64,1536]{1,0:T(8,128)(2,1)S(1)}, bf16[64,1536]{1,0:T(8,128)(2,1)S(1)}, u32[]{:S(2)}, u32[]{:S(2)}) collective-permute-start(bf16[64,1536]{1,0:T(8,128)(2,1)S(1)} %get-tuple-element.41), channel_id=1, source_target_pairs={{0,8},{4,12},{8,0},{12,4},{16,24},{20,28},{24,16},{28,20},{1,9},{5... | collective-permute-start | bytes 589832 | tf_op jit(solution)/shard_map/ppermute | solution.py:34
  33.1 15.8 %collective-permute-start.18 = (bf16[128,1536]{1,0:T(8,128)(2,1)S(1)}, bf16[128,1536]{1,0:T(8,128)(2,1)S(1)}, u32[]{:S(2)}, u32[]{:S(2)}) collective-permute-start(bf16[128,1536]{1,0:T(8,128)(2,1)S(1)} %join0.1.refs_8_.refs_3_.refs_5_), channel_id=1, source_target_pairs={{0,2},{1,3},{2,0},{3,1},{4,6},{5,7},{6,4},{7,5},{8,10},{9,11},{10,... | collective-permute-start | bytes 1179656 | tf_op jit(solution)/shard_map/ppermute | solution.py:34
  37.0 11.8 %collective-permute-start.17 = (bf16[64,1536]{1,0:T(8,128)(2,1)S(1)}, bf16[64,1536]{1,0:T(8,128)(2,1)S(1)}, u32[]{:S(2)}, u32[]{:S(2)}) collective-permute-start(bf16[64,1536]{1,0:T(8,128)(2,1)S(1)} %get-tuple-element.57), channel_id=1, source_target_pairs={{0,8},{4,12},{8,0},{12,4},{16,24},{20,28},{24,16},{28,20},{1,9},{5... | collective-permute-start | bytes 589832 | tf_op jit(solution)/shard_map/ppermute | solution.py:34
  42.6 7.8 %collective-permute-start.16 = (bf16[96,1536]{1,0:T(8,128)(2,1)S(1)}, bf16[96,1536]{1,0:T(8,128)(2,1)S(1)}, u32[]{:S(2)}, u32[]{:S(2)}) collective-permute-start(bf16[96,1536]{1,0:T(8,128)(2,1)S(1)} %stack2.1.refs_2_), channel_id=1, source_target_pairs={{0,4},{4,0},{8,12},{12,8},{16,20},{20,16},{24,28},{28,24},{1,5},{5... | collective-permute-start | bytes 884744 | tf_op jit(solution)/shard_map/ppermute | solution.py:34
  44.8 7.2 %collective-permute-start.13 = (bf16[32,1536]{1,0:T(8,128)(2,1)S(1)}, bf16[32,1536]{1,0:T(8,128)(2,1)S(1)}, u32[]{:S(2)}, u32[]{:S(2)}) collective-permute-start(bf16[32,1536]{1,0:T(8,128)(2,1)S(1)} %get-tuple-element.52), channel_id=1, source_target_pairs={{0,24},{4,28},{8,16},{12,20},{16,8},{20,12},{24,0},{28,4},{1,25},{... | collective-permute-start | bytes 294920 | tf_op jit(solution)/shard_map/ppermute | solution.py:34
  48.9 5.5 %collective-permute-start.12 = (bf16[32,1536]{1,0:T(8,128)(2,1)S(1)}, bf16[32,1536]{1,0:T(8,128)(2,1)S(1)}, u32[]{:S(2)}, u32[]{:S(2)}) collective-permute-start(bf16[32,1536]{1,0:T(8,128)(2,1)S(1)} %get-tuple-element.50), channel_id=1, source_target_pairs={{0,16},{4,20},{8,24},{12,28},{16,0},{20,4},{24,8},{28,12},{1,17},{... | collective-permute-start | bytes 294920 | tf_op jit(solution)/shard_map/ppermute | solution.py:34
  48.9 8.4 %collective-permute-start.21 = (bf16[128,1536]{1,0:T(8,128)(2,1)S(1)}, bf16[128,1536]{1,0:T(8,128)(2,1)S(1)}, u32[]{:S(2)}, u32[]{:S(2)}) collective-permute-start(bf16[128,1536]{1,0:T(8,128)(2,1)S(1)} %join1.1.refs_8_.refs_3_.refs_7_), channel_id=1, source_target_pairs={{0,2},{1,3},{2,0},{3,1},{4,6},{5,7},{6,4},{7,5},{8,10},{9,11},{10,... | collective-permute-start | bytes 1179656 | tf_op jit(solution)/shard_map/ppermute | solution.py:34
  51.2 5.7 %collective-permute-start.20 = (bf16[64,1536]{1,0:T(8,128)(2,1)S(1)}, bf16[64,1536]{1,0:T(8,128)(2,1)S(1)}, u32[]{:S(2)}, u32[]{:S(2)}) collective-permute-start(bf16[64,1536]{1,0:T(8,128)(2,1)S(1)} %get-tuple-element.59), channel_id=1, source_target_pairs={{0,8},{4,12},{8,0},{12,4},{16,24},{20,28},{24,16},{28,20},{1,9},{5... | collective-permute-start | bytes 589832 | tf_op jit(solution)/shard_map/ppermute | solution.py:34
  54.4 6.8 %collective-permute-start.19 = (bf16[96,1536]{1,0:T(8,128)(2,1)S(1)}, bf16[96,1536]{1,0:T(8,128)(2,1)S(1)}, u32[]{:S(2)}, u32[]{:S(2)}) collective-permute-start(bf16[96,1536]{1,0:T(8,128)(2,1)S(1)} %stack3.1.refs_2_), channel_id=1, source_target_pairs={{0,4},{4,0},{8,12},{12,8},{16,20},{20,16},{24,28},{28,24},{1,5},{5... | collective-permute-start | bytes 884744 | tf_op jit(solution)/shard_map/ppermute | solution.py:34
  57.4 10.3 %collective-permute-start.23 = (bf16[128,1536]{1,0:T(8,128)(2,1)S(1)}, bf16[128,1536]{1,0:T(8,128)(2,1)S(1)}, u32[]{:S(2)}, u32[]{:S(2)}) collective-permute-start(bf16[128,1536]{1,0:T(8,128)(2,1)S(1)} %join2.1.refs_8_.refs_3_.refs_9_), channel_id=1, source_target_pairs={{0,2},{1,3},{2,0},{3,1},{4,6},{5,7},{6,4},{7,5},{8,10},{9,11},{10,... | collective-permute-start | bytes 1179656 | tf_op jit(solution)/shard_map/ppermute | solution.py:34
  62.0 5.7 %collective-permute-start.22 = (bf16[64,1536]{1,0:T(8,128)(2,1)S(1)}, bf16[64,1536]{1,0:T(8,128)(2,1)S(1)}, u32[]{:S(2)}, u32[]{:S(2)}) collective-permute-start(bf16[64,1536]{1,0:T(8,128)(2,1)S(1)} %get-tuple-element.61), channel_id=1, source_target_pairs={{0,8},{4,12},{8,0},{12,4},{16,24},{20,28},{24,16},{28,20},{1,9},{5... | collective-permute-start | bytes 589832 | tf_op jit(solution)/shard_map/ppermute | solution.py:34
  67.7 7.8 %collective-permute-start.24 = (bf16[128,1536]{1,0:T(8,128)(2,1)S(1)}, bf16[128,1536]{1,0:T(8,128)(2,1)S(1)}, u32[]{:S(2)}, u32[]{:S(2)}) collective-permute-start(bf16[128,1536]{1,0:T(8,128)(2,1)S(1)} %join3.1.refs_11_.refs_5_), channel_id=1, source_target_pairs={{0,2},{1,3},{2,0},{3,1},{4,6},{5,7},{6,4},{7,5},{8,10},{9,11},{10,... | collective-permute-start | bytes 1179656 | tf_op jit(solution)/shard_map/ppermute | solution.py:34
  72.6 3.0 %collective-permute-start.25 = (bf16[128,1536]{1,0:T(8,128)(2,1)S(1)}, bf16[128,1536]{1,0:T(8,128)(2,1)S(1)}, u32[]{:S(2)}, u32[]{:S(2)}) collective-permute-start(bf16[128,1536]{1,0:T(8,128)(2,1)S(1)} %join3.1.refs_11_.refs_5_), channel_id=1, source_target_pairs={{0,1},{1,0},{2,3},{3,2},{4,5},{5,4},{6,7},{7,6},{8,9},{9,8},{10,11... | collective-permute-start | bytes 1179656 | tf_op jit(solution)/shard_map/ppermute | solution.py:34
  72.6 2.9 %collective-permute-start.27 = (bf16[128,1536]{1,0:T(8,128)(2,1)S(1)}, bf16[128,1536]{1,0:T(8,128)(2,1)S(1)}, u32[]{:S(2)}, u32[]{:S(2)}) collective-permute-start(bf16[128,1536]{1,0:T(8,128)(2,1)S(1)} %get-tuple-element.65), channel_id=1, source_target_pairs={{0,1},{1,0},{2,3},{3,2},{4,5},{5,4},{6,7},{7,6},{8,9},{9,8},{10,11... | collective-permute-start | bytes 1179656 | tf_op jit(solution)/shard_map/ppermute | solution.py:34
  73.1 2.4 %collective-permute-start.28 = (bf16[128,1536]{1,0:T(8,128)(2,1)S(1)}, bf16[128,1536]{1,0:T(8,128)(2,1)S(1)}, u32[]{:S(2)}, u32[]{:S(2)}) collective-permute-start(bf16[128,1536]{1,0:T(8,128)(2,1)S(1)} %get-tuple-element.66), channel_id=1, source_target_pairs={{0,1},{1,0},{2,3},{3,2},{4,5},{5,4},{6,7},{7,6},{8,9},{9,8},{10,11... | collective-permute-start | bytes 1179656 | tf_op jit(solution)/shard_map/ppermute | solution.py:34
  75.6 1.7 %collective-permute-start.26 = (bf16[128,1536]{1,0:T(8,128)(2,1)S(1)}, bf16[128,1536]{1,0:T(8,128)(2,1)S(1)}, u32[]{:S(2)}, u32[]{:S(2)}) collective-permute-start(bf16[128,1536]{1,0:T(8,128)(2,1)S(1)} %collective-permute-done.24.refs_6_), channel_id=1, source_target_pairs={{0,1},{1,0},{2,3},{3,2},{4,5},{5,4},{6,7},{7,6},{8,9},{9,8},{10,11... | collective-permute-start | bytes 1179656 | tf_op jit(solution)/shard_map/ppermute | solution.py:34

commit v6 on v5

--- a/solution.py
+++ b/solution.py
@@ -19,7 +19,7 @@
 CGATE = True
 PCUTS = 2
 STREAM = 3
-PTYPE = jnp.bfloat16
+PTYPE = jnp.float32
 TAIL = 1
 ORDER = "s"
 FL, FK, BY = 10**10, 1, 1

time: 79.5 us -> 79.5 us (level)
  transfers between devices with their start and end apart: 29 -> 29, of which waited for: 14 -> 15; matrix products, arithmetic and copies ran while one was open for 7% -> 7% of each run, Pallas kernels for 8% -> 8%
where the time goes in v6:
time: 79.5 us; the launch traced here: 79.4 us
  starting transfers between devices  34.1 us (43%)
  waiting for transfers between devices  29.3 us (37%)
  Pallas kernels  8.73 us (11%)
  local copies, waits for them, and re-layouts  5.2 us (7%)
  other arithmetic  1.63 us (2%)
    ppermute x29, starting transfers between devices, send(): lax.ppermute(value, axis, [(i, i ^ mask) for i in range(lax.axis_size(axi...  34.1 us
    ppermute x29, waiting for transfers between devices, send(): lax.ppermute(value, axis, [(i, i ^ mask) for i in range(lax.axis_size(axi...  29.3 us
    pallas_call x15, Pallas kernels, call(): pl.pallas_call(run, out_shape=tuple(outs), in_specs=[SMEM] * len(smem) +...  8.73 us
    another operation x20, local copies, waits for them, and re-layouts, column(): x[m, :, :, slice(*spans[c])].reshape(1, -1)  1.65 us
  transfers between devices with their start and end apart: 29, of which 15 were waited for; matrix products, arithmetic and copies ran while one was open for 7% of the time, Pallas kernels for 8%

profile of v6, /device:TPU:0, one launch (start us, length us, event | category | flops | bytes accessed | tf_op | source)
XLA Modules:
  0.0 79.4 jit_solution(18219509690775254667)
XLA Ops:
  0.1 1.1 %copy-done = bf16[1,256,1536]{2,1,0:T(8,128)(2,1)S(1)} copy-done((bf16[1,256,1536]{2,1,0:T(8,128)(2,1)S(1)}, bf16[1,256,1536]{2,1,0:T(8,128)(2,1)}, u32[]{:S(2)}) %copy-start) | copy-done | bytes 786456
  1.2 0.7 cut.1
  1.9 3.1 %collective-permute-start.1 = (bf16[64,1536]{1,0:T(8,128)(2,1)S(1)}, bf16[64,1536]{1,0:T(8,128)(2,1)S(1)}, u32[]{:S(2)}, u32[]{:S(2)}) collective-permute-start(bf16[64,1536]{1,0:T(8,128)(2,1)S(1)} %get-tuple-element.80), channel_id=1, source_target_pairs={{0,8},{4,12},{8,0},{12,4},{16,24},{20,28},{24,16},{28,20},{1,9},{5... | collective-permute-start | bytes 589832 | tf_op jit(solution)/shard_map/ppermute | solution.py:34
  5.0 2.6 %collective-permute-start.2 = (bf16[32,1536]{1,0:T(8,128)(2,1)S(1)}, bf16[32,1536]{1,0:T(8,128)(2,1)S(1)}, u32[]{:S(2)}, u32[]{:S(2)}) collective-permute-start(bf16[32,1536]{1,0:T(8,128)(2,1)S(1)} %get-tuple-element.38), channel_id=1, source_target_pairs={{0,16},{4,20},{8,24},{12,28},{16,0},{20,4},{24,8},{28,12},{1,17},{... | collective-permute-start | bytes 294920 | tf_op jit(solution)/shard_map/ppermute | solution.py:34
  7.6 1.7 %collective-permute-start = (bf16[128,1536]{1,0:T(8,128)(2,1)S(1)}, bf16[128,1536]{1,0:T(8,128)(2,1)S(1)}, u32[]{:S(2)}, u32[]{:S(2)}) collective-permute-start(bf16[128,1536]{1,0:T(8,128)(2,1)S(1)} %get-tuple-element.36.refs_3_.refs_2_), channel_id=1, source_target_pairs={{0,4},{4,0},{8,12},{12,8},{16,20},{20,16},{24,28},{28,24},{1,5},{5... | collective-permute-start | bytes 1179656 | tf_op jit(solution)/shard_map/ppermute | solution.py:34
  10.8 0.2 fusion.5
  11.0 0.6 dynamic_slice.4
  11.6 0.6 gather_fusion
  13.4 0.7 fusion.3
  15.1 1.3 %collective-permute-done.3.refs_2_.refs_6_ = bf16[32,1536]{1,0:T(8,128)(2,1)S(1)} collective-permute-done((bf16[32,1536]{1,0:T(8,128)(2,1)S(1)}, bf16[32,1536]{1,0:T(8,128)(2,1)S(1)}, u32[]{:S(2)}, u32[]{:S(2)}) %collective-permute-start.3) | collective-permute-done | bytes 98336 | tf_op jit(solution)/shard_map/ppermute | solution.py:34
  16.4 1.6 %collective-permute-start.5 = (bf16[96,1536]{1,0:T(8,128)(2,1)S(1)}, bf16[96,1536]{1,0:T(8,128)(2,1)S(1)}, u32[]{:S(2)}, u32[]{:S(2)}) collective-permute-start(bf16[96,1536]{1,0:T(8,128)(2,1)S(1)} %stack0.1.refs_8_), channel_id=1, source_target_pairs={{0,4},{4,0},{8,12},{12,8},{16,20},{20,16},{24,28},{28,24},{1,5},{5... | collective-permute-start | bytes 884744 | tf_op jit(solution)/shard_map/ppermute | solution.py:34
  18.0 1.5 %collective-permute-start.8 = (bf16[32,1536]{1,0:T(8,128)(2,1)S(1)}, bf16[32,1536]{1,0:T(8,128)(2,1)S(1)}, u32[]{:S(2)}, u32[]{:S(2)}) collective-permute-start(bf16[32,1536]{1,0:T(8,128)(2,1)S(1)} %get-tuple-element.46), channel_id=1, source_target_pairs={{0,24},{4,28},{8,16},{12,20},{16,8},{20,12},{24,0},{28,4},{1,25},{... | collective-permute-start | bytes 294920 | tf_op jit(solution)/shard_map/ppermute | solution.py:34
  19.6 0.8 collective-permute-start.7
  20.4 5.1 %collective-permute-done.5.refs_7_ = bf16[96,1536]{1,0:T(8,128)(2,1)S(1)} collective-permute-done((bf16[96,1536]{1,0:T(8,128)(2,1)S(1)}, bf16[96,1536]{1,0:T(8,128)(2,1)S(1)}, u32[]{:S(2)}, u32[]{:S(2)}) %collective-permute-start.5) | collective-permute-done | bytes 294944 | tf_op jit(solution)/shard_map/ppermute | solution.py:34
  25.5 0.7 choose0.1
  26.2 1.0 %collective-permute-start.10 = (bf16[64,1536]{1,0:T(8,128)(2,1)S(1)}, bf16[64,1536]{1,0:T(8,128)(2,1)S(1)}, u32[]{:S(2)}, u32[]{:S(2)}) collective-permute-start(bf16[64,1536]{1,0:T(8,128)(2,1)S(1)} %get-tuple-element.47), channel_id=1, source_target_pairs={{0,8},{4,12},{8,0},{12,4},{16,24},{20,28},{24,16},{28,20},{1,9},{5... | collective-permute-start | bytes 589832 | tf_op jit(solution)/shard_map/ppermute | solution.py:34
  27.2 1.0 %collective-permute-done.7.refs_1_.refs_5_ = bf16[32,1536]{1,0:T(8,128)(2,1)S(1)} collective-permute-done((bf16[32,1536]{1,0:T(8,128)(2,1)S(1)}, bf16[32,1536]{1,0:T(8,128)(2,1)S(1)}, u32[]{:S(2)}, u32[]{:S(2)}) %collective-permute-start.7) | collective-permute-done | bytes 98336 | tf_op jit(solution)/shard_map/ppermute | solution.py:34
  28.2 0.9 %collective-permute-start.9 = (bf16[96,1536]{1,0:T(8,128)(2,1)S(1)}, bf16[96,1536]{1,0:T(8,128)(2,1)S(1)}, u32[]{:S(2)}, u32[]{:S(2)}) collective-permute-start(bf16[96,1536]{1,0:T(8,128)(2,1)S(1)} %stack1.1.refs_2_), channel_id=1, source_target_pairs={{0,4},{4,0},{8,12},{12,8},{16,20},{20,16},{24,28},{28,24},{1,5},{5... | collective-permute-start | bytes 884744 | tf_op jit(solution)/shard_map/ppermute | solution.py:34
  29.1 3.2 %collective-permute-start.14 = (bf16[32,1536]{1,0:T(8,128)(2,1)S(1)}, bf16[32,1536]{1,0:T(8,128)(2,1)S(1)}, u32[]{:S(2)}, u32[]{:S(2)}) collective-permute-start(bf16[32,1536]{1,0:T(8,128)(2,1)S(1)} %get-tuple-element.54), channel_id=1, source_target_pairs={{0,16},{4,20},{8,24},{12,28},{16,0},{20,4},{24,8},{28,12},{1,17},{... | collective-permute-start | bytes 294920 | tf_op jit(solution)/shard_map/ppermute | solution.py:34
  32.3 0.2 collective-permute-start.15
  32.5 0.6 collective-permute-start.6
  33.1 2.1 %collective-permute-start.18 = (bf16[128,1536]{1,0:T(8,128)(2,1)S(1)}, bf16[128,1536]{1,0:T(8,128)(2,1)S(1)}, u32[]{:S(2)}, u32[]{:S(2)}) collective-permute-start(bf16[128,1536]{1,0:T(8,128)(2,1)S(1)} %join0.1.refs_8_.refs_3_.refs_5_), channel_id=1, source_target_pairs={{0,2},{1,3},{2,0},{3,1},{4,6},{5,7},{6,4},{7,5},{8,10},{9,11},{10,... | collective-permute-start | bytes 1179656 | tf_op jit(solution)/shard_map/ppermute | solution.py:34
  35.3 1.0 %collective-permute-done.9.refs_7_ = bf16[96,1536]{1,0:T(8,128)(2,1)S(1)} collective-permute-done((bf16[96,1536]{1,0:T(8,128)(2,1)S(1)}, bf16[96,1536]{1,0:T(8,128)(2,1)S(1)}, u32[]{:S(2)}, u32[]{:S(2)}) %collective-permute-start.9) | collective-permute-done | bytes 294944 | tf_op jit(solution)/shard_map/ppermute | solution.py:34
  36.3 0.7 choose1.1
  37.0 1.1 %collective-permute-start.17 = (bf16[64,1536]{1,0:T(8,128)(2,1)S(1)}, bf16[64,1536]{1,0:T(8,128)(2,1)S(1)}, u32[]{:S(2)}, u32[]{:S(2)}) collective-permute-start(bf16[64,1536]{1,0:T(8,128)(2,1)S(1)} %get-tuple-element.57), channel_id=1, source_target_pairs={{0,8},{4,12},{8,0},{12,4},{16,24},{20,28},{24,16},{28,20},{1,9},{5... | collective-permute-start | bytes 589832 | tf_op jit(solution)/shard_map/ppermute | solution.py:34
  38.1 1.5 %collective-permute-done.14.refs_1_.refs_5_ = bf16[32,1536]{1,0:T(8,128)(2,1)S(1)} collective-permute-done((bf16[32,1536]{1,0:T(8,128)(2,1)S(1)}, bf16[32,1536]{1,0:T(8,128)(2,1)S(1)}, u32[]{:S(2)}, u32[]{:S(2)}) %collective-permute-start.14) | collective-permute-done | bytes 98336 | tf_op jit(solution)/shard_map/ppermute | solution.py:34
  39.6 0.5 collective-permute-done.15.refs_2_.refs_6_
  40.1 2.5 %collective-permute-done.6.refs_0_.refs_4_ = bf16[64,1536]{1,0:T(8,128)(2,1)S(1)} collective-permute-done((bf16[64,1536]{1,0:T(8,128)(2,1)S(1)}, bf16[64,1536]{1,0:T(8,128)(2,1)S(1)}, u32[]{:S(2)}, u32[]{:S(2)}) %collective-permute-start.6) | collective-permute-done | bytes 196640 | tf_op jit(solution)/shard_map/ppermute | solution.py:34
  42.6 2.1 %collective-permute-start.16 = (bf16[96,1536]{1,0:T(8,128)(2,1)S(1)}, bf16[96,1536]{1,0:T(8,128)(2,1)S(1)}, u32[]{:S(2)}, u32[]{:S(2)}) collective-permute-start(bf16[96,1536]{1,0:T(8,128)(2,1)S(1)} %stack2.1.refs_2_), channel_id=1, source_target_pairs={{0,4},{4,0},{8,12},{12,8},{16,20},{20,16},{24,28},{28,24},{1,5},{5... | collective-permute-start | bytes 884744 | tf_op jit(solution)/shard_map/ppermute | solution.py:34
  44.8 4.1 %collective-permute-start.13 = (bf16[32,1536]{1,0:T(8,128)(2,1)S(1)}, bf16[32,1536]{1,0:T(8,128)(2,1)S(1)}, u32[]{:S(2)}, u32[]{:S(2)}) collective-permute-start(bf16[32,1536]{1,0:T(8,128)(2,1)S(1)} %get-tuple-element.52), channel_id=1, source_target_pairs={{0,24},{4,28},{8,16},{12,20},{16,8},{20,12},{24,0},{28,4},{1,25},{... | collective-permute-start | bytes 294920 | tf_op jit(solution)/shard_map/ppermute | solution.py:34
  48.9 1.6 %collective-permute-start.21 = (bf16[128,1536]{1,0:T(8,128)(2,1)S(1)}, bf16[128,1536]{1,0:T(8,128)(2,1)S(1)}, u32[]{:S(2)}, u32[]{:S(2)}) collective-permute-start(bf16[128,1536]{1,0:T(8,128)(2,1)S(1)} %join1.1.refs_8_.refs_3_.refs_7_), channel_id=1, source_target_pairs={{0,2},{1,3},{2,0},{3,1},{4,6},{5,7},{6,4},{7,5},{8,10},{9,11},{10,... | collective-permute-start | bytes 1179656 | tf_op jit(solution)/shard_map/ppermute | solution.py:34
  50.5 0.7 choose2.1
  51.2 0.7 collective-permute-start.20
  52.0 2.4 %collective-permute-done.12.refs_1_.refs_5_ = bf16[32,1536]{1,0:T(8,128)(2,1)S(1)} collective-permute-done((bf16[32,1536]{1,0:T(8,128)(2,1)S(1)}, bf16[32,1536]{1,0:T(8,128)(2,1)S(1)}, u32[]{:S(2)}, u32[]{:S(2)}) %collective-permute-start.12) | collective-permute-done | bytes 98336 | tf_op jit(solution)/shard_map/ppermute | solution.py:34
  54.4 0.9 %collective-permute-start.19 = (bf16[96,1536]{1,0:T(8,128)(2,1)S(1)}, bf16[96,1536]{1,0:T(8,128)(2,1)S(1)}, u32[]{:S(2)}, u32[]{:S(2)}) collective-permute-start(bf16[96,1536]{1,0:T(8,128)(2,1)S(1)} %stack3.1.refs_2_), channel_id=1, source_target_pairs={{0,4},{4,0},{8,12},{12,8},{16,20},{20,16},{24,28},{28,24},{1,5},{5... | collective-permute-start | bytes 884744 | tf_op jit(solution)/shard_map/ppermute | solution.py:34
  55.4 1.6 %collective-permute-done.20.refs_1_ = bf16[64,1536]{1,0:T(8,128)(2,1)S(1)} collective-permute-done((bf16[64,1536]{1,0:T(8,128)(2,1)S(1)}, bf16[64,1536]{1,0:T(8,128)(2,1)S(1)}, u32[]{:S(2)}, u32[]{:S(2)}) %collective-permute-start.20) | collective-permute-done | bytes 196640 | tf_op jit(solution)/shard_map/ppermute | solution.py:34
  57.0 0.4 collective-permute-done.21.refs_4_.refs_8_
  57.4 1.6 %collective-permute-start.23 = (bf16[128,1536]{1,0:T(8,128)(2,1)S(1)}, bf16[128,1536]{1,0:T(8,128)(2,1)S(1)}, u32[]{:S(2)}, u32[]{:S(2)}) collective-permute-start(bf16[128,1536]{1,0:T(8,128)(2,1)S(1)} %join2.1.refs_8_.refs_3_.refs_9_), channel_id=1, source_target_pairs={{0,2},{1,3},{2,0},{3,1},{4,6},{5,7},{6,4},{7,5},{8,10},{9,11},{10,... | collective-permute-start | bytes 1179656 | tf_op jit(solution)/shard_map/ppermute | solution.py:34
  59.0 2.2 %collective-permute-done.19.refs_7_ = bf16[96,1536]{1,0:T(8,128)(2,1)S(1)} collective-permute-done((bf16[96,1536]{1,0:T(8,128)(2,1)S(1)}, bf16[96,1536]{1,0:T(8,128)(2,1)S(1)}, u32[]{:S(2)}, u32[]{:S(2)}) %collective-permute-start.19) | collective-permute-done | bytes 294944 | tf_op jit(solution)/shard_map/ppermute | solution.py:34
  61.2 0.7 choose3.1
  62.2 5.5 %collective-permute-done.22.refs_1_ = bf16[64,1536]{1,0:T(8,128)(2,1)S(1)} collective-permute-done((bf16[64,1536]{1,0:T(8,128)(2,1)S(1)}, bf16[64,1536]{1,0:T(8,128)(2,1)S(1)}, u32[]{:S(2)}, u32[]{:S(2)}) %collective-permute-start.22) | collective-permute-done | bytes 196640 | tf_op jit(solution)/shard_map/ppermute | solution.py:34
  67.7 2.0 %collective-permute-start.24 = (bf16[128,1536]{1,0:T(8,128)(2,1)S(1)}, bf16[128,1536]{1,0:T(8,128)(2,1)S(1)}, u32[]{:S(2)}, u32[]{:S(2)}) collective-permute-start(bf16[128,1536]{1,0:T(8,128)(2,1)S(1)} %join3.1.refs_11_.refs_5_), channel_id=1, source_target_pairs={{0,2},{1,3},{2,0},{3,1},{4,6},{5,7},{6,4},{7,5},{8,10},{9,11},{10,... | collective-permute-start | bytes 1179656 | tf_op jit(solution)/shard_map/ppermute | solution.py:34
  69.7 2.9 %early.1 = (f32[256,1536]{1,0:T(8,128)S(1)}, f32[128,1536]{1,0:T(8,128)S(1)}, f32[128,1536]{1,0:T(8,128)S(1)}) custom-call(bf16[512,1536]{1,0:T(8,128)(2,1)S(1)} %pad_maximum_fusion.refs_0_, f32[512,1]{1,0:T(8,128)S(1)} %bitcast.42, bf16[512,32]{1,0:T(8,128)(2,1)S(1)} %pad_maximum_fusion.1.refs_9_.refs_2_, f32[1,768]{1,0:T(1,128)S(1)} %get-tuple-element.103.refs_10_.refs_3_, ...), custom_call_target="tpu_custom_call" | custom-call | flops 10000000000 | bytes 1 | tf_op jit(solution)/shard_map/early/pallas_call | solution.py:63
  72.6 0.5 collective-permute-start.28
  73.2 2.4 %collective-permute-done.24.refs_6_ = bf16[128,1536]{1,0:T(8,128)(2,1)S(1)} collective-permute-done((bf16[128,1536]{1,0:T(8,128)(2,1)S(1)}, bf16[128,1536]{1,0:T(8,128)(2,1)S(1)}, u32[]{:S(2)}, u32[]{:S(2)}) %collective-permute-start.24) | collective-permute-done | bytes 393248 | tf_op jit(solution)/shard_map/ppermute | solution.py:34
  75.6 1.0 %collective-permute-done.25.refs_7_ = bf16[128,1536]{1,0:T(8,128)(2,1)S(1)} collective-permute-done((bf16[128,1536]{1,0:T(8,128)(2,1)S(1)}, bf16[128,1536]{1,0:T(8,128)(2,1)S(1)}, u32[]{:S(2)}, u32[]{:S(2)}) %collective-permute-start.25) | collective-permute-done | bytes 393248 | tf_op jit(solution)/shard_map/ppermute | solution.py:34
  76.6 0.7 collective-permute-done.26.refs_8_
  77.3 2.1 %late3.1 = f32[256,1536]{1,0:T(8,128)} custom-call(bf16[256,1536]{1,0:T(8,128)(2,1)S(1)} %bitcast.37, f32[256,1]{1,0:T(8,128)S(1)} %copy.29.refs_4_.refs_1_, bf16[256,32]{1,0:T(8,128)(2,1)S(1)} %bitcast.40, f32[1,512]{1,0:T(1,128)S(1)} %get-tuple-element.102.refs_6_.refs_3_, s32[1,512]{1,0:T(1,128)S(1)} %get-tuple-element.104.refs_7_.refs_4_, ...), custom_call_target="tpu_custom_call" | custom-call | flops 1 | bytes 1 | tf_op jit(solution)/shard_map/late3/pallas_call | solution.py:63
  (124 shorter events, 4.1 us)
Async XLA Ops:
  0.1 1.1 %copy-start = (bf16[1,256,1536]{2,1,0:T(8,128)(2,1)S(1)}, bf16[1,256,1536]{2,1,0:T(8,128)(2,1)}, u32[]{:S(2)}) copy-start(bf16[1,256,1536]{2,1,0:T(8,128)(2,1)} %param.5) | copy-start | bytes 2359300
  1.2 6.4 %copy-start.5 = (s32[2,1,1,56]{3,2,1,0:T(1,128)S(1)}, s32[2,1,1,56]{3,2,1,0:T(1,128)}, u32[]{:S(2)}) copy-start(s32[2,1,1,56]{3,2,1,0:T(1,128)} %param.9) | copy-start | bytes 1348
  1.2 8.1 %copy-start.4 = (f32[1024]{0:T(1024)S(1)}, f32[1024]{0:T(1024)}, u32[]{:S(2)}) copy-start(f32[1024]{0:T(1024)} %param.7) | copy-start | bytes 12292
  1.2 9.5 %copy-start.2 = (s32[2,8]{1,0:T(2,128)S(1)}, s32[2,8]{1,0:T(2,128)}, u32[]{:S(2)}) copy-start(s32[2,8]{1,0:T(2,128)} %refs_1_.7) | copy-start | bytes 196
  1.2 9.8 %copy-start.3 = (f32[8]{0:T(128)S(1)}, f32[8]{0:T(128)}, u32[]{:S(2)}) copy-start(f32[8]{0:T(128)} %param.6) | copy-start | bytes 100
  1.9 14.5 %collective-permute-start.1 = (bf16[64,1536]{1,0:T(8,128)(2,1)S(1)}, bf16[64,1536]{1,0:T(8,128)(2,1)S(1)}, u32[]{:S(2)}, u32[]{:S(2)}) collective-permute-start(bf16[64,1536]{1,0:T(8,128)(2,1)S(1)} %get-tuple-element.80), channel_id=1, source_target_pairs={{0,8},{4,12},{8,0},{12,4},{16,24},{20,28},{24,16},{28,20},{1,9},{5... | collective-permute-start | bytes 589832 | tf_op jit(solution)/shard_map/ppermute | solution.py:34
  5.0 10.1 %collective-permute-start.2 = (bf16[32,1536]{1,0:T(8,128)(2,1)S(1)}, bf16[32,1536]{1,0:T(8,128)(2,1)S(1)}, u32[]{:S(2)}, u32[]{:S(2)}) collective-permute-start(bf16[32,1536]{1,0:T(8,128)(2,1)S(1)} %get-tuple-element.38), channel_id=1, source_target_pairs={{0,16},{4,20},{8,24},{12,28},{16,0},{20,4},{24,8},{28,12},{1,17},{... | collective-permute-start | bytes 294920 | tf_op jit(solution)/shard_map/ppermute | solution.py:34
  7.6 8.8 %collective-permute-start.3 = (bf16[32,1536]{1,0:T(8,128)(2,1)S(1)}, bf16[32,1536]{1,0:T(8,128)(2,1)S(1)}, u32[]{:S(2)}, u32[]{:S(2)}) collective-permute-start(bf16[32,1536]{1,0:T(8,128)(2,1)S(1)} %get-tuple-element.39), channel_id=1, source_target_pairs={{0,24},{4,28},{8,16},{12,20},{16,8},{20,12},{24,0},{28,4},{1,25},{... | collective-permute-start | bytes 294920 | tf_op jit(solution)/shard_map/ppermute | solution.py:34
  7.6 7.1 %collective-permute-start.4 = (s32[2,56]{1,0:T(2,128)S(1)}, s32[2,56]{1,0:T(2,128)S(1)}, u32[]{:S(2)}, u32[]{:S(2)}) collective-permute-start(s32[2,56]{1,0:T(2,128)S(1)} %bitcast.55), channel_id=1, source_target_pairs={{0,1},{1,0},{2,3},{3,2},{4,5},{5,4},{6,7},{7,6},{8,9},{9,8},{10,11... | collective-permute-start | bytes 1352 | tf_op jit(solution)/shard_map/ppermute | solution.py:34
  7.6 12.8 %collective-permute-start = (bf16[128,1536]{1,0:T(8,128)(2,1)S(1)}, bf16[128,1536]{1,0:T(8,128)(2,1)S(1)}, u32[]{:S(2)}, u32[]{:S(2)}) collective-permute-start(bf16[128,1536]{1,0:T(8,128)(2,1)S(1)} %get-tuple-element.36.refs_3_.refs_2_), channel_id=1, source_target_pairs={{0,4},{4,0},{8,12},{12,8},{16,20},{20,16},{24,28},{28,24},{1,5},{5... | collective-permute-start | bytes 1179656 | tf_op jit(solution)/shard_map/ppermute | solution.py:34
  16.4 3.9 %copy-start.1 = (bf16[1,256,1536]{2,1,0:T(8,128)(2,1)S(1)}, bf16[1,256,1536]{2,1,0:T(8,128)(2,1)}, u32[]{:S(2)}) copy-start(bf16[1,256,1536]{2,1,0:T(8,128)(2,1)} %param.5) | copy-start | bytes 2359300
  16.4 9.0 %collective-permute-start.5 = (bf16[96,1536]{1,0:T(8,128)(2,1)S(1)}, bf16[96,1536]{1,0:T(8,128)(2,1)S(1)}, u32[]{:S(2)}, u32[]{:S(2)}) collective-permute-start(bf16[96,1536]{1,0:T(8,128)(2,1)S(1)} %stack0.1.refs_8_), channel_id=1, source_target_pairs={{0,4},{4,0},{8,12},{12,8},{16,20},{20,16},{24,28},{28,24},{1,5},{5... | collective-permute-start | bytes 884744 | tf_op jit(solution)/shard_map/ppermute | solution.py:34
  18.0 9.1 %collective-permute-start.8 = (bf16[32,1536]{1,0:T(8,128)(2,1)S(1)}, bf16[32,1536]{1,0:T(8,128)(2,1)S(1)}, u32[]{:S(2)}, u32[]{:S(2)}) collective-permute-start(bf16[32,1536]{1,0:T(8,128)(2,1)S(1)} %get-tuple-element.46), channel_id=1, source_target_pairs={{0,24},{4,28},{8,16},{12,20},{16,8},{20,12},{24,0},{28,4},{1,25},{... | collective-permute-start | bytes 294920 | tf_op jit(solution)/shard_map/ppermute | solution.py:34
  19.6 8.6 %collective-permute-start.7 = (bf16[32,1536]{1,0:T(8,128)(2,1)S(1)}, bf16[32,1536]{1,0:T(8,128)(2,1)S(1)}, u32[]{:S(2)}, u32[]{:S(2)}) collective-permute-start(bf16[32,1536]{1,0:T(8,128)(2,1)S(1)} %get-tuple-element.44), channel_id=1, source_target_pairs={{0,16},{4,20},{8,24},{12,28},{16,0},{20,4},{24,8},{28,12},{1,17},{... | collective-permute-start | bytes 294920 | tf_op jit(solution)/shard_map/ppermute | solution.py:34
  20.4 12.7 %collective-permute-start.11 = (bf16[256,1536]{1,0:T(8,128)(2,1)S(1)}, bf16[256,1536]{1,0:T(8,128)(2,1)S(1)}, u32[]{:S(2)}, u32[]{:S(2)}) collective-permute-start(bf16[256,1536]{1,0:T(8,128)(2,1)S(1)} %bitcast.35), channel_id=1, source_target_pairs={{0,1},{1,0},{2,3},{3,2},{4,5},{5,4},{6,7},{7,6},{8,9},{9,8},{10,11... | collective-permute-start | bytes 2359304 | tf_op jit(solution)/shard_map/ppermute | solution.py:34
  26.2 6.3 %collective-permute-start.10 = (bf16[64,1536]{1,0:T(8,128)(2,1)S(1)}, bf16[64,1536]{1,0:T(8,128)(2,1)S(1)}, u32[]{:S(2)}, u32[]{:S(2)}) collective-permute-start(bf16[64,1536]{1,0:T(8,128)(2,1)S(1)} %get-tuple-element.47), channel_id=1, source_target_pairs={{0,8},{4,12},{8,0},{12,4},{16,24},{20,28},{24,16},{28,20},{1,9},{5... | collective-permute-start | bytes 589832 | tf_op jit(solution)/shard_map/ppermute | solution.py:34
  28.2 8.1 %collective-permute-start.9 = (bf16[96,1536]{1,0:T(8,128)(2,1)S(1)}, bf16[96,1536]{1,0:T(8,128)(2,1)S(1)}, u32[]{:S(2)}, u32[]{:S(2)}) collective-permute-start(bf16[96,1536]{1,0:T(8,128)(2,1)S(1)} %stack1.1.refs_2_), channel_id=1, source_target_pairs={{0,4},{4,0},{8,12},{12,8},{16,20},{20,16},{24,28},{28,24},{1,5},{5... | collective-permute-start | bytes 884744 | tf_op jit(solution)/shard_map/ppermute | solution.py:34
  29.1 10.5 %collective-permute-start.14 = (bf16[32,1536]{1,0:T(8,128)(2,1)S(1)}, bf16[32,1536]{1,0:T(8,128)(2,1)S(1)}, u32[]{:S(2)}, u32[]{:S(2)}) collective-permute-start(bf16[32,1536]{1,0:T(8,128)(2,1)S(1)} %get-tuple-element.54), channel_id=1, source_target_pairs={{0,16},{4,20},{8,24},{12,28},{16,0},{20,4},{24,8},{28,12},{1,17},{... | collective-permute-start | bytes 294920 | tf_op jit(solution)/shard_map/ppermute | solution.py:34
  32.3 7.8 %collective-permute-start.15 = (bf16[32,1536]{1,0:T(8,128)(2,1)S(1)}, bf16[32,1536]{1,0:T(8,128)(2,1)S(1)}, u32[]{:S(2)}, u32[]{:S(2)}) collective-permute-start(bf16[32,1536]{1,0:T(8,128)(2,1)S(1)} %get-tuple-element.56), channel_id=1, source_target_pairs={{0,24},{4,28},{8,16},{12,20},{16,8},{20,12},{24,0},{28,4},{1,25},{... | collective-permute-start | bytes 294920 | tf_op jit(solution)/shard_map/ppermute | solution.py:34
  32.5 10.1 %collective-permute-start.6 = (bf16[64,1536]{1,0:T(8,128)(2,1)S(1)}, bf16[64,1536]{1,0:T(8,128)(2,1)S(1)}, u32[]{:S(2)}, u32[]{:S(2)}) collective-permute-start(bf16[64,1536]{1,0:T(8,128)(2,1)S(1)} %get-tuple-element.41), channel_id=1, source_target_pairs={{0,8},{4,12},{8,0},{12,4},{16,24},{20,28},{24,16},{28,20},{1,9},{5... | collective-permute-start | bytes 589832 | tf_op jit(solution)/shard_map/ppermute | solution.py:34
  33.1 15.8 %collective-permute-start.18 = (bf16[128,1536]{1,0:T(8,128)(2,1)S(1)}, bf16[128,1536]{1,0:T(8,128)(2,1)S(1)}, u32[]{:S(2)}, u32[]{:S(2)}) collective-permute-start(bf16[128,1536]{1,0:T(8,128)(2,1)S(1)} %join0.1.refs_8_.refs_3_.refs_5_), channel_id=1, source_target_pairs={{0,2},{1,3},{2,0},{3,1},{4,6},{5,7},{6,4},{7,5},{8,10},{9,11},{10,... | collective-permute-start | bytes 1179656 | tf_op jit(solution)/shard_map/ppermute | solution.py:34
  37.0 11.8 %collective-permute-start.17 = (bf16[64,1536]{1,0:T(8,128)(2,1)S(1)}, bf16[64,1536]{1,0:T(8,128)(2,1)S(1)}, u32[]{:S(2)}, u32[]{:S(2)}) collective-permute-start(bf16[64,1536]{1,0:T(8,128)(2,1)S(1)} %get-tuple-element.57), channel_id=1, source_target_pairs={{0,8},{4,12},{8,0},{12,4},{16,24},{20,28},{24,16},{28,20},{1,9},{5... | collective-permute-start | bytes 589832 | tf_op jit(solution)/shard_map/ppermute | solution.py:34
  42.6 7.8 %collective-permute-start.16 = (bf16[96,1536]{1,0:T(8,128)(2,1)S(1)}, bf16[96,1536]{1,0:T(8,128)(2,1)S(1)}, u32[]{:S(2)}, u32[]{:S(2)}) collective-permute-start(bf16[96,1536]{1,0:T(8,128)(2,1)S(1)} %stack2.1.refs_2_), channel_id=1, source_target_pairs={{0,4},{4,0},{8,12},{12,8},{16,20},{20,16},{24,28},{28,24},{1,5},{5... | collective-permute-start | bytes 884744 | tf_op jit(solution)/shard_map/ppermute | solution.py:34
  44.8 7.2 %collective-permute-start.13 = (bf16[32,1536]{1,0:T(8,128)(2,1)S(1)}, bf16[32,1536]{1,0:T(8,128)(2,1)S(1)}, u32[]{:S(2)}, u32[]{:S(2)}) collective-permute-start(bf16[32,1536]{1,0:T(8,128)(2,1)S(1)} %get-tuple-element.52), channel_id=1, source_target_pairs={{0,24},{4,28},{8,16},{12,20},{16,8},{20,12},{24,0},{28,4},{1,25},{... | collective-permute-start | bytes 294920 | tf_op jit(solution)/shard_map/ppermute | solution.py:34
  48.9 5.5 %collective-permute-start.12 = (bf16[32,1536]{1,0:T(8,128)(2,1)S(1)}, bf16[32,1536]{1,0:T(8,128)(2,1)S(1)}, u32[]{:S(2)}, u32[]{:S(2)}) collective-permute-start(bf16[32,1536]{1,0:T(8,128)(2,1)S(1)} %get-tuple-element.50), channel_id=1, source_target_pairs={{0,16},{4,20},{8,24},{12,28},{16,0},{20,4},{24,8},{28,12},{1,17},{... | collective-permute-start | bytes 294920 | tf_op jit(solution)/shard_map/ppermute | solution.py:34
  48.9 8.4 %collective-permute-start.21 = (bf16[128,1536]{1,0:T(8,128)(2,1)S(1)}, bf16[128,1536]{1,0:T(8,128)(2,1)S(1)}, u32[]{:S(2)}, u32[]{:S(2)}) collective-permute-start(bf16[128,1536]{1,0:T(8,128)(2,1)S(1)} %join1.1.refs_8_.refs_3_.refs_7_), channel_id=1, source_target_pairs={{0,2},{1,3},{2,0},{3,1},{4,6},{5,7},{6,4},{7,5},{8,10},{9,11},{10,... | collective-permute-start | bytes 1179656 | tf_op jit(solution)/shard_map/ppermute | solution.py:34
  51.2 5.7 %collective-permute-start.20 = (bf16[64,1536]{1,0:T(8,128)(2,1)S(1)}, bf16[64,1536]{1,0:T(8,128)(2,1)S(1)}, u32[]{:S(2)}, u32[]{:S(2)}) collective-permute-start(bf16[64,1536]{1,0:T(8,128)(2,1)S(1)} %get-tuple-element.59), channel_id=1, source_target_pairs={{0,8},{4,12},{8,0},{12,4},{16,24},{20,28},{24,16},{28,20},{1,9},{5... | collective-permute-start | bytes 589832 | tf_op jit(solution)/shard_map/ppermute | solution.py:34
  54.4 6.8 %collective-permute-start.19 = (bf16[96,1536]{1,0:T(8,128)(2,1)S(1)}, bf16[96,1536]{1,0:T(8,128)(2,1)S(1)}, u32[]{:S(2)}, u32[]{:S(2)}) collective-permute-start(bf16[96,1536]{1,0:T(8,128)(2,1)S(1)} %stack3.1.refs_2_), channel_id=1, source_target_pairs={{0,4},{4,0},{8,12},{12,8},{16,20},{20,16},{24,28},{28,24},{1,5},{5... | collective-permute-start | bytes 884744 | tf_op jit(solution)/shard_map/ppermute | solution.py:34
  57.4 10.3 %collective-permute-start.23 = (bf16[128,1536]{1,0:T(8,128)(2,1)S(1)}, bf16[128,1536]{1,0:T(8,128)(2,1)S(1)}, u32[]{:S(2)}, u32[]{:S(2)}) collective-permute-start(bf16[128,1536]{1,0:T(8,128)(2,1)S(1)} %join2.1.refs_8_.refs_3_.refs_9_), channel_id=1, source_target_pairs={{0,2},{1,3},{2,0},{3,1},{4,6},{5,7},{6,4},{7,5},{8,10},{9,11},{10,... | collective-permute-start | bytes 1179656 | tf_op jit(solution)/shard_map/ppermute | solution.py:34
  62.0 5.7 %collective-permute-start.22 = (bf16[64,1536]{1,0:T(8,128)(2,1)S(1)}, bf16[64,1536]{1,0:T(8,128)(2,1)S(1)}, u32[]{:S(2)}, u32[]{:S(2)}) collective-permute-start(bf16[64,1536]{1,0:T(8,128)(2,1)S(1)} %get-tuple-element.61), channel_id=1, source_target_pairs={{0,8},{4,12},{8,0},{12,4},{16,24},{20,28},{24,16},{28,20},{1,9},{5... | collective-permute-start | bytes 589832 | tf_op jit(solution)/shard_map/ppermute | solution.py:34
  67.7 7.8 %collective-permute-start.24 = (bf16[128,1536]{1,0:T(8,128)(2,1)S(1)}, bf16[128,1536]{1,0:T(8,128)(2,1)S(1)}, u32[]{:S(2)}, u32[]{:S(2)}) collective-permute-start(bf16[128,1536]{1,0:T(8,128)(2,1)S(1)} %join3.1.refs_11_.refs_5_), channel_id=1, source_target_pairs={{0,2},{1,3},{2,0},{3,1},{4,6},{5,7},{6,4},{7,5},{8,10},{9,11},{10,... | collective-permute-start | bytes 1179656 | tf_op jit(solution)/shard_map/ppermute | solution.py:34
  72.6 4.7 %collective-permute-start.27 = (f32[128,1536]{1,0:T(8,128)S(1)}, f32[128,1536]{1,0:T(8,128)S(1)}, u32[]{:S(2)}, u32[]{:S(2)}) collective-permute-start(f32[128,1536]{1,0:T(8,128)S(1)} %get-tuple-element.65), channel_id=1, source_target_pairs={{0,1},{1,0},{2,3},{3,2},{4,5},{5,4},{6,7},{7,6},{8,9},{9,8},{10,11... | collective-permute-start | bytes 2359304 | tf_op jit(solution)/shard_map/ppermute | solution.py:34
  72.6 4.7 %collective-permute-start.28 = (f32[128,1536]{1,0:T(8,128)S(1)}, f32[128,1536]{1,0:T(8,128)S(1)}, u32[]{:S(2)}, u32[]{:S(2)}) collective-permute-start(f32[128,1536]{1,0:T(8,128)S(1)} %get-tuple-element.66), channel_id=1, source_target_pairs={{0,1},{1,0},{2,3},{3,2},{4,5},{5,4},{6,7},{7,6},{8,9},{9,8},{10,11... | collective-permute-start | bytes 2359304 | tf_op jit(solution)/shard_map/ppermute | solution.py:34
  73.1 3.5 %collective-permute-start.25 = (bf16[128,1536]{1,0:T(8,128)(2,1)S(1)}, bf16[128,1536]{1,0:T(8,128)(2,1)S(1)}, u32[]{:S(2)}, u32[]{:S(2)}) collective-permute-start(bf16[128,1536]{1,0:T(8,128)(2,1)S(1)} %join3.1.refs_11_.refs_5_), channel_id=1, source_target_pairs={{0,1},{1,0},{2,3},{3,2},{4,5},{5,4},{6,7},{7,6},{8,9},{9,8},{10,11... | collective-permute-start | bytes 1179656 | tf_op jit(solution)/shard_map/ppermute | solution.py:34
  75.6 1.7 %collective-permute-start.26 = (bf16[128,1536]{1,0:T(8,128)(2,1)S(1)}, bf16[128,1536]{1,0:T(8,128)(2,1)S(1)}, u32[]{:S(2)}, u32[]{:S(2)}) collective-permute-start(bf16[128,1536]{1,0:T(8,128)(2,1)S(1)} %collective-permute-done.24.refs_6_), channel_id=1, source_target_pairs={{0,1},{1,0},{2,3},{3,2},{4,5},{5,4},{6,7},{7,6},{8,9},{9,8},{10,11... | collective-permute-start | bytes 1179656 | tf_op jit(solution)/shard_map/ppermute | solution.py:34

commit v7 on v6

--- a/solution.py
+++ b/solution.py
@@ -24,7 +24,7 @@
 ORDER = "s"
 FL, FK, BY = 10**10, 1, 1
 FE = 10**10
-WS, WJ, WC = 10**10, 10**10, 10**10
+WS, WJ, WC = 10**10, 2 * 10**10, 2 * 10**10
 VMEM = pl.BlockSpec(memory_space=pltpu.VMEM)
 SMEM = pl.BlockSpec(memory_space=pltpu.SMEM)
 ANY = pl.BlockSpec(memory_space=pl.ANY)

time: 79.5 us -> 79.5 us (level)
  starting transfers between devices: 34.1 us -> 32.7 us
  waiting for transfers between devices: 29.3 us -> 30.6 us
    ppermute x29, starting transfers between devices: 34.1 us -> 32.7 us  [send(): lax.ppermute(value, axis, [(i, i ^ mask) for i in range(lax.axis_size(axi...]
    ppermute x29, waiting for transfers between devices: 29.3 us -> 30.6 us  [send(): lax.ppermute(value, axis, [(i, i ^ mask) for i in range(lax.axis_size(axi...]
  transfers between devices with their start and end apart: 29 -> 29, of which waited for: 15 -> 16; matrix products, arithmetic and copies ran while one was open for 7% -> 7% of each run, Pallas kernels for 8% -> 8%
where the time goes in v7:
time: 79.5 us; the launch traced here: 79.4 us
  starting transfers between devices  32.7 us (41%)
  waiting for transfers between devices  30.6 us (38%)
  Pallas kernels  8.74 us (11%)
  local copies, waits for them, and re-layouts  5.23 us (7%)
  other arithmetic  1.63 us (2%)
    ppermute x29, starting transfers between devices, send(): lax.ppermute(value, axis, [(i, i ^ mask) for i in range(lax.axis_size(axi...  32.7 us
    ppermute x29, waiting for transfers between devices, send(): lax.ppermute(value, axis, [(i, i ^ mask) for i in range(lax.axis_size(axi...  30.6 us
    pallas_call x15, Pallas kernels, call(): pl.pallas_call(run, out_shape=tuple(outs), in_specs=[SMEM] * len(smem) +...  8.74 us
    another operation x20, local copies, waits for them, and re-layouts, column(): x[m, :, :, slice(*spans[c])].reshape(1, -1)  1.65 us
  transfers between devices with their start and end apart: 29, of which 16 were waited for; matrix products, arithmetic and copies ran while one was open for 7% of the time, Pallas kernels for 8%

profile of v7, /device:TPU:0, one launch (start us, length us, event | category | flops | bytes accessed | tf_op | source)
XLA Modules:
  0.0 79.4 jit_solution(5823631192666276861)
XLA Ops:
  0.1 1.1 %copy-done = bf16[1,256,1536]{2,1,0:T(8,128)(2,1)S(1)} copy-done((bf16[1,256,1536]{2,1,0:T(8,128)(2,1)S(1)}, bf16[1,256,1536]{2,1,0:T(8,128)(2,1)}, u32[]{:S(2)}) %copy-start) | copy-done | bytes 786456
  1.2 0.7 cut.1
  1.9 3.1 %collective-permute-start.1 = (bf16[64,1536]{1,0:T(8,128)(2,1)S(1)}, bf16[64,1536]{1,0:T(8,128)(2,1)S(1)}, u32[]{:S(2)}, u32[]{:S(2)}) collective-permute-start(bf16[64,1536]{1,0:T(8,128)(2,1)S(1)} %get-tuple-element.80), channel_id=1, source_target_pairs={{0,8},{4,12},{8,0},{12,4},{16,24},{20,28},{24,16},{28,20},{1,9},{5... | collective-permute-start | bytes 589832 | tf_op jit(solution)/shard_map/ppermute | solution.py:34
  5.0 2.6 %collective-permute-start.2 = (bf16[32,1536]{1,0:T(8,128)(2,1)S(1)}, bf16[32,1536]{1,0:T(8,128)(2,1)S(1)}, u32[]{:S(2)}, u32[]{:S(2)}) collective-permute-start(bf16[32,1536]{1,0:T(8,128)(2,1)S(1)} %get-tuple-element.38), channel_id=1, source_target_pairs={{0,16},{4,20},{8,24},{12,28},{16,0},{20,4},{24,8},{28,12},{1,17},{... | collective-permute-start | bytes 294920 | tf_op jit(solution)/shard_map/ppermute | solution.py:34
  7.6 1.7 %collective-permute-start = (bf16[128,1536]{1,0:T(8,128)(2,1)S(1)}, bf16[128,1536]{1,0:T(8,128)(2,1)S(1)}, u32[]{:S(2)}, u32[]{:S(2)}) collective-permute-start(bf16[128,1536]{1,0:T(8,128)(2,1)S(1)} %get-tuple-element.36.refs_3_.refs_2_), channel_id=1, source_target_pairs={{0,4},{4,0},{8,12},{12,8},{16,20},{20,16},{24,28},{28,24},{1,5},{5... | collective-permute-start | bytes 1179656 | tf_op jit(solution)/shard_map/ppermute | solution.py:34
  10.8 0.2 fusion.5
  11.0 0.6 dynamic_slice.4
  11.6 0.6 gather_fusion
  13.4 0.7 fusion.3
  15.1 1.3 %collective-permute-done.3.refs_2_.refs_6_ = bf16[32,1536]{1,0:T(8,128)(2,1)S(1)} collective-permute-done((bf16[32,1536]{1,0:T(8,128)(2,1)S(1)}, bf16[32,1536]{1,0:T(8,128)(2,1)S(1)}, u32[]{:S(2)}, u32[]{:S(2)}) %collective-permute-start.3) | collective-permute-done | bytes 98336 | tf_op jit(solution)/shard_map/ppermute | solution.py:34
  16.5 1.6 %collective-permute-start.5 = (bf16[96,1536]{1,0:T(8,128)(2,1)S(1)}, bf16[96,1536]{1,0:T(8,128)(2,1)S(1)}, u32[]{:S(2)}, u32[]{:S(2)}) collective-permute-start(bf16[96,1536]{1,0:T(8,128)(2,1)S(1)} %stack0.1.refs_8_), channel_id=1, source_target_pairs={{0,4},{4,0},{8,12},{12,8},{16,20},{20,16},{24,28},{28,24},{1,5},{5... | collective-permute-start | bytes 884744 | tf_op jit(solution)/shard_map/ppermute | solution.py:34
  18.1 1.8 %collective-permute-start.8 = (bf16[32,1536]{1,0:T(8,128)(2,1)S(1)}, bf16[32,1536]{1,0:T(8,128)(2,1)S(1)}, u32[]{:S(2)}, u32[]{:S(2)}) collective-permute-start(bf16[32,1536]{1,0:T(8,128)(2,1)S(1)} %get-tuple-element.46), channel_id=1, source_target_pairs={{0,24},{4,28},{8,16},{12,20},{16,8},{20,12},{24,0},{28,4},{1,25},{... | collective-permute-start | bytes 294920 | tf_op jit(solution)/shard_map/ppermute | solution.py:34
  19.8 0.5 collective-permute-start.7
  20.4 5.1 %collective-permute-done.5.refs_7_ = bf16[96,1536]{1,0:T(8,128)(2,1)S(1)} collective-permute-done((bf16[96,1536]{1,0:T(8,128)(2,1)S(1)}, bf16[96,1536]{1,0:T(8,128)(2,1)S(1)}, u32[]{:S(2)}, u32[]{:S(2)}) %collective-permute-start.5) | collective-permute-done | bytes 294944 | tf_op jit(solution)/shard_map/ppermute | solution.py:34
  25.5 0.7 choose0.1
  26.2 1.0 %collective-permute-start.10 = (bf16[64,1536]{1,0:T(8,128)(2,1)S(1)}, bf16[64,1536]{1,0:T(8,128)(2,1)S(1)}, u32[]{:S(2)}, u32[]{:S(2)}) collective-permute-start(bf16[64,1536]{1,0:T(8,128)(2,1)S(1)} %get-tuple-element.47), channel_id=1, source_target_pairs={{0,8},{4,12},{8,0},{12,4},{16,24},{20,28},{24,16},{28,20},{1,9},{5... | collective-permute-start | bytes 589832 | tf_op jit(solution)/shard_map/ppermute | solution.py:34
  27.2 1.0 %collective-permute-done.7.refs_1_.refs_5_ = bf16[32,1536]{1,0:T(8,128)(2,1)S(1)} collective-permute-done((bf16[32,1536]{1,0:T(8,128)(2,1)S(1)}, bf16[32,1536]{1,0:T(8,128)(2,1)S(1)}, u32[]{:S(2)}, u32[]{:S(2)}) %collective-permute-start.7) | collective-permute-done | bytes 98336 | tf_op jit(solution)/shard_map/ppermute | solution.py:34
  28.2 1.4 %collective-permute-start.9 = (bf16[96,1536]{1,0:T(8,128)(2,1)S(1)}, bf16[96,1536]{1,0:T(8,128)(2,1)S(1)}, u32[]{:S(2)}, u32[]{:S(2)}) collective-permute-start(bf16[96,1536]{1,0:T(8,128)(2,1)S(1)} %stack1.1.refs_2_), channel_id=1, source_target_pairs={{0,4},{4,0},{8,12},{12,8},{16,20},{20,16},{24,28},{28,24},{1,5},{5... | collective-permute-start | bytes 884744 | tf_op jit(solution)/shard_map/ppermute | solution.py:34
  29.6 2.6 %collective-permute-start.14 = (bf16[32,1536]{1,0:T(8,128)(2,1)S(1)}, bf16[32,1536]{1,0:T(8,128)(2,1)S(1)}, u32[]{:S(2)}, u32[]{:S(2)}) collective-permute-start(bf16[32,1536]{1,0:T(8,128)(2,1)S(1)} %get-tuple-element.54), channel_id=1, source_target_pairs={{0,16},{4,20},{8,24},{12,28},{16,0},{20,4},{24,8},{28,12},{1,17},{... | collective-permute-start | bytes 294920 | tf_op jit(solution)/shard_map/ppermute | solution.py:34
  32.3 0.2 collective-permute-start.15
  32.5 1.0 %collective-permute-done.10.refs_1_ = bf16[64,1536]{1,0:T(8,128)(2,1)S(1)} collective-permute-done((bf16[64,1536]{1,0:T(8,128)(2,1)S(1)}, bf16[64,1536]{1,0:T(8,128)(2,1)S(1)}, u32[]{:S(2)}, u32[]{:S(2)}) %collective-permute-start.10) | collective-permute-done | bytes 196640 | tf_op jit(solution)/shard_map/ppermute | solution.py:34
  33.5 1.7 %collective-permute-start.18 = (bf16[128,1536]{1,0:T(8,128)(2,1)S(1)}, bf16[128,1536]{1,0:T(8,128)(2,1)S(1)}, u32[]{:S(2)}, u32[]{:S(2)}) collective-permute-start(bf16[128,1536]{1,0:T(8,128)(2,1)S(1)} %join0.1.refs_8_.refs_3_.refs_5_), channel_id=1, source_target_pairs={{0,2},{1,3},{2,0},{3,1},{4,6},{5,7},{6,4},{7,5},{8,10},{9,11},{10,... | collective-permute-start | bytes 1179656 | tf_op jit(solution)/shard_map/ppermute | solution.py:34
  35.2 1.1 %collective-permute-done.9.refs_7_ = bf16[96,1536]{1,0:T(8,128)(2,1)S(1)} collective-permute-done((bf16[96,1536]{1,0:T(8,128)(2,1)S(1)}, bf16[96,1536]{1,0:T(8,128)(2,1)S(1)}, u32[]{:S(2)}, u32[]{:S(2)}) %collective-permute-start.9) | collective-permute-done | bytes 294944 | tf_op jit(solution)/shard_map/ppermute | solution.py:34
  36.4 0.7 choose1.1
  37.1 1.0 %collective-permute-start.17 = (bf16[64,1536]{1,0:T(8,128)(2,1)S(1)}, bf16[64,1536]{1,0:T(8,128)(2,1)S(1)}, u32[]{:S(2)}, u32[]{:S(2)}) collective-permute-start(bf16[64,1536]{1,0:T(8,128)(2,1)S(1)} %get-tuple-element.57), channel_id=1, source_target_pairs={{0,8},{4,12},{8,0},{12,4},{16,24},{20,28},{24,16},{28,20},{1,9},{5... | collective-permute-start | bytes 589832 | tf_op jit(solution)/shard_map/ppermute | solution.py:34
  38.1 1.5 %collective-permute-done.14.refs_1_.refs_5_ = bf16[32,1536]{1,0:T(8,128)(2,1)S(1)} collective-permute-done((bf16[32,1536]{1,0:T(8,128)(2,1)S(1)}, bf16[32,1536]{1,0:T(8,128)(2,1)S(1)}, u32[]{:S(2)}, u32[]{:S(2)}) %collective-permute-start.14) | collective-permute-done | bytes 98336 | tf_op jit(solution)/shard_map/ppermute | solution.py:34
  39.6 0.5 collective-permute-done.15.refs_2_.refs_6_
  40.1 2.9 %collective-permute-done.6.refs_0_.refs_4_ = bf16[64,1536]{1,0:T(8,128)(2,1)S(1)} collective-permute-done((bf16[64,1536]{1,0:T(8,128)(2,1)S(1)}, bf16[64,1536]{1,0:T(8,128)(2,1)S(1)}, u32[]{:S(2)}, u32[]{:S(2)}) %collective-permute-start.6) | collective-permute-done | bytes 196640 | tf_op jit(solution)/shard_map/ppermute | solution.py:34
  43.0 1.9 %collective-permute-start.16 = (bf16[96,1536]{1,0:T(8,128)(2,1)S(1)}, bf16[96,1536]{1,0:T(8,128)(2,1)S(1)}, u32[]{:S(2)}, u32[]{:S(2)}) collective-permute-start(bf16[96,1536]{1,0:T(8,128)(2,1)S(1)} %stack2.1.refs_2_), channel_id=1, source_target_pairs={{0,4},{4,0},{8,12},{12,8},{16,20},{20,16},{24,28},{28,24},{1,5},{5... | collective-permute-start | bytes 884744 | tf_op jit(solution)/shard_map/ppermute | solution.py:34
  44.9 4.0 %collective-permute-start.13 = (bf16[32,1536]{1,0:T(8,128)(2,1)S(1)}, bf16[32,1536]{1,0:T(8,128)(2,1)S(1)}, u32[]{:S(2)}, u32[]{:S(2)}) collective-permute-start(bf16[32,1536]{1,0:T(8,128)(2,1)S(1)} %get-tuple-element.52), channel_id=1, source_target_pairs={{0,24},{4,28},{8,16},{12,20},{16,8},{20,12},{24,0},{28,4},{1,25},{... | collective-permute-start | bytes 294920 | tf_op jit(solution)/shard_map/ppermute | solution.py:34
  48.9 1.6 %collective-permute-start.21 = (bf16[128,1536]{1,0:T(8,128)(2,1)S(1)}, bf16[128,1536]{1,0:T(8,128)(2,1)S(1)}, u32[]{:S(2)}, u32[]{:S(2)}) collective-permute-start(bf16[128,1536]{1,0:T(8,128)(2,1)S(1)} %join1.1.refs_8_.refs_3_.refs_7_), channel_id=1, source_target_pairs={{0,2},{1,3},{2,0},{3,1},{4,6},{5,7},{6,4},{7,5},{8,10},{9,11},{10,... | collective-permute-start | bytes 1179656 | tf_op jit(solution)/shard_map/ppermute | solution.py:34
  50.5 0.7 choose2.1
  51.2 0.7 collective-permute-start.20
  52.0 2.4 %collective-permute-done.12.refs_1_.refs_5_ = bf16[32,1536]{1,0:T(8,128)(2,1)S(1)} collective-permute-done((bf16[32,1536]{1,0:T(8,128)(2,1)S(1)}, bf16[32,1536]{1,0:T(8,128)(2,1)S(1)}, u32[]{:S(2)}, u32[]{:S(2)}) %collective-permute-start.12) | collective-permute-done | bytes 98336 | tf_op jit(solution)/shard_map/ppermute | solution.py:34
  54.4 0.9 %collective-permute-start.19 = (bf16[96,1536]{1,0:T(8,128)(2,1)S(1)}, bf16[96,1536]{1,0:T(8,128)(2,1)S(1)}, u32[]{:S(2)}, u32[]{:S(2)}) collective-permute-start(bf16[96,1536]{1,0:T(8,128)(2,1)S(1)} %stack3.1.refs_2_), channel_id=1, source_target_pairs={{0,4},{4,0},{8,12},{12,8},{16,20},{20,16},{24,28},{28,24},{1,5},{5... | collective-permute-start | bytes 884744 | tf_op jit(solution)/shard_map/ppermute | solution.py:34
  55.3 1.6 %collective-permute-done.20.refs_1_ = bf16[64,1536]{1,0:T(8,128)(2,1)S(1)} collective-permute-done((bf16[64,1536]{1,0:T(8,128)(2,1)S(1)}, bf16[64,1536]{1,0:T(8,128)(2,1)S(1)}, u32[]{:S(2)}, u32[]{:S(2)}) %collective-permute-start.20) | collective-permute-done | bytes 196640 | tf_op jit(solution)/shard_map/ppermute | solution.py:34
  57.0 0.4 collective-permute-done.21.refs_4_.refs_8_
  57.4 1.6 %collective-permute-start.23 = (bf16[128,1536]{1,0:T(8,128)(2,1)S(1)}, bf16[128,1536]{1,0:T(8,128)(2,1)S(1)}, u32[]{:S(2)}, u32[]{:S(2)}) collective-permute-start(bf16[128,1536]{1,0:T(8,128)(2,1)S(1)} %join2.1.refs_8_.refs_3_.refs_9_), channel_id=1, source_target_pairs={{0,2},{1,3},{2,0},{3,1},{4,6},{5,7},{6,4},{7,5},{8,10},{9,11},{10,... | collective-permute-start | bytes 1179656 | tf_op jit(solution)/shard_map/ppermute | solution.py:34
  59.0 2.2 %collective-permute-done.19.refs_7_ = bf16[96,1536]{1,0:T(8,128)(2,1)S(1)} collective-permute-done((bf16[96,1536]{1,0:T(8,128)(2,1)S(1)}, bf16[96,1536]{1,0:T(8,128)(2,1)S(1)}, u32[]{:S(2)}, u32[]{:S(2)}) %collective-permute-start.19) | collective-permute-done | bytes 294944 | tf_op jit(solution)/shard_map/ppermute | solution.py:34
  61.2 0.7 choose3.1
  62.2 5.5 %collective-permute-done.22.refs_1_ = bf16[64,1536]{1,0:T(8,128)(2,1)S(1)} collective-permute-done((bf16[64,1536]{1,0:T(8,128)(2,1)S(1)}, bf16[64,1536]{1,0:T(8,128)(2,1)S(1)}, u32[]{:S(2)}, u32[]{:S(2)}) %collective-permute-start.22) | collective-permute-done | bytes 196640 | tf_op jit(solution)/shard_map/ppermute | solution.py:34
  67.7 2.0 %collective-permute-start.24 = (bf16[128,1536]{1,0:T(8,128)(2,1)S(1)}, bf16[128,1536]{1,0:T(8,128)(2,1)S(1)}, u32[]{:S(2)}, u32[]{:S(2)}) collective-permute-start(bf16[128,1536]{1,0:T(8,128)(2,1)S(1)} %join3.1.refs_11_.refs_5_), channel_id=1, source_target_pairs={{0,2},{1,3},{2,0},{3,1},{4,6},{5,7},{6,4},{7,5},{8,10},{9,11},{10,... | collective-permute-start | bytes 1179656 | tf_op jit(solution)/shard_map/ppermute | solution.py:34
  69.8 2.9 %early.1 = (f32[256,1536]{1,0:T(8,128)S(1)}, f32[128,1536]{1,0:T(8,128)S(1)}, f32[128,1536]{1,0:T(8,128)S(1)}) custom-call(bf16[512,1536]{1,0:T(8,128)(2,1)S(1)} %pad_maximum_fusion.refs_0_, f32[512,1]{1,0:T(8,128)S(1)} %bitcast.42, bf16[512,32]{1,0:T(8,128)(2,1)S(1)} %copy-done.6, f32[1,768]{1,0:T(1,128)S(1)} %get-tuple-element.103.refs_10_.refs_3_, ...), custom_call_target="tpu_custom_call" | custom-call | flops 10000000000 | bytes 1 | tf_op jit(solution)/shard_map/early/pallas_call | solution.py:63
  72.7 0.5 collective-permute-start.28
  73.3 2.3 %collective-permute-done.24.refs_6_ = bf16[128,1536]{1,0:T(8,128)(2,1)S(1)} collective-permute-done((bf16[128,1536]{1,0:T(8,128)(2,1)S(1)}, bf16[128,1536]{1,0:T(8,128)(2,1)S(1)}, u32[]{:S(2)}, u32[]{:S(2)}) %collective-permute-start.24) | collective-permute-done | bytes 393248 | tf_op jit(solution)/shard_map/ppermute | solution.py:34
  75.6 1.1 %collective-permute-done.25.refs_7_ = bf16[128,1536]{1,0:T(8,128)(2,1)S(1)} collective-permute-done((bf16[128,1536]{1,0:T(8,128)(2,1)S(1)}, bf16[128,1536]{1,0:T(8,128)(2,1)S(1)}, u32[]{:S(2)}, u32[]{:S(2)}) %collective-permute-start.25) | collective-permute-done | bytes 393248 | tf_op jit(solution)/shard_map/ppermute | solution.py:34
  76.7 0.6 collective-permute-done.26.refs_8_
  77.3 2.1 %late3.1 = f32[256,1536]{1,0:T(8,128)} custom-call(bf16[256,1536]{1,0:T(8,128)(2,1)S(1)} %bitcast.37, f32[256,1]{1,0:T(8,128)S(1)} %copy.29.refs_4_.refs_1_, bf16[256,32]{1,0:T(8,128)(2,1)S(1)} %bitcast.40, f32[1,512]{1,0:T(1,128)S(1)} %get-tuple-element.102.refs_6_.refs_3_, s32[1,512]{1,0:T(1,128)S(1)} %get-tuple-element.104.refs_7_.refs_4_, ...), custom_call_target="tpu_custom_call" | custom-call | flops 1 | bytes 1 | tf_op jit(solution)/shard_map/late3/pallas_call | solution.py:63
  (134 shorter events, 4.1 us)
Async XLA Ops:
  0.1 1.1 %copy-start = (bf16[1,256,1536]{2,1,0:T(8,128)(2,1)S(1)}, bf16[1,256,1536]{2,1,0:T(8,128)(2,1)}, u32[]{:S(2)}) copy-start(bf16[1,256,1536]{2,1,0:T(8,128)(2,1)} %param.5) | copy-start | bytes 2359300
  1.2 6.4 %copy-start.10 = (s32[2,1,1,56]{3,2,1,0:T(1,128)S(1)}, s32[2,1,1,56]{3,2,1,0:T(1,128)}, u32[]{:S(2)}) copy-start(s32[2,1,1,56]{3,2,1,0:T(1,128)} %param.9) | copy-start | bytes 1348
  1.2 8.1 %copy-start.9 = (f32[1024]{0:T(1024)S(1)}, f32[1024]{0:T(1024)}, u32[]{:S(2)}) copy-start(f32[1024]{0:T(1024)} %param.7) | copy-start | bytes 12292
  1.2 9.5 %copy-start.7 = (s32[2,8]{1,0:T(2,128)S(1)}, s32[2,8]{1,0:T(2,128)}, u32[]{:S(2)}) copy-start(s32[2,8]{1,0:T(2,128)} %refs_1_.7) | copy-start | bytes 196
  1.2 9.8 %copy-start.8 = (f32[8]{0:T(128)S(1)}, f32[8]{0:T(128)}, u32[]{:S(2)}) copy-start(f32[8]{0:T(128)} %param.6) | copy-start | bytes 100
  1.9 14.5 %collective-permute-start.1 = (bf16[64,1536]{1,0:T(8,128)(2,1)S(1)}, bf16[64,1536]{1,0:T(8,128)(2,1)S(1)}, u32[]{:S(2)}, u32[]{:S(2)}) collective-permute-start(bf16[64,1536]{1,0:T(8,128)(2,1)S(1)} %get-tuple-element.80), channel_id=1, source_target_pairs={{0,8},{4,12},{8,0},{12,4},{16,24},{20,28},{24,16},{28,20},{1,9},{5... | collective-permute-start | bytes 589832 | tf_op jit(solution)/shard_map/ppermute | solution.py:34
  5.0 10.1 %collective-permute-start.2 = (bf16[32,1536]{1,0:T(8,128)(2,1)S(1)}, bf16[32,1536]{1,0:T(8,128)(2,1)S(1)}, u32[]{:S(2)}, u32[]{:S(2)}) collective-permute-start(bf16[32,1536]{1,0:T(8,128)(2,1)S(1)} %get-tuple-element.38), channel_id=1, source_target_pairs={{0,16},{4,20},{8,24},{12,28},{16,0},{20,4},{24,8},{28,12},{1,17},{... | collective-permute-start | bytes 294920 | tf_op jit(solution)/shard_map/ppermute | solution.py:34
  7.6 8.8 %collective-permute-start.3 = (bf16[32,1536]{1,0:T(8,128)(2,1)S(1)}, bf16[32,1536]{1,0:T(8,128)(2,1)S(1)}, u32[]{:S(2)}, u32[]{:S(2)}) collective-permute-start(bf16[32,1536]{1,0:T(8,128)(2,1)S(1)} %get-tuple-element.39), channel_id=1, source_target_pairs={{0,24},{4,28},{8,16},{12,20},{16,8},{20,12},{24,0},{28,4},{1,25},{... | collective-permute-start | bytes 294920 | tf_op jit(solution)/shard_map/ppermute | solution.py:34
  7.6 7.1 %collective-permute-start.4 = (s32[2,56]{1,0:T(2,128)S(1)}, s32[2,56]{1,0:T(2,128)S(1)}, u32[]{:S(2)}, u32[]{:S(2)}) collective-permute-start(s32[2,56]{1,0:T(2,128)S(1)} %bitcast.55), channel_id=1, source_target_pairs={{0,1},{1,0},{2,3},{3,2},{4,5},{5,4},{6,7},{7,6},{8,9},{9,8},{10,11... | collective-permute-start | bytes 1352 | tf_op jit(solution)/shard_map/ppermute | solution.py:34
  7.6 12.8 %collective-permute-start = (bf16[128,1536]{1,0:T(8,128)(2,1)S(1)}, bf16[128,1536]{1,0:T(8,128)(2,1)S(1)}, u32[]{:S(2)}, u32[]{:S(2)}) collective-permute-start(bf16[128,1536]{1,0:T(8,128)(2,1)S(1)} %get-tuple-element.36.refs_3_.refs_2_), channel_id=1, source_target_pairs={{0,4},{4,0},{8,12},{12,8},{16,20},{20,16},{24,28},{28,24},{1,5},{5... | collective-permute-start | bytes 1179656 | tf_op jit(solution)/shard_map/ppermute | solution.py:34
  15.0 1.4 %copy-start.3 = (bf16[4,64,32]{2,1,0:T(8,128)(2,1)}, bf16[4,64,32]{2,1,0:T(8,128)(2,1)S(1)}, u32[]{:S(2)}) copy-start(bf16[4,64,32]{2,1,0:T(8,128)(2,1)S(1)} %broadcast_in_dim.16) | copy-start | bytes 49156
  15.1 1.4 %copy-start.5 = (bf16[512,32]{1,0:T(8,128)(2,1)}, bf16[512,32]{1,0:T(8,128)(2,1)S(1)}, u32[]{:S(2)}) copy-start(bf16[512,32]{1,0:T(8,128)(2,1)S(1)} %pad_maximum_fusion.1.refs_9_.refs_2_) | copy-start | bytes 98308
  16.4 4.0 %copy-start.1 = (bf16[1,256,1536]{2,1,0:T(8,128)(2,1)S(1)}, bf16[1,256,1536]{2,1,0:T(8,128)(2,1)}, u32[]{:S(2)}) copy-start(bf16[1,256,1536]{2,1,0:T(8,128)(2,1)} %param.5) | copy-start | bytes 2359300
  16.5 9.0 %collective-permute-start.5 = (bf16[96,1536]{1,0:T(8,128)(2,1)S(1)}, bf16[96,1536]{1,0:T(8,128)(2,1)S(1)}, u32[]{:S(2)}, u32[]{:S(2)}) collective-permute-start(bf16[96,1536]{1,0:T(8,128)(2,1)S(1)} %stack0.1.refs_8_), channel_id=1, source_target_pairs={{0,4},{4,0},{8,12},{12,8},{16,20},{20,16},{24,28},{28,24},{1,5},{5... | collective-permute-start | bytes 884744 | tf_op jit(solution)/shard_map/ppermute | solution.py:34
  18.1 9.1 %collective-permute-start.8 = (bf16[32,1536]{1,0:T(8,128)(2,1)S(1)}, bf16[32,1536]{1,0:T(8,128)(2,1)S(1)}, u32[]{:S(2)}, u32[]{:S(2)}) collective-permute-start(bf16[32,1536]{1,0:T(8,128)(2,1)S(1)} %get-tuple-element.46), channel_id=1, source_target_pairs={{0,24},{4,28},{8,16},{12,20},{16,8},{20,12},{24,0},{28,4},{1,25},{... | collective-permute-start | bytes 294920 | tf_op jit(solution)/shard_map/ppermute | solution.py:34
  19.8 8.4 %collective-permute-start.7 = (bf16[32,1536]{1,0:T(8,128)(2,1)S(1)}, bf16[32,1536]{1,0:T(8,128)(2,1)S(1)}, u32[]{:S(2)}, u32[]{:S(2)}) collective-permute-start(bf16[32,1536]{1,0:T(8,128)(2,1)S(1)} %get-tuple-element.44), channel_id=1, source_target_pairs={{0,16},{4,20},{8,24},{12,28},{16,0},{20,4},{24,8},{28,12},{1,17},{... | collective-permute-start | bytes 294920 | tf_op jit(solution)/shard_map/ppermute | solution.py:34
  20.4 13.1 %collective-permute-start.11 = (bf16[256,1536]{1,0:T(8,128)(2,1)S(1)}, bf16[256,1536]{1,0:T(8,128)(2,1)S(1)}, u32[]{:S(2)}, u32[]{:S(2)}) collective-permute-start(bf16[256,1536]{1,0:T(8,128)(2,1)S(1)} %bitcast.35), channel_id=1, source_target_pairs={{0,1},{1,0},{2,3},{3,2},{4,5},{5,4},{6,7},{7,6},{8,9},{9,8},{10,11... | collective-permute-start | bytes 2359304 | tf_op jit(solution)/shard_map/ppermute | solution.py:34
  26.2 7.3 %collective-permute-start.10 = (bf16[64,1536]{1,0:T(8,128)(2,1)S(1)}, bf16[64,1536]{1,0:T(8,128)(2,1)S(1)}, u32[]{:S(2)}, u32[]{:S(2)}) collective-permute-start(bf16[64,1536]{1,0:T(8,128)(2,1)S(1)} %get-tuple-element.47), channel_id=1, source_target_pairs={{0,8},{4,12},{8,0},{12,4},{16,24},{20,28},{24,16},{28,20},{1,9},{5... | collective-permute-start | bytes 589832 | tf_op jit(solution)/shard_map/ppermute | solution.py:34
  28.2 8.1 %collective-permute-start.9 = (bf16[96,1536]{1,0:T(8,128)(2,1)S(1)}, bf16[96,1536]{1,0:T(8,128)(2,1)S(1)}, u32[]{:S(2)}, u32[]{:S(2)}) collective-permute-start(bf16[96,1536]{1,0:T(8,128)(2,1)S(1)} %stack1.1.refs_2_), channel_id=1, source_target_pairs={{0,4},{4,0},{8,12},{12,8},{16,20},{20,16},{24,28},{28,24},{1,5},{5... | collective-permute-start | bytes 884744 | tf_op jit(solution)/shard_map/ppermute | solution.py:34
  29.6 10.0 %collective-permute-start.14 = (bf16[32,1536]{1,0:T(8,128)(2,1)S(1)}, bf16[32,1536]{1,0:T(8,128)(2,1)S(1)}, u32[]{:S(2)}, u32[]{:S(2)}) collective-permute-start(bf16[32,1536]{1,0:T(8,128)(2,1)S(1)} %get-tuple-element.54), channel_id=1, source_target_pairs={{0,16},{4,20},{8,24},{12,28},{16,0},{20,4},{24,8},{28,12},{1,17},{... | collective-permute-start | bytes 294920 | tf_op jit(solution)/shard_map/ppermute | solution.py:34
  32.3 7.8 %collective-permute-start.15 = (bf16[32,1536]{1,0:T(8,128)(2,1)S(1)}, bf16[32,1536]{1,0:T(8,128)(2,1)S(1)}, u32[]{:S(2)}, u32[]{:S(2)}) collective-permute-start(bf16[32,1536]{1,0:T(8,128)(2,1)S(1)} %get-tuple-element.56), channel_id=1, source_target_pairs={{0,24},{4,28},{8,16},{12,20},{16,8},{20,12},{24,0},{28,4},{1,25},{... | collective-permute-start | bytes 294920 | tf_op jit(solution)/shard_map/ppermute | solution.py:34
  33.5 9.5 %collective-permute-start.6 = (bf16[64,1536]{1,0:T(8,128)(2,1)S(1)}, bf16[64,1536]{1,0:T(8,128)(2,1)S(1)}, u32[]{:S(2)}, u32[]{:S(2)}) collective-permute-start(bf16[64,1536]{1,0:T(8,128)(2,1)S(1)} %get-tuple-element.41), channel_id=1, source_target_pairs={{0,8},{4,12},{8,0},{12,4},{16,24},{20,28},{24,16},{28,20},{1,9},{5... | collective-permute-start | bytes 589832 | tf_op jit(solution)/shard_map/ppermute | solution.py:34
  33.5 15.4 %collective-permute-start.18 = (bf16[128,1536]{1,0:T(8,128)(2,1)S(1)}, bf16[128,1536]{1,0:T(8,128)(2,1)S(1)}, u32[]{:S(2)}, u32[]{:S(2)}) collective-permute-start(bf16[128,1536]{1,0:T(8,128)(2,1)S(1)} %join0.1.refs_8_.refs_3_.refs_5_), channel_id=1, source_target_pairs={{0,2},{1,3},{2,0},{3,1},{4,6},{5,7},{6,4},{7,5},{8,10},{9,11},{10,... | collective-permute-start | bytes 1179656 | tf_op jit(solution)/shard_map/ppermute | solution.py:34
  37.1 11.8 %collective-permute-start.17 = (bf16[64,1536]{1,0:T(8,128)(2,1)S(1)}, bf16[64,1536]{1,0:T(8,128)(2,1)S(1)}, u32[]{:S(2)}, u32[]{:S(2)}) collective-permute-start(bf16[64,1536]{1,0:T(8,128)(2,1)S(1)} %get-tuple-element.57), channel_id=1, source_target_pairs={{0,8},{4,12},{8,0},{12,4},{16,24},{20,28},{24,16},{28,20},{1,9},{5... | collective-permute-start | bytes 589832 | tf_op jit(solution)/shard_map/ppermute | solution.py:34
  43.0 7.5 %collective-permute-start.16 = (bf16[96,1536]{1,0:T(8,128)(2,1)S(1)}, bf16[96,1536]{1,0:T(8,128)(2,1)S(1)}, u32[]{:S(2)}, u32[]{:S(2)}) collective-permute-start(bf16[96,1536]{1,0:T(8,128)(2,1)S(1)} %stack2.1.refs_2_), channel_id=1, source_target_pairs={{0,4},{4,0},{8,12},{12,8},{16,20},{20,16},{24,28},{28,24},{1,5},{5... | collective-permute-start | bytes 884744 | tf_op jit(solution)/shard_map/ppermute | solution.py:34
  44.9 7.1 %collective-permute-start.13 = (bf16[32,1536]{1,0:T(8,128)(2,1)S(1)}, bf16[32,1536]{1,0:T(8,128)(2,1)S(1)}, u32[]{:S(2)}, u32[]{:S(2)}) collective-permute-start(bf16[32,1536]{1,0:T(8,128)(2,1)S(1)} %get-tuple-element.52), channel_id=1, source_target_pairs={{0,24},{4,28},{8,16},{12,20},{16,8},{20,12},{24,0},{28,4},{1,25},{... | collective-permute-start | bytes 294920 | tf_op jit(solution)/shard_map/ppermute | solution.py:34
  48.9 5.5 %collective-permute-start.12 = (bf16[32,1536]{1,0:T(8,128)(2,1)S(1)}, bf16[32,1536]{1,0:T(8,128)(2,1)S(1)}, u32[]{:S(2)}, u32[]{:S(2)}) collective-permute-start(bf16[32,1536]{1,0:T(8,128)(2,1)S(1)} %get-tuple-element.50), channel_id=1, source_target_pairs={{0,16},{4,20},{8,24},{12,28},{16,0},{20,4},{24,8},{28,12},{1,17},{... | collective-permute-start | bytes 294920 | tf_op jit(solution)/shard_map/ppermute | solution.py:34
  48.9 8.4 %collective-permute-start.21 = (bf16[128,1536]{1,0:T(8,128)(2,1)S(1)}, bf16[128,1536]{1,0:T(8,128)(2,1)S(1)}, u32[]{:S(2)}, u32[]{:S(2)}) collective-permute-start(bf16[128,1536]{1,0:T(8,128)(2,1)S(1)} %join1.1.refs_8_.refs_3_.refs_7_), channel_id=1, source_target_pairs={{0,2},{1,3},{2,0},{3,1},{4,6},{5,7},{6,4},{7,5},{8,10},{9,11},{10,... | collective-permute-start | bytes 1179656 | tf_op jit(solution)/shard_map/ppermute | solution.py:34
  51.2 5.7 %collective-permute-start.20 = (bf16[64,1536]{1,0:T(8,128)(2,1)S(1)}, bf16[64,1536]{1,0:T(8,128)(2,1)S(1)}, u32[]{:S(2)}, u32[]{:S(2)}) collective-permute-start(bf16[64,1536]{1,0:T(8,128)(2,1)S(1)} %get-tuple-element.59), channel_id=1, source_target_pairs={{0,8},{4,12},{8,0},{12,4},{16,24},{20,28},{24,16},{28,20},{1,9},{5... | collective-permute-start | bytes 589832 | tf_op jit(solution)/shard_map/ppermute | solution.py:34
  54.4 6.8 %collective-permute-start.19 = (bf16[96,1536]{1,0:T(8,128)(2,1)S(1)}, bf16[96,1536]{1,0:T(8,128)(2,1)S(1)}, u32[]{:S(2)}, u32[]{:S(2)}) collective-permute-start(bf16[96,1536]{1,0:T(8,128)(2,1)S(1)} %stack3.1.refs_2_), channel_id=1, source_target_pairs={{0,4},{4,0},{8,12},{12,8},{16,20},{20,16},{24,28},{28,24},{1,5},{5... | collective-permute-start | bytes 884744 | tf_op jit(solution)/shard_map/ppermute | solution.py:34
  57.4 4.7 %copy-start.2 = (bf16[1,256,1536]{2,1,0:T(8,128)(2,1)S(1)}, bf16[1,256,1536]{2,1,0:T(8,128)(2,1)}, u32[]{:S(2)}) copy-start(bf16[1,256,1536]{2,1,0:T(8,128)(2,1)} %param.5) | copy-start | bytes 2359300
  57.4 10.3 %collective-permute-start.23 = (bf16[128,1536]{1,0:T(8,128)(2,1)S(1)}, bf16[128,1536]{1,0:T(8,128)(2,1)S(1)}, u32[]{:S(2)}, u32[]{:S(2)}) collective-permute-start(bf16[128,1536]{1,0:T(8,128)(2,1)S(1)} %join2.1.refs_8_.refs_3_.refs_9_), channel_id=1, source_target_pairs={{0,2},{1,3},{2,0},{3,1},{4,6},{5,7},{6,4},{7,5},{8,10},{9,11},{10,... | collective-permute-start | bytes 1179656 | tf_op jit(solution)/shard_map/ppermute | solution.py:34
  62.0 5.7 %collective-permute-start.22 = (bf16[64,1536]{1,0:T(8,128)(2,1)S(1)}, bf16[64,1536]{1,0:T(8,128)(2,1)S(1)}, u32[]{:S(2)}, u32[]{:S(2)}) collective-permute-start(bf16[64,1536]{1,0:T(8,128)(2,1)S(1)} %get-tuple-element.61), channel_id=1, source_target_pairs={{0,8},{4,12},{8,0},{12,4},{16,24},{20,28},{24,16},{28,20},{1,9},{5... | collective-permute-start | bytes 589832 | tf_op jit(solution)/shard_map/ppermute | solution.py:34
  67.7 2.1 %copy-start.6 = (bf16[512,32]{1,0:T(8,128)(2,1)S(1)}, bf16[512,32]{1,0:T(8,128)(2,1)}, u32[]{:S(2)}) copy-start(bf16[512,32]{1,0:T(8,128)(2,1)} %copy-done.5) | copy-start | bytes 98308
  67.7 9.6 %copy-start.4 = (bf16[4,64,32]{2,1,0:T(8,128)(2,1)S(1)}, bf16[4,64,32]{2,1,0:T(8,128)(2,1)}, u32[]{:S(2)}) copy-start(bf16[4,64,32]{2,1,0:T(8,128)(2,1)} %copy-done.3) | copy-start | bytes 49156
  67.7 7.8 %collective-permute-start.24 = (bf16[128,1536]{1,0:T(8,128)(2,1)S(1)}, bf16[128,1536]{1,0:T(8,128)(2,1)S(1)}, u32[]{:S(2)}, u32[]{:S(2)}) collective-permute-start(bf16[128,1536]{1,0:T(8,128)(2,1)S(1)} %join3.1.refs_11_.refs_5_), channel_id=1, source_target_pairs={{0,2},{1,3},{2,0},{3,1},{4,6},{5,7},{6,4},{7,5},{8,10},{9,11},{10,... | collective-permute-start | bytes 1179656 | tf_op jit(solution)/shard_map/ppermute | solution.py:34
  72.6 4.7 %collective-permute-start.27 = (f32[128,1536]{1,0:T(8,128)S(1)}, f32[128,1536]{1,0:T(8,128)S(1)}, u32[]{:S(2)}, u32[]{:S(2)}) collective-permute-start(f32[128,1536]{1,0:T(8,128)S(1)} %get-tuple-element.65), channel_id=1, source_target_pairs={{0,1},{1,0},{2,3},{3,2},{4,5},{5,4},{6,7},{7,6},{8,9},{9,8},{10,11... | collective-permute-start | bytes 2359304 | tf_op jit(solution)/shard_map/ppermute | solution.py:34
  72.7 4.6 %collective-permute-start.28 = (f32[128,1536]{1,0:T(8,128)S(1)}, f32[128,1536]{1,0:T(8,128)S(1)}, u32[]{:S(2)}, u32[]{:S(2)}) collective-permute-start(f32[128,1536]{1,0:T(8,128)S(1)} %get-tuple-element.66), channel_id=1, source_target_pairs={{0,1},{1,0},{2,3},{3,2},{4,5},{5,4},{6,7},{7,6},{8,9},{9,8},{10,11... | collective-permute-start | bytes 2359304 | tf_op jit(solution)/shard_map/ppermute | solution.py:34
  73.2 3.5 %collective-permute-start.25 = (bf16[128,1536]{1,0:T(8,128)(2,1)S(1)}, bf16[128,1536]{1,0:T(8,128)(2,1)S(1)}, u32[]{:S(2)}, u32[]{:S(2)}) collective-permute-start(bf16[128,1536]{1,0:T(8,128)(2,1)S(1)} %join3.1.refs_11_.refs_5_), channel_id=1, source_target_pairs={{0,1},{1,0},{2,3},{3,2},{4,5},{5,4},{6,7},{7,6},{8,9},{9,8},{10,11... | collective-permute-start | bytes 1179656 | tf_op jit(solution)/shard_map/ppermute | solution.py:34
  75.6 1.7 %collective-permute-start.26 = (bf16[128,1536]{1,0:T(8,128)(2,1)S(1)}, bf16[128,1536]{1,0:T(8,128)(2,1)S(1)}, u32[]{:S(2)}, u32[]{:S(2)}) collective-permute-start(bf16[128,1536]{1,0:T(8,128)(2,1)S(1)} %collective-permute-done.24.refs_6_), channel_id=1, source_target_pairs={{0,1},{1,0},{2,3},{3,2},{4,5},{5,4},{6,7},{7,6},{8,9},{9,8},{10,11... | collective-permute-start | bytes 1179656 | tf_op jit(solution)/shard_map/ppermute | solution.py:34
